TPU v7x, 32 devices: a whole 2x2x4 slice. The times are simulated.
32 devices in a mesh: img: 16 (over z, x, core), band: 2 (over y).
Axes of the slice: x: 2, y: 2, z: 4, core: 2. Of those that a mesh axis runs over, the one named last changes fastest.
Arguments:
- latents: bfloat16 [32, 1024, 1152], P('img', 'band'), may hold values from -6 to 6
- cotangent: bfloat16 [32, 1024, 1152], P('img', 'band'), may hold values from -6 to 6
- labels: int32 [32], P('img'), may hold values from 0 to 999
- group_ids: int32 [32], P('img'), may hold values from 0 to 7
- group_logits: float32 [8], replicated, may hold values from -4 to 4
- row_pos: int32 [1024], P('band'), may hold values from 0 to 63
- col_pos: int32 [1024], P('band'), may hold values from 0 to 63
- time_weight: bfloat16 [256, 1152], replicated, may hold values from -0.375 to 0.375
- class_table: bfloat16 [1000, 1152], replicated, may hold values from -6 to 6
- ada_weight: bfloat16 [1152, 6912], replicated, may hold values from -0.1875 to 0.1875
- ada_bias: float32 [6912], replicated, may hold values from -3 to 3
- qkv_weight: bfloat16 [1152, 3456], replicated, may hold values from -0.1875 to 0.1875
- query_gain: float32 [72], replicated, may hold values from 0.1 to 1.9
- key_gain: float32 [72], replicated, may hold values from 0.1 to 1.9
- proj_weight: bfloat16 [1152, 1152], replicated, may hold values from -0.75 to 0.75
- gateup_weight: bfloat16 [1152, 6144], replicated, may hold values from -0.1875 to 0.1875
- down_weight: bfloat16 [3072, 1152], replicated, may hold values from -0.109375 to 0.109375
Outputs:
- result: bfloat16 [32, 1024, 1152], P('img', 'band')
- grad_latents: bfloat16 [32, 1024, 1152], P('img', 'band')
- grad_time: float32 [256, 1152], P('img', 'band')
- grad_class: float32 [1000, 1152], replicated
- grad_ada: float32 [1152, 6912], P('img', 'band')
- grad_ada_bias: float32 [6912], replicated
- grad_qkv: float32 [1152, 3456], P('img', 'band')
- grad_query_gain: float32 [72], replicated
- grad_key_gain: float32 [72], replicated
- grad_proj: float32 [1152, 1152], P('img', 'band')
- grad_gateup: float32 [1152, 6144], P('img', 'band')
- grad_down: float32 [3072, 1152], P('img', 'band')
All inputs are finite; a program needn't handle non-finite values.
Results may differ from a plain program's by a relative error of at most 0.018.
Values may be sent and summed in bfloat16 or wider, within the bound.
A program may use at most 384 MiB of HBM per device.

v0:
```python
import math

import jax
import jax.numpy as jnp
from jax import lax
from jax.sharding import PartitionSpec as P

HEADS = 16
HD = 72
FF = 3072
NCLASS = 1000
FREQ = 256
GROUPS = 8


highest = lax.Precision.HIGHEST
epsilon = 1e-06


def unit_rms(values):
    return values * lax.rsqrt(jnp.mean(values * values, axis=-1, keepdims=True) + epsilon)


def unit_rms_back(values, grads):
    factor = lax.rsqrt(jnp.mean(values * values, axis=-1, keepdims=True) + epsilon)
    normed = values * factor
    return factor * (grads - normed * jnp.mean(grads * normed, axis=-1, keepdims=True))


def rope_tables(row_pos, col_pos, quarter):
    frequency = jnp.exp(-math.log(10000.0) * jnp.arange(quarter, dtype=jnp.float32) / quarter)
    row_angle = row_pos.astype(jnp.float32)[:, None] * frequency[None, :]
    col_angle = col_pos.astype(jnp.float32)[:, None] * frequency[None, :]
    cosine = jnp.concatenate(
        [jnp.cos(row_angle), jnp.cos(row_angle), jnp.cos(col_angle), jnp.cos(col_angle)], axis=-1
    )
    sine = jnp.concatenate(
        [-jnp.sin(row_angle), jnp.sin(row_angle), -jnp.sin(col_angle), jnp.sin(col_angle)], axis=-1
    )
    return (cosine, sine)


def partner(values, quarter):
    return jnp.concatenate(
        [
            values[..., quarter : 2 * quarter],
            values[..., :quarter],
            values[..., 3 * quarter :],
            values[..., 2 * quarter : 3 * quarter],
        ],
        axis=-1,
    )


def time_features(times, half):
    frequency = jnp.exp(-math.log(10000.0) * jnp.arange(half, dtype=jnp.float32) / half)
    angles = 1000.0 * times[:, None] * frequency[None, :]
    return jnp.concatenate([jnp.cos(angles), jnp.sin(angles)], axis=-1)


def silu_slope(values):
    sigma = jax.nn.sigmoid(values)
    return sigma * (1.0 + values * (1.0 - sigma))


def per_device(
    latents,
    cotangent,
    labels,
    group_ids,
    group_logits,
    row_pos,
    col_pos,
    time_weight,
    class_table,
    ada_weight,
    ada_bias,
    qkv_weight,
    query_gain,
    key_gain,
    proj_weight,
    gateup_weight,
    down_weight,
):
    images, rows, width = latents.shape
    quarter = HD // 4
    scaling = HD ** (-0.5)
    group_hot = (group_ids[:, None] == jnp.arange(GROUPS, dtype=jnp.int32)[None, :]).astype(
        jnp.float32
    )
    times = jax.nn.sigmoid(jnp.dot(group_hot, group_logits, precision=highest))
    features = time_features(times, FREQ // 2).astype(jnp.bfloat16)
    class_hot = (labels[:, None] == jnp.arange(NCLASS, dtype=jnp.int32)[None, :]).astype(
        jnp.bfloat16
    )
    before = jnp.dot(features, time_weight, preferred_element_type=jnp.float32) + jnp.dot(
        class_hot, class_table, preferred_element_type=jnp.float32
    )
    condition = jax.nn.silu(before).astype(jnp.bfloat16)
    modulation = jnp.dot(condition, ada_weight, preferred_element_type=jnp.float32) + ada_bias
    pieces = [modulation[:, None, member * width : (member + 1) * width] for member in range(6)]
    shift_one, scale_one, gate_one, shift_two, scale_two, gate_two = pieces
    cosine, sine = rope_tables(row_pos, col_pos, quarter)
    cosine = cosine[None, :, None, :]
    sine = sine[None, :, None, :]

    def turned(values):
        return values * cosine + partner(values, quarter) * sine

    def turned_back(grads):
        return grads * cosine + partner(grads * sine, quarter)

    source = latents.astype(jnp.float32)
    normed_one = unit_rms(source)
    entry_one = (normed_one * (1.0 + scale_one) + shift_one).astype(jnp.bfloat16)
    projected = jnp.einsum("bpd,de->bpe", entry_one, qkv_weight, preferred_element_type=jnp.float32)
    shape = (images, rows, HEADS, HD)
    query_raw = projected[..., :width].reshape(shape)
    key_raw = projected[..., width : 2 * width].reshape(shape)
    value_bf = projected[..., 2 * width :].reshape(shape).astype(jnp.bfloat16)
    query_unit = unit_rms(query_raw)
    key_unit = unit_rms(key_raw)
    query_bf = turned(query_unit * query_gain).astype(jnp.bfloat16)
    key_bf = turned(key_unit * key_gain).astype(jnp.bfloat16)
    peak = jnp.full((images, HEADS, rows), -1e30, jnp.float32)
    key_piece = lax.all_gather(key_bf, "band", axis=1, tiled=True)
    value_piece = lax.all_gather(value_bf, "band", axis=1, tiled=True)
    scores = (
        jnp.einsum("bqhd,bkhd->bhqk", query_bf, key_piece, preferred_element_type=jnp.float32)
        * scaling
    )
    new_peak = jnp.maximum(peak, jnp.max(scores, axis=-1))
    weights = jnp.exp(scores - new_peak[..., None])
    total = jnp.sum(weights, axis=-1)
    update = jnp.einsum(
        "bhqk,bkhd->bqhd",
        weights.astype(jnp.bfloat16),
        value_piece,
        preferred_element_type=jnp.float32,
    )
    accum = update
    peak, total, accum = (new_peak, total, accum)
    mixed = accum / jnp.transpose(total, (0, 2, 1))[..., None]
    log_total = peak + jnp.log(total)
    mixed_bf = mixed.reshape(images, rows, width).astype(jnp.bfloat16)
    attended = jnp.einsum("bpd,de->bpe", mixed_bf, proj_weight, preferred_element_type=jnp.float32)
    middle = source + gate_one * attended
    normed_two = unit_rms(middle)
    entry_two = (normed_two * (1.0 + scale_two) + shift_two).astype(jnp.bfloat16)
    gate_up = jnp.einsum(
        "bpd,de->bpe", entry_two, gateup_weight, preferred_element_type=jnp.float32
    )
    gate_part = gate_up[..., :FF]
    up_part = gate_up[..., FF:]
    hidden = (jax.nn.silu(gate_part) * up_part).astype(jnp.bfloat16)
    fed = jnp.einsum("bpf,fd->bpd", hidden, down_weight, preferred_element_type=jnp.float32)
    result = (middle + gate_two * fed).astype(jnp.bfloat16)
    upstream = cotangent.astype(jnp.float32)
    fed_grad = (upstream * gate_two).astype(jnp.bfloat16)
    grad_gate_two = jnp.sum(upstream * fed, axis=1)
    grad_down = jnp.einsum("bpf,bpd->fd", hidden, fed_grad, preferred_element_type=jnp.float32)
    hidden_grad = jnp.einsum(
        "bpd,fd->bpf", fed_grad, down_weight, preferred_element_type=jnp.float32
    )
    gate_grad = hidden_grad * up_part * silu_slope(gate_part)
    up_grad = hidden_grad * jax.nn.silu(gate_part)
    gate_up_grad = jnp.concatenate([gate_grad, up_grad], axis=-1).astype(jnp.bfloat16)
    grad_gateup = jnp.einsum(
        "bpd,bpe->de", entry_two, gate_up_grad, preferred_element_type=jnp.float32
    )
    entry_two_grad = jnp.einsum(
        "bpe,de->bpd", gate_up_grad, gateup_weight, preferred_element_type=jnp.float32
    )
    grad_scale_two = jnp.sum(entry_two_grad * normed_two, axis=1)
    grad_shift_two = jnp.sum(entry_two_grad, axis=1)
    middle_grad = upstream + unit_rms_back(middle, entry_two_grad * (1.0 + scale_two))
    grad_gate_one = jnp.sum(middle_grad * attended, axis=1)
    attended_grad = (middle_grad * gate_one).astype(jnp.bfloat16)
    grad_proj = jnp.einsum(
        "bpd,bpe->de", mixed_bf, attended_grad, preferred_element_type=jnp.float32
    )
    mixed_grad = jnp.einsum(
        "bpe,de->bpd", attended_grad, proj_weight, preferred_element_type=jnp.float32
    )
    mixed_grad_bf = mixed_grad.reshape(shape).astype(jnp.bfloat16)
    offsets = jnp.transpose(jnp.sum(mixed_grad_bf.astype(jnp.float32) * mixed, axis=-1), (0, 2, 1))
    key_piece = lax.all_gather(key_bf, "band", axis=1, tiled=True)
    value_piece = lax.all_gather(value_bf, "band", axis=1, tiled=True)
    scores = (
        jnp.einsum("bqhd,bkhd->bhqk", query_bf, key_piece, preferred_element_type=jnp.float32)
        * scaling
    )
    probs = jnp.exp(scores - log_total[..., None])
    prob_grad = jnp.einsum(
        "bqhd,bkhd->bhqk", mixed_grad_bf, value_piece, preferred_element_type=jnp.float32
    )
    score_grad = (probs * (prob_grad - offsets[..., None])).astype(jnp.bfloat16)
    query_grad = (
        jnp.einsum("bhqk,bkhd->bqhd", score_grad, key_piece, preferred_element_type=jnp.float32)
        * scaling
    )
    key_term = (
        jnp.einsum("bhqk,bqhd->bkhd", score_grad, query_bf, preferred_element_type=jnp.float32)
        * scaling
    )
    value_term = jnp.einsum(
        "bhqk,bqhd->bkhd",
        probs.astype(jnp.bfloat16),
        mixed_grad_bf,
        preferred_element_type=jnp.float32,
    )
    key_grads = key_term
    value_grads = value_term
    query_grad, key_grads, value_grads = (query_grad, key_grads, value_grads)
    key_local, value_local = (
        lax.psum_scatter(
            key_grads.astype(jnp.bfloat16), "band", scatter_dimension=1, tiled=True
        ).astype(jnp.float32),
        lax.psum_scatter(
            value_grads.astype(jnp.bfloat16), "band", scatter_dimension=1, tiled=True
        ).astype(jnp.float32),
    )
    query_turned = turned_back(query_grad)
    key_turned = turned_back(key_local)
    local_query_gain = jnp.sum(query_turned * query_unit, axis=(0, 1, 2))
    local_key_gain = jnp.sum(key_turned * key_unit, axis=(0, 1, 2))
    query_raw_grad = unit_rms_back(query_raw, query_turned * query_gain)
    key_raw_grad = unit_rms_back(key_raw, key_turned * key_gain)
    flat = (images, rows, width)
    projected_grad = jnp.concatenate(
        [query_raw_grad.reshape(flat), key_raw_grad.reshape(flat), value_local.reshape(flat)],
        axis=-1,
    ).astype(jnp.bfloat16)
    grad_qkv = jnp.einsum(
        "bpd,bpe->de", entry_one, projected_grad, preferred_element_type=jnp.float32
    )
    entry_one_grad = jnp.einsum(
        "bpe,de->bpd", projected_grad, qkv_weight, preferred_element_type=jnp.float32
    )
    grad_scale_one = jnp.sum(entry_one_grad * normed_one, axis=1)
    grad_shift_one = jnp.sum(entry_one_grad, axis=1)
    source_grad = middle_grad + unit_rms_back(source, entry_one_grad * (1.0 + scale_one))
    grad_latents = source_grad.astype(jnp.bfloat16)
    band_partial = jnp.concatenate(
        [
            grad_shift_one,
            grad_scale_one,
            grad_gate_one,
            grad_shift_two,
            grad_scale_two,
            grad_gate_two,
        ],
        axis=-1,
    )
    modulation_grad, band_query_gain, band_key_gain = (
        lax.psum(band_partial.astype(jnp.bfloat16), "band").astype(jnp.float32),
        lax.psum(local_query_gain[None, :].astype(jnp.bfloat16), "band").astype(jnp.float32),
        lax.psum(local_key_gain[None, :].astype(jnp.bfloat16), "band").astype(jnp.float32),
    )
    condition_grad = jnp.dot(modulation_grad, ada_weight.astype(jnp.float32).T, precision=highest)
    before_grad = condition_grad * silu_slope(before)
    condition_all, features_all, modulation_all, before_all, query_gain_rows, key_gain_rows = (
        lax.all_gather(
            condition.astype(jnp.float32).astype(jnp.bfloat16), "img", axis=0, tiled=True
        ).astype(jnp.float32),
        lax.all_gather(
            features.astype(jnp.float32).astype(jnp.bfloat16), "img", axis=0, tiled=True
        ).astype(jnp.float32),
        lax.all_gather(modulation_grad.astype(jnp.bfloat16), "img", axis=0, tiled=True).astype(
            modulation_grad.dtype
        ),
        lax.all_gather(before_grad.astype(jnp.bfloat16), "img", axis=0, tiled=True).astype(
            before_grad.dtype
        ),
        lax.all_gather(band_query_gain.astype(jnp.bfloat16), "img", axis=0, tiled=True).astype(
            band_query_gain.dtype
        ),
        lax.all_gather(band_key_gain.astype(jnp.bfloat16), "img", axis=0, tiled=True).astype(
            band_key_gain.dtype
        ),
    )
    labels_all = lax.all_gather(labels, "img", axis=0, tiled=True)
    img_index = lax.axis_index("img")
    band_index = lax.axis_index("band")
    ada_rows = width // lax.axis_size("img")
    ada_cols = 6 * width // lax.axis_size("band")
    time_rows = FREQ // lax.axis_size("img")
    time_cols = width // lax.axis_size("band")
    condition_part = lax.dynamic_slice_in_dim(condition_all, img_index * ada_rows, ada_rows, 1)
    modulation_part = lax.dynamic_slice_in_dim(modulation_all, band_index * ada_cols, ada_cols, 1)
    sum_ada = jnp.dot(condition_part.T, modulation_part, precision=highest)
    features_part = lax.dynamic_slice_in_dim(features_all, img_index * time_rows, time_rows, 1)
    before_part = lax.dynamic_slice_in_dim(before_all, band_index * time_cols, time_cols, 1)
    sum_time = jnp.dot(features_part.T, before_part, precision=highest)
    class_all = (labels_all[:, None] == jnp.arange(NCLASS, dtype=jnp.int32)[None, :]).astype(
        jnp.float32
    )
    sum_class = jnp.dot(class_all.T, before_all, precision=highest)
    sum_bias = jnp.sum(modulation_all, axis=0)
    sum_query_gain = jnp.sum(query_gain_rows, axis=0)
    sum_key_gain = jnp.sum(key_gain_rows, axis=0)
    part_qkv, part_proj, part_gateup, part_down = (
        lax.psum_scatter(
            grad_qkv.astype(jnp.bfloat16), "img", scatter_dimension=0, tiled=True
        ).astype(jnp.float32),
        lax.psum_scatter(
            grad_proj.astype(jnp.bfloat16), "img", scatter_dimension=0, tiled=True
        ).astype(jnp.float32),
        lax.psum_scatter(
            grad_gateup.astype(jnp.bfloat16), "img", scatter_dimension=0, tiled=True
        ).astype(jnp.float32),
        lax.psum_scatter(
            grad_down.astype(jnp.bfloat16), "img", scatter_dimension=0, tiled=True
        ).astype(jnp.float32),
    )
    sum_qkv, sum_proj, sum_gateup, sum_down = (
        lax.psum_scatter(
            part_qkv.astype(jnp.bfloat16), "band", scatter_dimension=1, tiled=True
        ).astype(jnp.float32),
        lax.psum_scatter(
            part_proj.astype(jnp.bfloat16), "band", scatter_dimension=1, tiled=True
        ).astype(jnp.float32),
        lax.psum_scatter(
            part_gateup.astype(jnp.bfloat16), "band", scatter_dimension=1, tiled=True
        ).astype(jnp.float32),
        lax.psum_scatter(
            part_down.astype(jnp.bfloat16), "band", scatter_dimension=1, tiled=True
        ).astype(jnp.float32),
    )
    return (
        result,
        grad_latents,
        sum_time,
        sum_class,
        sum_ada,
        sum_bias,
        sum_qkv,
        sum_query_gain,
        sum_key_gain,
        sum_proj,
        sum_gateup,
        sum_down,
    )


def solution(mesh):
    return jax.shard_map(
        per_device,
        mesh=mesh,
        in_specs=(
            P("img", "band", None),
            P("img", "band", None),
            P("img"),
            P("img"),
            P(),
            P("band"),
            P("band"),
            P(),
            P(),
            P(),
            P(),
            P(),
            P(),
            P(),
            P(),
            P(),
            P(),
        ),
        out_specs=(
            P("img", "band", None),
            P("img", "band", None),
            P("img", "band"),
            P(),
            P("img", "band"),
            P(),
            P("img", "band"),
            P(),
            P(),
            P("img", "band"),
            P("img", "band"),
            P("img", "band"),
        ),
        check_vma=False,
    )
```

profile of v0, /device:TPU:0, one launch (start us, length us, event | category | flops | bytes accessed | tf_op | source)
XLA Modules:
  0.0 978.1 jit_solution(6065977088026414276)
XLA Ops:
  11.8 7.8 convolution_add_fusion
  21.5 12.7 %fusion.17 = f32[2,512,3456]{2,1,0:T(8,128)S(1)} fusion(bf16[1152,3456]{1,0:T(8,128)(2,1)} %param.28, bf16[2,512,1152]{2,1,0:T(8,128)(2,1)S(1)} %copy-done.7, f32[2,1152]{1,0:T(2,128)S(1)} %get-tuple-element.64, f32[2,1152]{1,0:T(2,128)S(1)} %get-tuple-element.65, f32[2,512]{1,0:T(2,128)S(1)} %add_rsqrt_fusion.3), kind=kOutput, calls=%fused_computation.29 | convolution fusion | flops 8159625216 | bytes 24500224 | tf_op jit(solution)/shard_map/bpd,de->bpe/dot_general | solution.py:116
  34.2 4.5 fusion.93
  42.1 6.1 copy.53
  51.2 6.1 copy.52
  61.1 6.1 multiply_multiply_fusion
  74.8 8.6 fusion.44
  87.4 4.3 copy.51
  91.8 57.1 %all-gather.11.cloned.1.call-done = bf16[2,1024,16,72]{1,3,2,0:T(8,128)(2,1)} async-done(((bf16[2,512,16,72]{1,3,2,0:T(8,128)(2,1)}), bf16[2,1024,16,72]{1,3,2,0:T(8,128)(2,1)}) %all-gather.11.cloned.1.call-update) | async-done | bytes 4718608 | tf_op jit(solution)/shard_map/all_gather | solution.py:126
  148.9 28.9 %multiply_reduce_fusion = (f32[2,16,512]{2,1,0:T(8,128)S(1)}, f32[2,16,512,1024]{3,2,1,0:T(8,128)}) fusion(bf16[2,512,16,72]{1,3,2,0:T(8,128)(2,1)} %get-tuple-element.58, bf16[2,1024,16,72]{1,3,2,0:T(8,128)(2,1)} %all-gather.11.cloned.1.call-done), kind=kOutput, calls=%fused_computation.6 | convolution fusion | flops 2449457152 | bytes 74252288 | tf_op jit(solution)/shard_map/bqhd,bkhd->bhqk/dot_general | solution.py:129
  178.5 21.3 %fusion = f32[2,16,512]{2,1,0:T(8,128)S(1)} fusion(f32[2,16,512,1024]{3,2,1,0:T(8,128)} %get-tuple-element.79, f32[2,16,512]{2,1,0:T(8,128)S(1)} %broadcast_maximum_fusion), kind=kLoop, calls=%fused_computation.3 | loop fusion | flops 50315264 | bytes 67239936 | tf_op jit(solution)/shard_map/reduce_sum | solution.py:134
  199.8 13.9 %all-gather.9.cloned.1.call-done = bf16[2,1024,16,72]{1,3,2,0:T(8,128)(2,1)} async-done(((bf16[2,512,16,72]{1,3,2,0:T(8,128)(2,1)}), bf16[2,1024,16,72]{1,3,2,0:T(8,128)(2,1)}) %all-gather.9.cloned.1.call-update) | async-done | bytes 4718608 | tf_op jit(solution)/shard_map/all_gather | solution.py:127
  213.7 28.0 %fusion.99 = (bf16[2,512,16,72]{1,3,2,0:T(8,128)(2,1)}, f32[2,512,16,72]{1,3,2,0:T(8,128)}) fusion(f32[2,512,16]{1,2,0:T(8,128)S(1)} %bitcast.147, bf16[2,1024,16,72]{1,3,2,0:T(8,128)(2,1)} %all-gather.9.cloned.1.call-done, f32[2,16,512,1024]{3,2,1,0:T(8,128)} %get-tuple-element.79, f32[2,16,512]{2,1,0:T(8,128)S(1)} %broadcast_maximum_fusion), kind=kOutput, calls=%fused_computation.182 | convolution fusion | flops 2468610048 | bytes 79036416 | tf_op jit(solution)/shard_map/bhqk,bkhd->bqhd/dot_general | solution.py:135
  241.7 8.7 multiply_reduce_fusion.9
  250.5 24.7 %fusion.12 = f32[2,512,6144]{2,1,0:T(8,128)} fusion(bf16[1152,6144]{1,0:T(8,128)(2,1)} %param.32, f32[2,512,1152]{2,1,0:T(8,128)S(1)} %get-tuple-element.31, f32[2,1152]{1,0:T(2,128)S(1)} %get-tuple-element.62, f32[2,1152]{1,0:T(2,128)S(1)} %get-tuple-element.63, f32[2,512]{1,0:T(2,128)S(1)} %add_rsqrt_fusion.2), kind=kOutput, calls=%fused_computation.17 | convolution fusion | flops 14500233216 | bytes 44062720 | tf_op jit(solution)/shard_map/bpd,de->bpe/dot_general | solution.py:150
  275.2 21.9 %multiply_convert_fusion.2 = (bf16[2,512,3072]{2,1,0:T(8,128)(2,1)}, bf16[2,512,3072]{2,1,0:T(8,128)(2,1)}, bf16[2,512,3072]{2,1,0:T(8,128)(2,1)}) fusion(f32[2,512,6144]{2,1,0:T(8,128)} %fusion.12, bf16[3072,1152]{1,0:T(8,128)(2,1)} %param.33, bf16[2,512,1152]{2,1,0:T(8,128)(2,1)S(1)} %copy-done.53, f32[2,1152]{1,0:T(2,128)S(1)} %copy-done.35), kind=kOutput, calls=%fused_computation.21 | convolution fusion | flops 7298482176 | bytes 53486592 | tf_op jit(solution)/shard_map/bpd,fd->bpf/dot_general | solution.py:162
  297.1 25.8 %multiply_reduce_fusion.3 = (bf16[2,1152]{1,0:T(2,128)(2,1)}, f32[2,512]{1,0:T(2,128)S(1)}, bf16[2,1152]{1,0:T(2,128)(2,1)}, f32[2,512,1152]{2,1,0:T(8,128)}) fusion(f32[2,512,1152]{2,1,0:T(8,128)} %copy-done.56, f32[2,512]{1,0:T(2,128)S(1)} %add_rsqrt_fusion.2, f32[2,1152]{1,0:T(2,128)S(1)} %get-tuple-element.63, bf16[1152,6144]{1,0:T(8,128)(2,1)} %param.32, ...), kind=kOutput, calls=%fused_computation.76 | convolution fusion | flops 14528932864 | bytes 36202496 | tf_op jit(solution)/shard_map/bpe,de->bpd/dot_general | solution.py:171
  322.8 19.0 %fusion.39 = (bf16[2,1152]{1,0:T(2,128)(2,1)}, bf16[2,512,1152]{2,1,0:T(8,128)(2,1)}, bf16[2,1152]{1,0:T(2,128)(2,1)}, f32[2,512,1152]{2,1,0:T(8,128)S(1)}) fusion(bf16[2,512,1152]{2,1,0:T(8,128)(2,1)} %param.18, f32[2,512,1152]{2,1,0:T(8,128)} %copy-done.56, f32[2,1152]{1,0:T(2,128)S(1)} %copy-done.35, f32[2,512,1152]{2,1,0:T(8,128)} %get-tuple-element.82, ...), kind=kOutput, calls=%fused_computation.61 | convolution fusion | flops 7264268288 | bytes 36998144 | tf_op jit(solution)/shard_map/bpf,fd->bpd/dot_general | solution.py:156
  344.0 4.5 fusion.19
  348.4 7.3 convolution_convert_fusion
  362.4 40.3 %multiply_convert_fusion = bf16[2,16,512,1024]{3,2,1,0:T(8,128)(2,1)} fusion(f32[2,16,512,1024]{3,2,1,0:T(8,128)} %get-tuple-element.79, f32[2,16,512]{2,1,0:T(8,128)S(1)} %bitcast.146, f32[2,16,512]{2,1,0:T(8,128)S(1)} %log_add_fusion, bf16[2,512,16,72]{1,3,2,0:T(8,128)(2,1)S(1)} %bitcast.135, bf16[2,1024,16,72]{1,3,2,0:T(8,128)(2,1)} %all-gather.9.cloned.1.call-done), kind=kOutput, calls=%fused_computation | convolution fusion | flops 2499805184 | bytes 107872256 | tf_op jit(solution)/shard_map/bqhd,bkhd->bhqk/dot_general | solution.py:194
  402.7 19.5 %fusion.40 = bf16[2,1024,16,72]{1,3,2,0:T(8,128)(2,1)} fusion(bf16[2,512,16,72]{1,3,2,0:T(8,128)(2,1)} %get-tuple-element.58, bf16[2,16,512,1024]{3,2,1,0:T(8,128)(2,1)} %multiply_convert_fusion), kind=kOutput, calls=%fused_computation.62 | convolution fusion | flops 2420637696 | bytes 40632320 | tf_op jit(solution)/shard_map/bhqk,bqhd->bkhd/dot_general | solution.py:203
  422.3 27.1 %convert_bitcast_fusion = bf16[2,1024,16,72]{1,3,2,0:T(8,128)(2,1)} fusion(bf16[2,512,16,72]{1,3,2,0:T(8,128)(2,1)S(1)} %bitcast.136, f32[2,16,512,1024]{3,2,1,0:T(8,128)} %get-tuple-element.79, f32[2,16,512]{2,1,0:T(8,128)S(1)} %log_add_fusion), kind=kOutput, calls=%fused_computation.78 | convolution fusion | flops 2468610048 | bytes 74252288 | tf_op jit(solution)/shard_map/bhqk,bqhd->bkhd/dot_general | solution.py:206
  451.5 12.3 %bitcast_convert_fusion.1 = bf16[3072,1152]{1,0:T(8,128)(2,1)} fusion(bf16[2,512,3072]{2,1,0:T(8,128)(2,1)} %get-tuple-element.34, bf16[2,512,1152]{2,1,0:T(8,128)(2,1)S(1)} %copy-done.54, f32[2,1152]{1,0:T(2,128)S(1)} %copy-done.35), kind=kOutput, calls=%fused_computation.14 | convolution fusion | flops 7254835200 | bytes 15737856 | tf_op jit(solution)/shard_map/bpf,bpd->fd/dot_general | solution.py:161
  464.7 20.7 %bitcast_multiply_fusion = (f32[2,512,16,72]{1,3,2,0:T(8,128)}, f32[2,16,72,512]{3,2,1,0:T(8,128)}) fusion(f32[512,72]{0,1:T(8,128)S(1)} %copy-done.10, bf16[2,1024,16,72]{1,3,2,0:T(8,128)(2,1)} %all-gather.11.cloned.1.call-done, bf16[2,16,512,1024]{3,2,1,0:T(8,128)(2,1)} %multiply_convert_fusion), kind=kOutput, calls=%fused_computation.71 | convolution fusion | flops 2417098752 | bytes 47857664 | tf_op jit(solution)/shard_map/bhqk,bkhd->bqhd/dot_general | solution.py:199
  485.4 4.6 fusion.94
  505.0 4.0 multiply_convert_fusion.5
  509.0 4.4 copy.57
  513.4 31.4 %reduce-scatter.23.cloned.1.call-done = bf16[2,512,16,72]{1,3,2,0:T(8,128)(2,1)} async-done(((bf16[2,1024,16,72]{1,3,2,0:T(8,128)(2,1)}), bf16[2,512,16,72]{1,3,2,0:T(8,128)(2,1)}) %reduce-scatter.23.cloned.1.call-update) | async-done | bytes 2359312 | tf_op jit(solution)/shard_map/reduce_scatter | solution.py:219
  544.8 4.5 copy.58
  549.3 14.1 %fusion.9 = bf16[1152,3456]{1,0:T(8,128)(2,1)} fusion(bf16[2,512,1152]{2,1,0:T(8,128)(2,1)} %copy.58, bf16[2,512,1152]{2,1,0:T(8,128)(2,1)} %copy.57, bf16[2,512,1152]{2,1,0:T(8,128)(2,1)} %copy.56, bf16[2,512,1152]{2,1,0:T(8,128)(2,1)S(1)} %copy-done.8, f32[2,1152]{1,0:T(2,128)S(1)} %copy-done.34, f32[2,1152]{1,0:T(2,128)S(1)} %copy-done.26, ...), kind=kOutput, calls=%fused_computation.13 | convolution fusion | flops 8184840192 | bytes 17422336 | tf_op jit(solution)/shard_map/bpd,bpe->de/dot_general | solution.py:234
  564.1 22.1 %bitcast_convert_fusion = bf16[1152,6144]{1,0:T(8,128)(2,1)} fusion(bf16[2,512,3072]{2,1,0:T(8,128)(2,1)} %get-tuple-element.33, bf16[2,512,3072]{2,1,0:T(8,128)(2,1)} %get-tuple-element.32, f32[2,512,1152]{2,1,0:T(8,128)} %copy-done.56, f32[2,1152]{1,0:T(2,128)S(1)} %copy-done.30, f32[2,1152]{1,0:T(2,128)S(1)} %copy-done.32, f32[2,512]{1,0:T(2,128)S(1)} %copy-done.49), kind=kOutput, calls=%fused_computation.11 | convolution fusion | flops 14532476928 | bytes 31479808 | tf_op jit(solution)/shard_map/bpd,bpe->de/dot_general | solution.py:168
  587.0 22.1 %all-gather.2 = bf16[16,2,1152]{2,1,0:T(2,128)(2,1)S(1)} all-gather(bf16[1,2,1152]{2,1,0:T(2,128)(2,1)S(1)} %fusion.92), channel_id=1, replica_groups=mesh['img'=16,'band'=2] {'img'}, dimensions={0}, use_global_device_ids=true | all-gather | bytes 78336 | tf_op jit(solution)/shard_map/all_gather | solution.py:263
  609.1 17.7 %all-gather = bf16[16,2,256]{2,1,0:T(2,128)(2,1)S(1)} all-gather(bf16[1,2,256]{2,1,0:T(2,128)(2,1)S(1)} %fusion.91), channel_id=1, replica_groups=mesh['img'=16,'band'=2] {'img'}, dimensions={0}, use_global_device_ids=true | all-gather | bytes 17408 | tf_op jit(solution)/shard_map/all_gather | solution.py:266
  628.4 9.3 all-reduce
  639.5 15.8 %fusion.36 = (bf16[2,1152]{1,0:T(2,128)(2,1)S(1)}, f32[2,512]{1,0:T(2,128)S(1)}, bf16[2,1152]{1,0:T(2,128)(2,1)S(1)}, f32[2,512,1152]{2,1,0:T(8,128)}) fusion(bf16[2,512,1152]{2,1,0:T(8,128)(2,1)S(1)} %copy-done.8, f32[2,512]{1,0:T(2,128)S(1)} %copy-done.28, f32[2,1152]{1,0:T(2,128)S(1)} %copy-done.26, bf16[1152,3456]{1,0:T(8,128)(2,1)} %param.28, ...), kind=kOutput, calls=%fused_computation.58 | convolution fusion | flops 8184392704 | bytes 22145024 | tf_op jit(solution)/shard_map/bpe,de->bpd/dot_general | solution.py:237
  657.6 7.7 all-reduce.3
  665.4 93.8 %reduce-scatter.37.cloned.1.call-done = bf16[72,3456]{1,0:T(8,128)(2,1)} async-done(((bf16[1152,3456]{1,0:T(8,128)(2,1)}), bf16[72,3456]{1,0:T(8,128)(2,1)}) %reduce-scatter.37.cloned.1.call-update) | async-done | bytes 497680
  761.5 9.7 fusion.53
  771.2 20.4 %all-gather.1 = bf16[16,2,1152]{2,1,0:T(2,128)(2,1)S(1)} all-gather(bf16[1,2,1152]{2,1,0:T(2,128)(2,1)S(1)} %fusion.53), channel_id=1, replica_groups=mesh['img'=16,'band'=2] {'img'}, dimensions={0}, use_global_device_ids=true | all-gather | bytes 78336 | tf_op jit(solution)/shard_map/all_gather | solution.py:272
  791.6 19.9 %all-gather.3 = bf16[16,2,6912]{2,1,0:T(2,128)(2,1)S(1)} all-gather(bf16[1,2,6912]{2,1,0:T(2,128)(2,1)S(1)} %bitcast.151), channel_id=1, replica_groups=mesh['img'=16,'band'=2] {'img'}, dimensions={0}, use_global_device_ids=true | all-gather | bytes 470016 | tf_op jit(solution)/shard_map/all_gather | solution.py:269
  811.6 20.0 %all-gather.5 = bf16[16,1,72]{2,1,0:T(2,128)(2,1)S(1)} all-gather(bf16[1,1,72]{2,1,0:T(2,128)(2,1)S(1)} %bitcast.155), channel_id=1, replica_groups=mesh['img'=16,'band'=2] {'img'}, dimensions={0}, use_global_device_ids=true | all-gather | bytes 2448 | tf_op jit(solution)/shard_map/all_gather | solution.py:278
  831.6 18.2 %all-gather.4 = bf16[16,1,72]{2,1,0:T(2,128)(2,1)S(1)} all-gather(bf16[1,1,72]{2,1,0:T(2,128)(2,1)S(1)} %bitcast.154), channel_id=1, replica_groups=mesh['img'=16,'band'=2] {'img'}, dimensions={0}, use_global_device_ids=true | all-gather | bytes 2448 | tf_op jit(solution)/shard_map/all_gather | solution.py:275
  853.3 56.9 %reduce-scatter.25.cloned.1.call-done = bf16[72,6144]{1,0:T(8,128)(2,1)} async-done(((bf16[1152,6144]{1,0:T(8,128)(2,1)}), bf16[72,6144]{1,0:T(8,128)(2,1)}) %reduce-scatter.25.cloned.1.call-update) | async-done | bytes 884752 | tf_op jit(solution)/shard_map/reduce_scatter | solution.py:309
  913.9 6.9 fusion.35
  920.7 6.0 reduce-scatter.35.cloned.1.call-done
  928.7 19.5 %reduce-scatter.31.cloned.1.call-done = bf16[1728,72]{1,0:T(8,128)(2,1)} async-done(((bf16[3456,72]{1,0:T(8,128)(2,1)}), bf16[1728,72]{1,0:T(8,128)(2,1)}) %reduce-scatter.31.cloned.1.call-update) | async-done | bytes 248848
  950.2 18.7 %reduce-scatter.27.cloned.1.call-done = bf16[72,3072]{1,0:T(8,128)(2,1)} async-done(((bf16[72,6144]{1,0:T(8,128)(2,1)}), bf16[72,3072]{1,0:T(8,128)(2,1)}) %reduce-scatter.27.cloned.1.call-update) | async-done | bytes 442384 | tf_op jit(solution)/shard_map/reduce_scatter | solution.py:323
  (218 shorter events, 77.3 us)
Async XLA Ops:
  7.2 234.5 %copy-start = (bf16[1152,1152]{1,0:T(8,128)(2,1)S(1)}, bf16[1152,1152]{1,0:T(8,128)(2,1)}, u32[]{:S(2)}) copy-start(bf16[1152,1152]{1,0:T(8,128)(2,1)} %param.31) | copy-start | bytes 7962628
  7.2 141.7 %all-gather.11.cloned.1.call-start = ((), (), s32[]{:S(2)}) async-start(), calls=%async_computation.11 | async-start | bytes 7077888 | tf_op jit(solution)/shard_map/all_gather | solution.py:126
  11.8 7.9 copy-start.23
  11.8 8.5 copy-start.7
  20.3 13.9 %copy-start.33 = (f32[2,1152]{1,0:T(2,128)}, f32[2,1152]{1,0:T(2,128)S(1)}, u32[]{:S(2)}) copy-start(f32[2,1152]{1,0:T(2,128)S(1)} %get-tuple-element.64) | copy-start | bytes 27652
  20.3 230.1 %copy-start.29 = (f32[2,1152]{1,0:T(2,128)}, f32[2,1152]{1,0:T(2,128)S(1)}, u32[]{:S(2)}) copy-start(f32[2,1152]{1,0:T(2,128)S(1)} %get-tuple-element.62) | copy-start | bytes 27652
  20.3 302.5 %copy-start.31 = (f32[2,1152]{1,0:T(2,128)}, f32[2,1152]{1,0:T(2,128)S(1)}, u32[]{:S(2)}) copy-start(f32[2,1152]{1,0:T(2,128)S(1)} %get-tuple-element.63) | copy-start | bytes 27652
  34.2 7.9 copy-start.6
  51.2 9.3 copy-start.16
  61.1 6.1 copy-start.18
  74.8 8.6 copy-start.12
  74.8 8.6 copy-start.14
  83.4 130.3 %all-gather.9.cloned.1.call-start = ((), (), s32[]{:S(2)}) async-start(), calls=%async_computation.10 | async-start | bytes 7077888 | tf_op jit(solution)/shard_map/all_gather | solution.py:127
  91.7 357.8 %reduce-scatter.39.cloned.1.call-start = ((), (), s32[]{:S(2)}) async-start(), calls=%async_computation.21 | async-start | bytes 2820096
  250.4 24.8 %copy-start.56 = (f32[2,512,1152]{2,1,0:T(8,128)}, f32[2,512,1152]{2,1,0:T(8,128)S(1)}, u32[]{:S(2)}) copy-start(f32[2,512,1152]{2,1,0:T(8,128)S(1)} %get-tuple-element.31) | copy-start | bytes 14155780
  250.4 72.4 %copy-start.48 = (f32[2,512]{1,0:T(2,128)}, f32[2,512]{1,0:T(2,128)S(1)}, u32[]{:S(2)}) copy-start(f32[2,512]{1,0:T(2,128)S(1)} %add_rsqrt_fusion.2) | copy-start | bytes 12292
  250.4 24.7 %copy-start.35 = (f32[2,1152]{1,0:T(2,128)S(1)}, f32[2,1152]{1,0:T(2,128)}, u32[]{:S(2)}) copy-start(f32[2,1152]{1,0:T(2,128)} %get-tuple-element.61) | copy-start | bytes 27652
  250.4 24.7 %copy-start.53 = (bf16[2,512,1152]{2,1,0:T(8,128)(2,1)S(1)}, bf16[2,512,1152]{2,1,0:T(8,128)(2,1)}, u32[]{:S(2)}) copy-start(bf16[2,512,1152]{2,1,0:T(8,128)(2,1)} %param.18) | copy-start | bytes 7077892
  322.8 21.1 %copy-start.11 = (bf16[2,512,16,72]{1,3,2,0:T(8,128)(2,1)S(1)}, bf16[2,512,16,72]{1,3,2,0:T(8,128)(2,1)}, u32[]{:S(2)}) copy-start(bf16[2,512,16,72]{1,3,2,0:T(8,128)(2,1)} %get-tuple-element.80) | copy-start | bytes 7077892
  348.4 7.3 copy-start.22
  355.8 141.7 %reduce-scatter.21.cloned.1.call-start = ((), (), s32[]{:S(2)}) async-start(), calls=%async_computation.12 | async-start | bytes 7077888 | tf_op jit(solution)/shard_map/reduce_scatter | solution.py:216
  422.2 122.6 %reduce-scatter.23.cloned.1.call-start = ((), (), s32[]{:S(2)}) async-start(), calls=%async_computation.13 | async-start | bytes 7077888 | tf_op jit(solution)/shard_map/reduce_scatter | solution.py:219
  449.4 188.3 %reduce-scatter.33.cloned.1.call-start = ((), (), s32[]{:S(2)}) async-start(), calls=%async_computation.18 | async-start | bytes 442368
  451.5 203.9 %reduce-scatter.29.cloned.1.call-start = ((), (), s32[]{:S(2)}) async-start(), calls=%async_computation.16 | async-start | bytes 7520256 | tf_op jit(solution)/shard_map/reduce_scatter | solution.py:312
  463.8 26.2 %slice-start = ((s8[4718592]{0:T(1024)(128)(4,1)}), s8[524288]{0:T(1024)(128)(4,1)S(1)}, s32[]{:S(2)}) async-start(s8[4718592]{0:T(1024)(128)(4,1)} %bitcast.124), calls=%async_computation.22 | async-start | bytes 1048576
  463.8 295.3 %reduce-scatter.37.cloned.1.call-start = ((), (), s32[]{:S(2)}) async-start(), calls=%async_computation.20 | async-start | bytes 8460288
  464.7 25.3 %slice-start.1 = ((s8[4718592]{0:T(1024)(128)(4,1)}), s8[4194304]{0:T(1024)(128)(4,1)S(1)}, s32[]{:S(2)}) async-start(s8[4718592]{0:T(1024)(128)(4,1)} %bitcast.124), calls=%async_computation.23 | async-start | bytes 8388608
  485.4 4.7 copy-start.5
  485.4 4.7 copy-start.19
  485.4 4.7 copy-start.20
  485.4 4.7 copy-start.37
  509.0 40.3 %copy-start.8 = (bf16[2,512,1152]{2,1,0:T(8,128)(2,1)S(1)}, bf16[2,512,1152]{2,1,0:T(8,128)(2,1)}, u32[]{:S(2)}) copy-start(bf16[2,512,1152]{2,1,0:T(8,128)(2,1)} %param.17) | copy-start | bytes 7077892
  509.0 40.3 %copy-start.26 = (f32[2,1152]{1,0:T(2,128)S(1)}, f32[2,1152]{1,0:T(2,128)}, u32[]{:S(2)}) copy-start(f32[2,1152]{1,0:T(2,128)} %copy-done.25) | copy-start | bytes 27652
  509.0 40.3 %copy-start.28 = (f32[2,512]{1,0:T(2,128)S(1)}, f32[2,512]{1,0:T(2,128)}, u32[]{:S(2)}) copy-start(f32[2,512]{1,0:T(2,128)} %copy-done.27) | copy-start | bytes 12292
  509.0 40.3 %copy-start.34 = (f32[2,1152]{1,0:T(2,128)S(1)}, f32[2,1152]{1,0:T(2,128)}, u32[]{:S(2)}) copy-start(f32[2,1152]{1,0:T(2,128)} %copy-done.33) | copy-start | bytes 27652
  563.4 346.8 %reduce-scatter.25.cloned.1.call-start = ((), (), s32[]{:S(2)}) async-start(), calls=%async_computation.14 | async-start | bytes 15040512 | tf_op jit(solution)/shard_map/reduce_scatter | solution.py:309
  586.2 22.8 %copy-start.41 = (bf16[2,128]{1,0:T(2,128)(2,1)S(1)}, bf16[2,128]{1,0:T(2,128)(2,1)}, u32[]{:S(2)}) copy-start(bf16[2,128]{1,0:T(2,128)(2,1)} %copy-done.40) | copy-start | bytes 1540
  586.2 22.9 %copy-start.43 = (bf16[2,128]{1,0:T(2,128)(2,1)S(1)}, bf16[2,128]{1,0:T(2,128)(2,1)}, u32[]{:S(2)}) copy-start(bf16[2,128]{1,0:T(2,128)(2,1)} %copy-done.42) | copy-start | bytes 1540
  586.3 40.6 %copy-start.55 = (u32[32]{0:T(128)S(1)}, u32[32]{0:T(128)}, u32[]{:S(2)}) copy-start(u32[32]{0:T(128)} %constant.77) | copy-start | bytes 388
  586.3 41.9 %copy-start.52 = (s32[2]{0:T(128)S(1)}, s32[2]{0:T(128)}, u32[]{:S(2)}) copy-start(s32[2]{0:T(128)} %param.19) | copy-start | bytes 28
  586.3 340.4 %reduce-scatter.35.cloned.1.call-start = ((), (), s32[]{:S(2)}) async-start(), calls=%async_computation.19 | async-start | bytes 884736
  639.5 18.0 %copy-start.47 = (bf16[2,1152]{1,0:T(2,128)(2,1)S(1)}, bf16[2,1152]{1,0:T(2,128)(2,1)}, u32[]{:S(2)}) copy-start(bf16[2,1152]{1,0:T(2,128)(2,1)} %get-tuple-element.39) | copy-start | bytes 13828
  639.5 18.1 %copy-start.45 = (bf16[2,1152]{1,0:T(2,128)(2,1)S(1)}, bf16[2,1152]{1,0:T(2,128)(2,1)}, u32[]{:S(2)}) copy-start(bf16[2,1152]{1,0:T(2,128)(2,1)} %get-tuple-element.20) | copy-start | bytes 13828
  639.5 18.1 %copy-start.44 = (bf16[2,1152]{1,0:T(2,128)(2,1)S(1)}, bf16[2,1152]{1,0:T(2,128)(2,1)}, u32[]{:S(2)}) copy-start(bf16[2,1152]{1,0:T(2,128)(2,1)} %get-tuple-element.16) | copy-start | bytes 13828
  639.5 18.1 %copy-start.46 = (bf16[2,1152]{1,0:T(2,128)(2,1)S(1)}, bf16[2,1152]{1,0:T(2,128)(2,1)}, u32[]{:S(2)}) copy-start(bf16[2,1152]{1,0:T(2,128)(2,1)} %get-tuple-element.37) | copy-start | bytes 13828
  657.5 290.7 %reduce-scatter.31.cloned.1.call-start = ((), (), s32[]{:S(2)}) async-start(), calls=%async_computation.17 | async-start | bytes 1327104
  761.4 207.4 %reduce-scatter.27.cloned.1.call-start = ((), (), s32[]{:S(2)}) async-start(), calls=%async_computation.15 | async-start | bytes 1327104 | tf_op jit(solution)/shard_map/reduce_scatter | solution.py:323
  913.9 57.0 %copy-start.1 = (bf16[1152,1152]{1,0:T(8,128)(2,1)S(1)}, bf16[1152,1152]{1,0:T(8,128)(2,1)}, u32[]{:S(2)}) copy-start(bf16[1152,1152]{1,0:T(8,128)(2,1)} %param.31) | copy-start | bytes 7962628
  (25 other events, 51.1 us)
Sparse Core Ops, SparseCore 0:
  83.5 65.3 all-gather.10
  151.0 62.6 all-gather.8
  355.9 63.8 reduce-scatter.38
  422.3 60.2 reduce-scatter.20
  484.8 59.9 reduce-scatter.22
  547.6 12.0 reduce-scatter.32
  564.2 90.3 reduce-scatter.28
  658.7 100.4 reduce-scatter.36
  763.9 146.2 reduce-scatter.24
  912.4 14.2 reduce-scatter.34
  929.6 18.5 reduce-scatter.30
  950.3 18.5 reduce-scatter.26
where the time goes:
time: 983 us; the launch traced here: 978 us
  matrix products  381 us (39%)
  waiting for transfers between devices  297 us (30%)
  blocking collectives  135 us (14%)
  other arithmetic  75.2 us (8%)
  local copies, waits for them, and re-layouts  72.9 us (7%)
  between operations  16.1 us (2%)
    unnamed x17, waiting for transfers between devices  119 us
    all_gather x1, waiting for transfers between devices, per_device(): key_piece = lax.all_gather(key_bf, 'band', axis=1, tiled=True)  57.1 us
    reduce_scatter x1, waiting for transfers between devices, per_device(): lax.psum_scatter(grad_gateup.astype(jnp.bfloat16), 'img', scatter_dimensi...  56.9 us
    dot_general x1, matrix products, per_device(): jnp.einsum('bqhd,bkhd->bhqk', mixed_grad_bf, value_piece, preferred_eleme...  40.3 us
    reduce_scatter x1, waiting for transfers between devices, per_device(): lax.psum_scatter(value_grads.astype(jnp.bfloat16), 'band', scatter_dimens...  31.4 us
    dot_general x1, matrix products, per_device(): jnp.einsum('bqhd,bkhd->bhqk', query_bf, key_piece, preferred_element_type...  28.9 us
    dot_general x1, matrix products, per_device(): jnp.einsum('bhqk,bkhd->bqhd', weights.astype(jnp.bfloat16), value_piece,...  28 us
    dot_general x1, matrix products, per_device(): jnp.einsum('bhqk,bqhd->bkhd', probs.astype(jnp.bfloat16), mixed_grad_bf,...  27.1 us
  transfers between devices with their start and end apart: 12, of which 8 were waited for; matrix products, arithmetic and copies ran while one was open for 31% of the time, Pallas kernels for 0%

commit v1 on v0

--- a/solution.py
+++ b/solution.py
@@ -3,6 +3,8 @@
 import jax
 import jax.numpy as jnp
 from jax import lax
+from jax.experimental import pallas as pl
+from jax.experimental.pallas import tpu as pltpu
 from jax.sharding import PartitionSpec as P
 
 HEADS = 16
@@ -63,7 +65,7 @@
     return sigma * (1.0 + values * (1.0 - sigma))
 
 
-def per_device(
+def per_device_banded(
     latents,
     cotangent,
     labels,
@@ -343,6 +345,712 @@
     )
 
 
+HDP = 80
+LOG2E = math.log2(math.e)
+VMEM_MAX = 62 * 2**20
+bf16 = jnp.bfloat16
+f32 = jnp.float32
+
+
+def dot(left, right, left_dim, right_dim):
+    return lax.dot_general(
+        left, right, (((left_dim,), (right_dim,)), ((), ())), preferred_element_type=f32
+    )
+
+
+def params_of(**extra):
+    return pltpu.CompilerParams(vmem_limit_bytes=VMEM_MAX, **extra)
+
+
+def whole(shape):
+    return pl.BlockSpec(shape, lambda *_: (0,) * len(shape), pipeline_mode=pl.Buffered(1))
+
+
+def cost(flops, bytes_accessed, transcendentals=0):
+    return pl.CostEstimate(
+        flops=int(flops), bytes_accessed=int(bytes_accessed), transcendentals=int(transcendentals)
+    )
+
+
+def partner_rows(values, low_half):
+    quarter = HD // 4
+    return jnp.where(
+        low_half, pltpu.roll(values, HD - quarter, 0), pltpu.roll(values, quarter, 0)
+    )
+
+
+def low_half_mask(patches):
+    row = lax.broadcasted_iota(jnp.int32, (HD, patches), 0)
+    quarter = HD // 4
+    return (row < quarter) | ((row >= 2 * quarter) & (row < 3 * quarter))
+
+
+def tail_rows(first, second, patches):
+    row = lax.broadcasted_iota(jnp.int32, (HDP - HD, patches), 0)
+    return jnp.where(row == 0, first, jnp.where(row == 1, second, 0.0))
+
+
+def split_two(values):
+    high = values.astype(bf16).astype(f32)
+    return high, values - high
+
+
+def front_kernel(
+    x_ref, scale_ref, shift_ref, w_ref, gains_ref, cos_ref, sin_ref,
+    entry_ref, heads_ref, unit_ref, factor_ref,
+):
+    section = pl.program_id(0)
+    patches = x_ref.shape[0]
+
+    @pl.when(section == 0)
+    def _():
+        source = x_ref[...].astype(f32)
+        normed = source * lax.rsqrt(jnp.mean(source * source, axis=1, keepdims=True) + epsilon)
+        entry_ref[...] = (normed * (1.0 + scale_ref[...]) + shift_ref[...]).astype(bf16)
+
+    raw = dot(w_ref[...], entry_ref[...], 0, 1)
+
+    @pl.when(section < 2)
+    def _():
+        mask = low_half_mask(patches)
+        extra = tail_rows(*[jnp.where(section == 1, 1.0, 0.0)] * 2, patches)
+        gain = gains_ref[0]
+        for head in range(HEADS):
+            part = raw[head * HD : (head + 1) * HD, :]
+            factor = lax.rsqrt(jnp.mean(part * part, axis=0, keepdims=True) + epsilon)
+            unit = part * factor
+            scaled = unit * gain
+            turned = scaled * cos_ref[...] + partner_rows(scaled, mask) * sin_ref[...]
+            heads_ref[0, head] = jnp.concatenate([turned, extra], axis=0).astype(bf16)
+            unit_ref[0, head] = unit.astype(bf16)
+            factor_ref[0, head] = factor
+
+    @pl.when(section == 2)
+    def _():
+        extra = tail_rows(1.0, 1.0, patches)
+        for head in range(HEADS):
+            part = raw[head * HD : (head + 1) * HD, :]
+            heads_ref[0, head] = jnp.concatenate([part, extra], axis=0).astype(bf16)
+
+
+def front(x, scale, shift, qkv_weight, gains, cosine, sine):
+    patches, width = x.shape
+    last = lambda s: jnp.minimum(s, 1)
+    return pl.pallas_call(
+        front_kernel,
+        grid=(3,),
+        in_specs=[
+            whole((patches, width)),
+            whole((1, width)),
+            whole((1, width)),
+            pl.BlockSpec((width, width), lambda s: (0, s)),
+            pl.BlockSpec((1, HD, 1), lambda s: (last(s), 0, 0)),
+            whole((HD, patches)),
+            whole((HD, patches)),
+        ],
+        out_specs=[
+            pl.BlockSpec((patches, width), lambda s: (0, 0)),
+            pl.BlockSpec((1, HEADS, HDP, patches), lambda s: (s, 0, 0, 0)),
+            pl.BlockSpec((1, HEADS, HD, patches), lambda s: (last(s), 0, 0, 0)),
+            pl.BlockSpec((1, HEADS, 1, patches), lambda s: (last(s), 0, 0, 0)),
+        ],
+        out_shape=[
+            jax.ShapeDtypeStruct((patches, width), bf16),
+            jax.ShapeDtypeStruct((3, HEADS, HDP, patches), bf16),
+            jax.ShapeDtypeStruct((2, HEADS, HD, patches), bf16),
+            jax.ShapeDtypeStruct((2, HEADS, 1, patches), f32),
+        ],
+        compiler_params=params_of(),
+        cost_estimate=cost(6 * patches * width * width, 24e6),
+        name="front",
+    )(x, scale, shift, qkv_weight, gains, cosine, sine)
+
+
+def attend_kernel(q_ref, k_ref, v_ref, mixed_ref, lse_ref, qext_ref):
+    patches = q_ref.shape[-1]
+    step = patches // 2
+    key = k_ref[...]
+    value = v_ref[...]
+    for start in range(0, patches, step):
+        columns = slice(start, start + step)
+        scores = dot(key, q_ref[:, columns], 0, 0)
+        weights = jnp.exp2(scores).astype(bf16)
+        summed = dot(value, weights, 1, 0)
+        total = summed[HD : HD + 1, :]
+        mixed_ref[:, columns] = (summed[:HD, :] / total).astype(bf16)
+        high, low = split_two(-jnp.log2(total))
+        extra = jnp.concatenate([jnp.zeros((HD, step), f32), tail_rows(high, low, step)], axis=0)
+        qext_ref[:, columns] = q_ref[:, columns] + extra.astype(bf16)
+
+
+def attend(heads):
+    patches = heads.shape[-1]
+    section = lambda member: pl.BlockSpec(
+        (None, None, HDP, patches), lambda h: (member, h, 0, 0)
+    )
+    return pl.pallas_call(
+        lambda q, k, v, mixed, qext: attend_kernel(q, k, v, mixed, None, qext),
+        grid=(HEADS,),
+        in_specs=[section(0), section(1), section(2)],
+        out_specs=[
+            pl.BlockSpec((None, HD, patches), lambda h: (h, 0, 0)),
+            pl.BlockSpec((None, HDP, patches), lambda h: (h, 0, 0)),
+        ],
+        out_shape=[
+            jax.ShapeDtypeStruct((HEADS, HD, patches), bf16),
+            jax.ShapeDtypeStruct((HEADS, HDP, patches), bf16),
+        ],
+        compiler_params=params_of(),
+        cost_estimate=cost(8 * HEADS * patches * patches * HDP, 14e6, HEADS * patches * patches),
+        name="attend",
+    )(heads, heads, heads)
+
+
+def middle_kernel(
+    mixed_ref, w_ref, x_ref, c_ref, vectors_ref, attended_ref, entry_ref, fed_grad_ref
+):
+    attended = dot(mixed_ref[...], w_ref[...], 0, 0)
+    attended_bf = attended.astype(bf16)
+    attended_ref[...] = attended_bf
+    gate_one, scale_two, shift_two, gate_two = [vectors_ref[i : i + 1, :] for i in range(4)]
+    middle = x_ref[...].astype(f32) + gate_one * attended_bf.astype(f32)
+    normed = middle * lax.rsqrt(jnp.mean(middle * middle, axis=1, keepdims=True) + epsilon)
+    entry_ref[...] = (normed * (1.0 + scale_two) + shift_two).astype(bf16)
+    fed_grad_ref[...] = (c_ref[...].astype(f32) * gate_two).astype(bf16)
+
+
+def middle_step(mixed, proj_weight, x, c, vectors):
+    patches, width = x.shape
+    rows = 256
+    block = pl.BlockSpec((rows, width), lambda t: (t, 0))
+    return pl.pallas_call(
+        middle_kernel,
+        grid=(patches // rows,),
+        in_specs=[
+            pl.BlockSpec((width, rows), lambda t: (0, t)),
+            whole((width, width)),
+            block,
+            block,
+            whole((8, width)),
+        ],
+        out_specs=[block] * 3,
+        out_shape=[jax.ShapeDtypeStruct((patches, width), bf16)] * 3,
+        compiler_params=params_of(),
+        cost_estimate=cost(2 * patches * width * width, 17e6),
+        name="middle",
+    )(mixed, proj_weight, x, c, vectors)
+
+
+def mlp_kernel(
+    entry_ref, fed_grad_ref, wg_ref, wu_ref, wd_ref,
+    fed_ref, entry_grad_ref, down_ref, gate_out_ref, up_out_ref,
+    hidden_ref, gate_grad_ref, up_grad_ref,
+):
+    tile = pl.program_id(0)
+    entry = entry_ref[...]
+    fed_grad = fed_grad_ref[...]
+    gate = dot(entry, wg_ref[...], 1, 0)
+    up = dot(entry, wu_ref[...], 1, 0)
+    sigma = jax.nn.sigmoid(gate)
+    silu = gate * sigma
+    hidden_ref[...] = (silu * up).astype(bf16)
+    hidden_grad = dot(fed_grad, wd_ref[...], 1, 1)
+    gate_grad_ref[...] = (hidden_grad * up * (sigma * (1.0 + gate * (1.0 - sigma)))).astype(bf16)
+    up_grad_ref[...] = (hidden_grad * silu).astype(bf16)
+    fed = dot(hidden_ref[...], wd_ref[...], 1, 0)
+    entry_grad = dot(gate_grad_ref[...], wg_ref[...], 1, 1) + dot(
+        up_grad_ref[...], wu_ref[...], 1, 1
+    )
+
+    @pl.when(tile == 0)
+    def _():
+        fed_ref[...] = fed
+        entry_grad_ref[...] = entry_grad
+
+    @pl.when(tile > 0)
+    def _():
+        fed_ref[...] += fed
+        entry_grad_ref[...] += entry_grad
+
+    down_ref[...] = dot(hidden_ref[...], fed_grad, 0, 0).astype(bf16)
+    gate_out_ref[...] = dot(entry, gate_grad_ref[...], 0, 0).astype(bf16)
+    up_out_ref[...] = dot(entry, up_grad_ref[...], 0, 0).astype(bf16)
+
+
+def mlp(entry, fed_grad, gateup_weight, down_weight):
+    patches, width = entry.shape
+    inner = down_weight.shape[0]
+    tile = 512
+    tiles = inner // tile
+    return pl.pallas_call(
+        mlp_kernel,
+        grid=(tiles,),
+        in_specs=[
+            whole((patches, width)),
+            whole((patches, width)),
+            pl.BlockSpec((width, tile), lambda t: (0, t)),
+            pl.BlockSpec((width, tile), lambda t: (0, tiles + t)),
+            pl.BlockSpec((tile, width), lambda t: (t, 0)),
+        ],
+        out_specs=[
+            pl.BlockSpec((patches, width), lambda t: (0, 0)),
+            pl.BlockSpec((patches, width), lambda t: (0, 0)),
+            pl.BlockSpec((tile, width), lambda t: (t, 0)),
+            pl.BlockSpec((width, tile), lambda t: (0, t)),
+            pl.BlockSpec((width, tile), lambda t: (0, t)),
+        ],
+        out_shape=[
+            jax.ShapeDtypeStruct((patches, width), f32),
+            jax.ShapeDtypeStruct((patches, width), f32),
+            jax.ShapeDtypeStruct((inner, width), bf16),
+            jax.ShapeDtypeStruct((width, inner), bf16),
+            jax.ShapeDtypeStruct((width, inner), bf16),
+        ],
+        scratch_shapes=[pltpu.VMEM((patches, tile), bf16)] * 3,
+        compiler_params=params_of(),
+        cost_estimate=cost(18 * patches * width * inner, 56e6),
+        name="mlp",
+    )(entry, fed_grad, gateup_weight, gateup_weight, down_weight)
+
+
+def turn_kernel(
+    fed_ref, entry_grad_ref, x_ref, attended_ref, c_ref, mixed_ref, w_ref, vectors_ref,
+    result_ref, middle_grad_ref, mixed_grad_ref, grad_proj_ref, sums_ref, total_ref,
+):
+    step = pl.program_id(0)
+    gate_one, scale_two, _, gate_two = [vectors_ref[i : i + 1, :] for i in range(4)]
+    attended = attended_ref[...].astype(f32)
+    upstream = c_ref[...].astype(f32)
+    fed = fed_ref[...]
+    middle = x_ref[...].astype(f32) + gate_one * attended
+    result_ref[...] = (middle + gate_two * fed).astype(bf16)
+    factor = lax.rsqrt(jnp.mean(middle * middle, axis=1, keepdims=True) + epsilon)
+    normed = middle * factor
+    entry_grad = entry_grad_ref[...]
+    inner = entry_grad * (1.0 + scale_two)
+    middle_grad = upstream + factor * (
+        inner - normed * jnp.mean(inner * normed, axis=1, keepdims=True)
+    )
+    middle_grad_ref[...] = middle_grad
+    attended_grad = (middle_grad * gate_one).astype(bf16)
+    mixed_grad_ref[...] = dot(w_ref[...], attended_grad, 1, 1).astype(bf16)
+    grad_proj = dot(mixed_ref[...], attended_grad, 1, 0)
+    add = lambda v: jnp.sum(v, axis=0, keepdims=True)
+    sums = jnp.concatenate(
+        [
+            add(middle_grad * attended),
+            add(entry_grad),
+            add(entry_grad * normed),
+            add(upstream * fed),
+            jnp.zeros((4, fed.shape[1]), f32),
+        ],
+        axis=0,
+    )
+
+    @pl.when(step == 0)
+    def _():
+        total_ref[...] = grad_proj
+        sums_ref[...] = sums
+
+    @pl.when(step > 0)
+    def _():
+        total_ref[...] += grad_proj
+        sums_ref[...] += sums
+
+    @pl.when(step == pl.num_programs(0) - 1)
+    def _():
+        grad_proj_ref[...] = total_ref[...].astype(bf16)
+
+
+def turn_step(fed, entry_grad, x, attended, c, mixed, proj_weight, vectors):
+    patches, width = x.shape
+    rows = 256
+    block = pl.BlockSpec((rows, width), lambda t: (t, 0))
+    across = pl.BlockSpec((width, rows), lambda t: (0, t))
+    return pl.pallas_call(
+        turn_kernel,
+        grid=(patches // rows,),
+        in_specs=[block] * 5 + [across, whole((width, width)), whole((8, width))],
+        out_specs=[
+            block,
+            block,
+            across,
+            pl.BlockSpec((width, width), lambda t: (0, 0)),
+            pl.BlockSpec((8, width), lambda t: (0, 0)),
+        ],
+        out_shape=[
+            jax.ShapeDtypeStruct((patches, width), bf16),
+            jax.ShapeDtypeStruct((patches, width), f32),
+            jax.ShapeDtypeStruct((width, patches), bf16),
+            jax.ShapeDtypeStruct((width, width), bf16),
+            jax.ShapeDtypeStruct((8, width), f32),
+        ],
+        scratch_shapes=[pltpu.VMEM((width, width), f32)],
+        compiler_params=params_of(),
+        cost_estimate=cost(4 * patches * width * width, 35e6),
+        name="turn",
+    )(fed, entry_grad, x, attended, c, mixed, proj_weight, vectors)
+
+
+def attend_back_kernel(
+    q_ref, k_ref, v_ref, mg_ref, mixed_ref, unit_ref, factor_ref, gains_ref, cos_ref, sin_ref,
+    out_ref, gain_out_ref, mg_ext_ref, acc_ref,
+):
+    head = pl.program_id(0)
+    patches = q_ref.shape[-1]
+    step = patches // 2
+    scaling = HD ** (-0.5)
+    mixed_grad = mg_ref[...].astype(f32)
+    offsets = jnp.sum(mixed_grad * mixed_ref[...].astype(f32), axis=0, keepdims=True)
+    high, low = split_two(-offsets)
+    mg_ext_ref[...] = jnp.concatenate(
+        [mixed_grad, tail_rows(high, low, patches)], axis=0
+    ).astype(bf16)
+    key = k_ref[...]
+    value = v_ref[...]
+    for start in range(0, patches, step):
+        columns = slice(start, start + step)
+        query = q_ref[:, columns]
+        grads = mg_ext_ref[:, columns]
+        probs = jnp.exp2(dot(key, query, 0, 0))
+        score_grad = (probs * dot(value, grads, 0, 0)).astype(bf16)
+        probs_bf = probs.astype(bf16)
+        acc_ref[0, :, columns] = dot(key, score_grad, 1, 0)
+        key_term = dot(query, score_grad, 1, 1)
+        value_term = dot(grads, probs_bf, 1, 1)
+        if start == 0:
+            acc_ref[1] = key_term
+            acc_ref[2] = value_term
+        else:
+            acc_ref[1] += key_term
+            acc_ref[2] += value_term
+    mask = low_half_mask(patches)
+    for member, weight in ((0, scaling), (1, 1.0 / LOG2E)):
+        grads = acc_ref[member, :HD, :] * weight
+        turned = grads * cos_ref[...] + partner_rows(grads * sin_ref[...], mask)
+        unit = unit_ref[member].astype(f32)
+        product = turned * unit
+
+        @pl.when(head == 0)
+        def _():
+            gain_out_ref[member] = product
+
+        @pl.when(head > 0)
+        def _():
+            gain_out_ref[member] += product
+
+        inner = turned * gains_ref[member]
+        raw = factor_ref[member] * (inner - unit * jnp.mean(inner * unit, axis=0, keepdims=True))
+        out_ref[member] = raw.astype(bf16)
+    out_ref[2] = acc_ref[2, :HD, :].astype(bf16)
+
+
+def attend_back(query, heads, mixed_grad, mixed, unit, factor, gains, cosine, sine):
+    patches = query.shape[-1]
+    section = lambda member: pl.BlockSpec(
+        (None, None, HDP, patches), lambda h: (member, h, 0, 0)
+    )
+    single = lambda rows: pl.BlockSpec((None, rows, patches), lambda h: (h, 0, 0))
+    pair = lambda rows: pl.BlockSpec((2, None, rows, patches), lambda h: (0, h, 0, 0))
+    return pl.pallas_call(
+        attend_back_kernel,
+        grid=(HEADS,),
+        in_specs=[
+            single(HDP),
+            section(1),
+            section(2),
+            single(HD),
+            single(HD),
+            pair(HD),
+            pair(1),
+            whole((2, HD, 1)),
+            whole((HD, patches)),
+            whole((HD, patches)),
+        ],
+        out_specs=[
+            pl.BlockSpec((3, None, HD, patches), lambda h: (0, h, 0, 0)),
+            pl.BlockSpec((2, HD, patches), lambda h: (0, 0, 0)),
+        ],
+        out_shape=[
+            jax.ShapeDtypeStruct((3, HEADS, HD, patches), bf16),
+            jax.ShapeDtypeStruct((2, HD, patches), f32),
+        ],
+        scratch_shapes=[
+            pltpu.VMEM((HDP, patches), bf16),
+            pltpu.VMEM((3, HDP, patches), f32),
+        ],
+        compiler_params=params_of(),
+        cost_estimate=cost(20 * HEADS * patches * patches * HDP, 32e6, HEADS * patches**2),
+        name="attend_back",
+    )(query, heads, heads, mixed_grad, mixed, unit, factor, gains, cosine, sine)
+
+
+def back_kernel(pg_ref, w_ref, entry_ref, grad_ref, entry_grad_ref):
+    section = pl.program_id(0)
+    grad_ref[...] = dot(entry_ref[...], pg_ref[...], 0, 1).astype(bf16)
+    term = dot(w_ref[...], pg_ref[...], 1, 0)
+
+    @pl.when(section == 0)
+    def _():
+        entry_grad_ref[...] = term
+
+    @pl.when(section > 0)
+    def _():
+        entry_grad_ref[...] += term
+
+
+def back_step(projected_grad, qkv_weight, entry):
+    patches, width = entry.shape
+    return pl.pallas_call(
+        back_kernel,
+        grid=(3,),
+        in_specs=[
+            pl.BlockSpec((None, width, patches), lambda s: (s, 0, 0)),
+            pl.BlockSpec((width, width), lambda s: (0, s)),
+            whole((patches, width)),
+        ],
+        out_specs=[
+            pl.BlockSpec((width, width), lambda s: (0, s)),
+            pl.BlockSpec((width, patches), lambda s: (0, 0)),
+        ],
+        out_shape=[
+            jax.ShapeDtypeStruct((width, 3 * width), bf16),
+            jax.ShapeDtypeStruct((width, patches), f32),
+        ],
+        compiler_params=params_of(),
+        cost_estimate=cost(12 * patches * width * width, 32e6),
+        name="back",
+    )(projected_grad, qkv_weight, entry)
+
+
+def last_kernel(entry_grad_ref, x_ref, middle_grad_ref, scale_ref, out_ref, sums_ref):
+    step = pl.program_id(0)
+    entry_grad = entry_grad_ref[...].T
+    source = x_ref[...].astype(f32)
+    factor = lax.rsqrt(jnp.mean(source * source, axis=1, keepdims=True) + epsilon)
+    normed = source * factor
+    inner = entry_grad * (1.0 + scale_ref[...])
+    grads = middle_grad_ref[...] + factor * (
+        inner - normed * jnp.mean(inner * normed, axis=1, keepdims=True)
+    )
+    out_ref[...] = grads.astype(bf16)
+    add = lambda v: jnp.sum(v, axis=0, keepdims=True)
+    sums = jnp.concatenate(
+        [add(entry_grad), add(entry_grad * normed), jnp.zeros((6, source.shape[1]), f32)], axis=0
+    )
+
+    @pl.when(step == 0)
+    def _():
+        sums_ref[...] = sums
+
+    @pl.when(step > 0)
+    def _():
+        sums_ref[...] += sums
+
+
+def last_step(entry_grad, x, middle_grad, scale):
+    patches, width = x.shape
+    rows = 256
+    block = pl.BlockSpec((rows, width), lambda t: (t, 0))
+    return pl.pallas_call(
+        last_kernel,
+        grid=(patches // rows,),
+        in_specs=[
+            pl.BlockSpec((width, rows), lambda t: (0, t)),
+            block,
+            block,
+            whole((1, width)),
+        ],
+        out_specs=[block, pl.BlockSpec((8, width), lambda t: (0, 0))],
+        out_shape=[
+            jax.ShapeDtypeStruct((patches, width), bf16),
+            jax.ShapeDtypeStruct((8, width), f32),
+        ],
+        compiler_params=params_of(),
+        cost_estimate=cost(20 * patches * width, 17e6),
+        name="last",
+    )(entry_grad, x, middle_grad, scale)
+
+
+def pick(values, index):
+    return lax.dynamic_index_in_dim(values, index, 0, keepdims=False)
+
+
+def per_device_whole(
+    latents,
+    cotangent,
+    labels,
+    group_ids,
+    group_logits,
+    row_pos,
+    col_pos,
+    time_weight,
+    class_table,
+    ada_weight,
+    ada_bias,
+    qkv_weight,
+    query_gain,
+    key_gain,
+    proj_weight,
+    gateup_weight,
+    down_weight,
+):
+    width = latents.shape[-1]
+    bands = lax.axis_size("band")
+    img_index = lax.axis_index("img")
+    band_index = lax.axis_index("band")
+    half = latents.shape[1]
+
+    def exchange(own):
+        parts = [pick(own, band_index)]
+        for shift in range(1, bands):
+            pairs = [(i, (i + shift) % bands) for i in range(bands)]
+            away = pick(own, lax.rem(band_index + shift, bands))
+            parts.append(lax.ppermute(away, "band", pairs))
+        return jnp.concatenate(parts, axis=0)
+
+    def give_back(values):
+        back = [values[:half]]
+        for shift in range(1, bands):
+            pairs = [(i, (i - shift) % bands) for i in range(bands)]
+            back.append(
+                lax.ppermute(values[shift * half : (shift + 1) * half], "band", pairs)
+            )
+        stacked = jnp.stack(back)
+        order = lax.rem(jnp.arange(bands) - band_index + bands, bands)
+        return jnp.take(stacked, order, axis=0)
+
+    x = exchange(latents)
+    c = exchange(cotangent)
+    places = jnp.stack([row_pos, col_pos], axis=1)
+    place_parts = [places]
+    for shift in range(1, bands):
+        pairs = [(i, (i + shift) % bands) for i in range(bands)]
+        place_parts.append(lax.ppermute(places, "band", pairs))
+    places = jnp.concatenate(place_parts, axis=0)
+
+    quarter = HD // 4
+    frequency = jnp.exp(-math.log(10000.0) * jnp.arange(quarter, dtype=f32) / quarter)
+    angles = frequency[:, None] * places.astype(f32).T[:, None, :]
+    cosine, sine = jnp.cos(angles), jnp.sin(angles)
+    cosine = jnp.concatenate([cosine[0], cosine[0], cosine[1], cosine[1]], axis=0)
+    sine = jnp.concatenate([-sine[0], sine[0], -sine[1], sine[1]], axis=0)
+
+    def condition_of(group_ids, labels):
+        group_hot = (group_ids[:, None] == jnp.arange(GROUPS, dtype=jnp.int32)[None, :]).astype(f32)
+        times = jax.nn.sigmoid(jnp.dot(group_hot, group_logits, precision=highest))
+        features = time_features(times, FREQ // 2).astype(bf16)
+        before = jnp.dot(features, time_weight, preferred_element_type=f32) + jnp.take(
+            class_table, labels, axis=0
+        ).astype(f32)
+        return features, before, jax.nn.silu(before).astype(bf16)
+
+    own_group = pick(group_ids, band_index)[None]
+    own_label = pick(labels, band_index)[None]
+    _, _, condition = condition_of(own_group, own_label)
+    modulation = jnp.dot(condition, ada_weight, preferred_element_type=f32) + ada_bias
+    modes = modulation.reshape(6, width)
+    shift_one, scale_one = modes[0:1], modes[1:2]
+    vectors = jnp.concatenate([modes[2:3], modes[4:5], modes[3:4], modes[5:6], modes[2:6]], axis=0)
+
+    scaling = HD ** (-0.5)
+    gains = jnp.stack([query_gain, key_gain])[:, :, None]
+    scaled_gains = gains * jnp.array([scaling * LOG2E, 1.0], f32)[:, None, None]
+    entry_one, heads, unit, factor = front(
+        x, scale_one, shift_one, qkv_weight, scaled_gains, cosine, sine
+    )
+    mixed, query = attend(heads)
+    patches = x.shape[0]
+    mixed_flat = mixed.reshape(width, patches)
+    attended, entry_two, fed_grad = middle_step(mixed_flat, proj_weight, x, c, vectors)
+    fed, entry_two_grad, grad_down, grad_gate, grad_up = mlp(
+        entry_two, fed_grad, gateup_weight, down_weight
+    )
+    result, middle_grad, mixed_grad, grad_proj, sums_two = turn_step(
+        fed, entry_two_grad, x, attended, c, mixed_flat, proj_weight, vectors
+    )
+    projected_grad, gain_terms = attend_back(
+        query, heads, mixed_grad.reshape(HEADS, HD, patches), mixed, unit, factor, gains,
+        cosine, sine,
+    )
+    grad_qkv, entry_one_grad = back_step(
+        projected_grad.reshape(3, width, patches), qkv_weight, entry_one
+    )
+    grad_latents, sums_one = last_step(entry_one_grad, x, middle_grad, scale_one)
+
+    everything = ("img", "band")
+    own_grad = jnp.concatenate(
+        [
+            sums_one[0],
+            sums_one[1],
+            sums_two[0],
+            sums_two[1],
+            sums_two[2],
+            sums_two[3],
+            jnp.sum(gain_terms, axis=2).reshape(-1),
+        ]
+    ).astype(bf16)
+    gathered = lax.all_gather(own_grad[None], everything, axis=0, tiled=True)
+    codes = lax.all_gather(
+        jnp.stack([group_ids, labels], axis=1), "img", axis=0, tiled=True
+    )
+    modulation_all = gathered[:, : 6 * width]
+    gain_sums = jnp.sum(gathered[:, 6 * width :].astype(f32), axis=0)
+    sum_query_gain, sum_key_gain = gain_sums[:HD], gain_sums[HD:]
+    features_all, before_all, condition_all = condition_of(codes[:, 0], codes[:, 1])
+    before_grad = lax.dot_general(
+        modulation_all, ada_weight, (((1,), (1,)), ((), ())), preferred_element_type=f32
+    ) * silu_slope(before_all)
+    ada_rows = width // lax.axis_size("img")
+    ada_cols = 6 * width // bands
+    time_rows = FREQ // lax.axis_size("img")
+    time_cols = width // bands
+    condition_part = lax.dynamic_slice_in_dim(condition_all, img_index * ada_rows, ada_rows, 1)
+    modulation_part = lax.dynamic_slice_in_dim(modulation_all, band_index * ada_cols, ada_cols, 1)
+    sum_ada = jnp.dot(condition_part.T, modulation_part, preferred_element_type=f32)
+    features_part = lax.dynamic_slice_in_dim(features_all, img_index * time_rows, time_rows, 1)
+    before_part = lax.dynamic_slice_in_dim(before_grad, band_index * time_cols, time_cols, 1)
+    sum_time = jnp.dot(features_part.astype(f32).T, before_part, precision=highest)
+    class_all = (codes[:, 1][:, None] == jnp.arange(NCLASS, dtype=jnp.int32)[None, :]).astype(f32)
+    sum_class = jnp.dot(class_all.T, before_grad, precision=highest)
+    sum_bias = jnp.sum(modulation_all.astype(f32), axis=0)
+
+    def scattered(grad, dim):
+        part = lax.psum_scatter(grad, "img", scatter_dimension=0, tiled=True)
+        return part
+
+    part_down = scattered(grad_down, 0)
+    part_gate = scattered(grad_gate, 0)
+    part_up = scattered(grad_up, 0)
+    part_gateup = jnp.concatenate([part_gate, part_up], axis=1)
+    part_proj = scattered(grad_proj, 0)
+    part_qkv = scattered(grad_qkv, 0)
+    sum_qkv, sum_proj, sum_gateup, sum_down = [
+        lax.psum_scatter(part, "band", scatter_dimension=1, tiled=True).astype(f32)
+        for part in (part_qkv, part_proj, part_gateup, part_down)
+    ]
+    return (
+        give_back(result),
+        give_back(grad_latents),
+        sum_time,
+        sum_class,
+        sum_ada,
+        sum_bias,
+        sum_qkv,
+        sum_query_gain,
+        sum_key_gain,
+        sum_proj,
+        sum_gateup,
+        sum_down,
+    )
+
+
+def per_device(latents, *others):
+    if latents.shape[0] == lax.axis_size("band"):
+        return per_device_whole(latents, *others)
+    return per_device_banded(latents, *others)
+
+
 def solution(mesh):
     return jax.shard_map(
         per_device,

time: 983 us -> 751 us (0.76)
  matrix products: 381 us -> 26.8 us
  Pallas kernels: 0 us -> 255 us
  other arithmetic: 75.2 us -> 31.4 us
  blocking collectives: 135 us -> 95.2 us
  local copies, waits for them, and re-layouts: 72.9 us -> 34.2 us
  waiting for transfers between devices: 297 us -> 279 us
    dot_general x26 -> x8, matrix products: 381 us -> 26.8 us  [the longest x1 10.3 us: per_device_whole(): lax.dot_general(modulation_all, ada_weight, (((1,), (1,)), ((), ())), pre...]
    pallas_call x0 -> x8, Pallas kernels: none -> 255 us  [the longest x1 89.5 us: mlp(): pl.pallas_call(mlp_kernel, grid=(tiles,), in_specs=[whole((patches, width...]
    all_gather x2 -> x0, waiting for transfers between devices: 71.1 us -> none  [the longest x1 57.1 us: per_device(): key_piece = lax.all_gather(key_bf, 'band', axis=1, tiled=True)]
    reduce_scatter x5 -> x4, waiting for transfers between devices: 107 us -> 157 us  [the longest x3 137 us: scattered(): part = lax.psum_scatter(grad, 'img', scatter_dimension=0, tiled=True)]
    reduce_sum x10 -> x3, other arithmetic: 39.2 us -> 1.92 us  [the longest x1 1.19 us: per_device_whole(): jnp.sum(gain_terms, axis=2).reshape(-1)]
    slice x9 -> x6, local copies, waits for them, and re-layouts: 36.5 us -> 1.35 us  [the longest x1 0.6 us: per_device_whole(): modes[5:6]]
    all_gather x6 -> x2, blocking collectives: 118 us -> 95.2 us  [the longest x1 72.7 us: per_device_whole(): gathered = lax.all_gather(own_grad[None], everything, axis=0, tiled=True)]
    convert_element_type x8 -> x6, other arithmetic: 19.7 us -> 5.08 us  [the longest x4 4.32 us: per_device_whole(): lax.psum_scatter(part, 'band', scatter_dimension=1, tiled=True).astype(f32)]
  transfers between devices with their start and end apart: 12 -> 14, of which waited for: 8 -> 7; matrix products, arithmetic and copies ran while one was open for 31% -> 11% of each run, Pallas kernels for 0% -> 18%
where the time goes in v1:
time: 751 us; the launch traced here: 746 us
  waiting for transfers between devices  279 us (37%)
  Pallas kernels  255 us (34%)
  blocking collectives  95.2 us (13%)
  local copies, waits for them, and re-layouts  34.2 us (5%)
  other arithmetic  31.4 us (4%)
  matrix products  26.8 us (4%)
  between operations  17.2 us (2%)
    reduce_scatter x3, waiting for transfers between devices, scattered(): part = lax.psum_scatter(grad, 'img', scatter_dimension=0, tiled=True)  137 us
    unnamed x14, waiting for transfers between devices  115 us
    pallas_call x1, Pallas kernels, mlp(): pl.pallas_call(mlp_kernel, grid=(tiles,), in_specs=[whole((patches, width...  89.5 us
    all_gather x1, blocking collectives, per_device_whole(): gathered = lax.all_gather(own_grad[None], everything, axis=0, tiled=True)  72.7 us
    pallas_call x1, Pallas kernels, attend_back(): pl.pallas_call(attend_back_kernel, grid=(HEADS,), in_specs=[single(HDP),...  58.9 us
    pallas_call x1, Pallas kernels, back_step(): pl.pallas_call(back_kernel, grid=(3,), in_specs=[pl.BlockSpec((None, widt...  26.6 us
    pallas_call x1, Pallas kernels, front(): pl.pallas_call(front_kernel, grid=(3,), in_specs=[whole((patches, width))...  23.6 us
    all_gather x1, blocking collectives, per_device_whole(): lax.all_gather(jnp.stack([group_ids, labels], axis=1), 'img', axis=0, til...  22.6 us
  transfers between devices with their start and end apart: 14, of which 7 were waited for; matrix products, arithmetic and copies ran while one was open for 11% of the time, Pallas kernels for 18%

profile of v1, /device:TPU:0, one launch (start us, length us, event | category | flops | bytes accessed | tf_op | source)
XLA Modules:
  0.0 746.5 jit_solution(10433495222504035946)
XLA Ops:
  7.3 3.0 dynamic-slice_bitcast_fusion.3
  10.3 3.0 collective-permute-start
  13.4 1.2 dynamic-slice_bitcast_fusion.1
  14.6 2.0 collective-permute-start.2
  19.7 1.2 fusion.23
  22.8 7.7 %convolution_reduce_fusion = f32[6912]{0:T(1024)S(1)} fusion(bf16[1152,1]{0,1:T(2,128)(2,1)S(1)} %reshape.334, bf16[1152,6912]{1,0:T(8,128)(2,1)} %param.29), kind=kOutput, calls=%fused_computation.17 | convolution fusion | flops 15925248 | bytes 15955200 | tf_op jit(solution)/shard_map/dot_general | solution.py:951
  32.9 7.5 %collective-permute-done.1 = s32[512,2]{0,1:T(2,128)S(1)} collective-permute-done((s32[512,2]{0,1:T(2,128)S(1)}, s32[512,2]{0,1:T(2,128)S(1)}, u32[]{:S(2)}, u32[]{:S(2)}) %collective-permute-start.1) | collective-permute-done | bytes 4128 | tf_op jit(solution)/shard_map/ppermute | solution.py:929
  42.7 2.9 pad_maximum_fusion.x_ref
  45.5 23.6 %front.1 = (bf16[1024,1152]{1,0:T(8,128)(2,1)}, bf16[3,16,80,1024]{3,2,1,0:T(8,128)(2,1)}, bf16[2,16,72,1024]{3,2,1,0:T(8,128)(2,1)}, f32[2,16,1,1024]{3,2,1,0:T(1,128)}) custom-call(bf16[1024,1152]{1,0:T(8,128)(2,1)} %pad_maximum_fusion.x_ref, f32[1,1152]{1,0:T(1,128)} %get-tuple-element.93.scale_ref, f32[1,1152]{1,0:T(1,128)} %get-tuple-element.92.shift_ref, ...), custom_call_target="tpu_custom_call" | custom-call | flops 8153726976 | bytes 24000000 | tf_op jit(solution)/shard_map/front/pallas_call | solution.py:439
  69.1 20.4 %attend.1 = (bf16[16,72,1024]{2,1,0:T(8,128)(2,1)}, bf16[16,80,1024]{2,1,0:T(8,128)(2,1)}) custom-call(bf16[3,16,80,1024]{3,2,1,0:T(8,128)(2,1)} %get-tuple-element.38.q.k.v.k_ref.v_ref, bf16[3,16,80,1024]{3,2,1,0:T(8,128)(2,1)} %get-tuple-element.38.q.k.v.k_ref.v_ref, bf16[3,16,80,1024]{3,2,1,0:T(8,128)(2,1)} %get-tuple-element.38.q.k.v.k_ref.v_ref), custom_call_target="tpu_custom_call" | custom-call | flops 10737418240 | bytes 14000000 | tf_op jit(solution)/shard_map/attend/pallas_call | solution.py:491
  89.6 2.8 pad_maximum_fusion.1.c_ref
  92.4 9.5 %middle.1 = (bf16[1024,1152]{1,0:T(8,128)(2,1)}, bf16[1024,1152]{1,0:T(8,128)(2,1)}, bf16[1024,1152]{1,0:T(8,128)(2,1)}) custom-call(bf16[1152,1024]{1,0:T(8,128)(2,1)} %bitcast.90, bf16[1152,1152]{1,0:T(8,128)(2,1)} %w_ref.6, bf16[1024,1152]{1,0:T(8,128)(2,1)} %pad_maximum_fusion.x_ref, bf16[1024,1152]{1,0:T(8,128)(2,1)} %pad_maximum_fusion.1.c_ref, ...), custom_call_target="tpu_custom_call" | custom-call | flops 2717908992 | bytes 17000000 | tf_op jit(solution)/shard_map/middle/pallas_call | solution.py:526
  101.9 89.5 %mlp.1 = (f32[1024,1152]{1,0:T(8,128)}, f32[1024,1152]{1,0:T(8,128)}, bf16[3072,1152]{1,0:T(8,128)(2,1)}, bf16[1152,3072]{1,0:T(8,128)(2,1)}, bf16[1152,3072]{1,0:T(8,128)(2,1)}) custom-call(bf16[1024,1152]{1,0:T(8,128)(2,1)} %get-tuple-element.40.entry_ref, bf16[1024,1152]{1,0:T(8,128)(2,1)} %get-tuple-element.41.fed_grad_ref, bf16[1152,6144]{1,0:T(8,128)(2,1)} %wu_ref.1, ...), custom_call_target="tpu_custom_call" | custom-call | flops 65229815808 | bytes 56000000 | tf_op jit(solution)/shard_map/mlp/pallas_call | solution.py:585
  191.4 18.8 %turn.1 = (bf16[1024,1152]{1,0:T(8,128)(2,1)}, f32[1024,1152]{1,0:T(8,128)}, bf16[1152,1024]{1,0:T(8,128)(2,1)}, bf16[1152,1152]{1,0:T(8,128)(2,1)}, f32[8,1152]{1,0:T(8,128)}) custom-call(f32[1024,1152]{1,0:T(8,128)} %get-tuple-element.42.fed_ref, f32[1024,1152]{1,0:T(8,128)} %get-tuple-element.43.entry_grad_ref, bf16[1024,1152]{1,0:T(8,128)(2,1)} %pad_maximum_fusion.x_ref, ...), custom_call_target="tpu_custom_call" | custom-call | flops 5435817984 | bytes 35000000 | tf_op jit(solution)/shard_map/turn/pallas_call | solution.py:670
  213.1 58.9 %attend_back.1 = (bf16[3,16,72,1024]{3,2,1,0:T(8,128)(2,1)}, f32[2,72,1024]{2,1,0:T(8,128)}) custom-call(bf16[16,80,1024]{2,1,0:T(8,128)(2,1)} %get-tuple-element.46.q_ref, bf16[3,16,80,1024]{3,2,1,0:T(8,128)(2,1)} %get-tuple-element.38.q.k.v.k_ref.v_ref, bf16[3,16,80,1024]{3,2,1,0:T(8,128)(2,1)} %get-tuple-element.38.q.k.v.k_ref.v_ref, ...), custom_call_target="tpu_custom_call" | custom-call | flops 26843545600 | bytes 32000000 | tf_op jit(solution)/shard_map/attend_back/pallas_call | solution.py:755
  272.0 26.6 %back.1 = (bf16[1152,3456]{1,0:T(8,128)(2,1)}, f32[1152,1024]{1,0:T(8,128)}) custom-call(bf16[3,1152,1024]{2,1,0:T(8,128)(2,1)} %bitcast.114, bf16[1152,3456]{1,0:T(8,128)(2,1)} %w_ref.7, bf16[1024,1152]{1,0:T(8,128)(2,1)} %get-tuple-element.51.entry_ref), custom_call_target="tpu_custom_call" | custom-call | flops 16307453952 | bytes 32000000 | tf_op jit(solution)/shard_map/back/pallas_call | solution.py:804
  299.4 22.6 %all-gather = s32[16,2,2]{2,1,0:T(2,128)S(1)} all-gather(s32[1,2,2]{2,1,0:T(2,128)S(1)} %bitcast.104), channel_id=1, replica_groups=mesh['img'=16,'band'=2] {'img'}, dimensions={0}, use_global_device_ids=true | all-gather | bytes 272 | tf_op jit(solution)/shard_map/all_gather | solution.py:994
  322.1 2.6 gather_fusion
  327.3 7.6 %last.1 = (bf16[1024,1152]{1,0:T(8,128)(2,1)}, f32[8,1152]{1,0:T(8,128)}) custom-call(f32[1152,1024]{1,0:T(8,128)} %get-tuple-element.52.entry_grad_ref, bf16[1024,1152]{1,0:T(8,128)(2,1)} %pad_maximum_fusion.x_ref, f32[1024,1152]{1,0:T(8,128)} %get-tuple-element.53.middle_grad_ref, f32[1,1152]{1,0:T(1,128)} %get-tuple-element.93.scale_ref), custom_call_target="tpu_custom_call" | custom-call | flops 23592960 | bytes 17000000 | tf_op jit(solution)/shard_map/last/pallas_call | solution.py:855
  336.5 1.2 reduce_sum.27
  337.9 72.7 %all-gather.1 = bf16[32,1,7056]{2,1,0:T(2,128)(2,1)S(1)} all-gather(bf16[1,1,7056]{2,1,0:T(2,128)(2,1)S(1)} %bitcast.99), channel_id=1, replica_groups=mesh['img'=16,'band'=2] {'img','band'}, dimensions={0}, use_global_device_ids=true | all-gather | bytes 465696 | tf_op jit(solution)/shard_map/all_gather | solution.py:993
  410.8 1.8 copy.55
  412.7 1.6 slice_bitcast_fusion.1
  414.3 0.9 collective-permute-start.3
  415.2 2.1 copy.57
  417.4 3.2 slice_bitcast_fusion
  420.6 1.1 collective-permute-start.4
  421.7 43.1 %reduce-scatter.20.cloned.1.call-done = bf16[72,3072]{1,0:T(8,128)(2,1)} async-done(((bf16[1152,3072]{1,0:T(8,128)(2,1)}), bf16[72,3072]{1,0:T(8,128)(2,1)}) %reduce-scatter.20.cloned.1.call-update) | async-done | bytes 442384 | tf_op jit(solution)/shard_map/reduce_scatter | solution.py:1019
  464.8 94.0 %reduce-scatter.22.cloned.1.call-done = bf16[72,3072]{1,0:T(8,128)(2,1)} async-done(((bf16[1152,3072]{1,0:T(8,128)(2,1)}), bf16[72,3072]{1,0:T(8,128)(2,1)}) %reduce-scatter.22.cloned.1.call-update) | async-done | bytes 442384 | tf_op jit(solution)/shard_map/reduce_scatter | solution.py:1019
  558.8 2.1 pad_maximum_fusion.4
  561.1 10.3 %convolution_multiply_fusion = f32[32,1152]{1,0:T(8,128)S(1)} fusion(bf16[1152,6912]{1,0:T(8,128)(2,1)} %param.29, f32[32,1152]{1,0:T(8,128)S(1)} %get-tuple-element.105, bf16[32,7056]{1,0:T(8,128)(2,1)S(1)} %bitcast.85), kind=kOutput, calls=%fused_computation.10 | convolution fusion | flops 509902848 | bytes 16662528 | tf_op jit(solution)/shard_map/dot_general | solution.py:1001
  572.3 2.1 fusion.5
  575.8 4.4 fusion.7
  580.2 1.0 copy-done.5
  581.2 1.6 pad_maximum_fusion.2
  582.8 80.4 %reduce-scatter.34.cloned.1.call-done = bf16[72,3456]{1,0:T(8,128)(2,1)} async-done(((bf16[1152,3456]{1,0:T(8,128)(2,1)}), bf16[72,3456]{1,0:T(8,128)(2,1)}) %reduce-scatter.34.cloned.1.call-update) | async-done | bytes 497680
  663.2 2.3 copy.53
  665.5 3.3 pad_maximum_fusion.3
  668.7 2.4 gather_fusion.1
  671.1 4.2 gather_fusion.2
  675.3 4.4 broadcast_select_fusion
  679.7 1.0 copy.56
  681.4 14.0 %reduce-scatter.32.cloned.1.call-done = bf16[576,192]{1,0:T(8,128)(2,1)} async-done(((bf16[1152,192]{1,0:T(8,128)(2,1)}), bf16[576,192]{1,0:T(8,128)(2,1)}) %reduce-scatter.32.cloned.1.call-update) | async-done | bytes 221200
  695.5 1.1 copy.58
  697.4 19.4 %reduce-scatter.24.cloned.1.call-done = bf16[72,3072]{1,0:T(8,128)(2,1)} async-done(((bf16[72,6144]{1,0:T(8,128)(2,1)}), bf16[72,3072]{1,0:T(8,128)(2,1)}) %reduce-scatter.24.cloned.1.call-update) | async-done | bytes 442384 | tf_op jit(solution)/shard_map/reduce_scatter | solution.py:1029
  716.8 2.0 convert_element_type.65
  718.8 18.8 %reduce-scatter.28.cloned.1.call-done = bf16[1728,72]{1,0:T(8,128)(2,1)} async-done(((bf16[3456,72]{1,0:T(8,128)(2,1)}), bf16[1728,72]{1,0:T(8,128)(2,1)}) %reduce-scatter.28.cloned.1.call-update) | async-done | bytes 248848
  737.7 1.2 copy.54
  (137 shorter events, 20.1 us)
Async XLA Ops:
  7.2 14.6 %copy-start = (bf16[256,1152]{1,0:T(8,128)(2,1)S(1)}, bf16[256,1152]{1,0:T(8,128)(2,1)}, u32[]{:S(2)}) copy-start(bf16[256,1152]{1,0:T(8,128)(2,1)} %param.27) | copy-start | bytes 1769476
  7.2 403.6 %reduce-scatter.36.cloned.1.call-start = ((), (), s32[]{:S(2)}) async-start(), calls=%async_computation.17 | async-start | bytes 2820096
  7.3 6.0 copy-start.11
  7.3 6.0 copy-start.12
  7.3 6.1 copy-start.3
  10.3 32.4 %collective-permute-start = (bf16[512,1152]{1,0:T(8,128)(2,1)}, bf16[512,1152]{1,0:T(8,128)(2,1)}, u32[]{:S(2)}, u32[]{:S(2)}) collective-permute-start(bf16[512,1152]{1,0:T(8,128)(2,1)} %get-tuple-element.81), channel_id=1, source_target_pairs={{0,1},{1,0},{2,3},{3,2},{4,5},{5,4},{6,7},{7,6},{8,9},{9,8},{10,11... | collective-permute-start | bytes 3538952 | tf_op jit(solution)/shard_map/ppermute | solution.py:909
  13.2 3.3 copy-start.21
  13.3 5.8 copy-start.19
  13.3 6.4 copy-start.23
  13.3 27.1 %collective-permute-start.1 = (s32[512,2]{0,1:T(2,128)S(1)}, s32[512,2]{0,1:T(2,128)S(1)}, u32[]{:S(2)}, u32[]{:S(2)}) collective-permute-start(s32[512,2]{0,1:T(2,128)S(1)} %pad_add_fusion), channel_id=1, source_target_pairs={{0,1},{1,0},{2,3},{3,2},{4,5},{5,4},{6,7},{7,6},{8,9},{9,8},{10,11... | collective-permute-start | bytes 12296 | tf_op jit(solution)/shard_map/ppermute | solution.py:929
  14.6 75.0 %collective-permute-start.2 = (bf16[512,1152]{1,0:T(8,128)(2,1)}, bf16[512,1152]{1,0:T(8,128)(2,1)}, u32[]{:S(2)}, u32[]{:S(2)}) collective-permute-start(bf16[512,1152]{1,0:T(8,128)(2,1)} %get-tuple-element.79), channel_id=1, source_target_pairs={{0,1},{1,0},{2,3},{3,2},{4,5},{5,4},{6,7},{7,6},{8,9},{9,8},{10,11... | collective-permute-start | bytes 3538952 | tf_op jit(solution)/shard_map/ppermute | solution.py:909
  22.8 7.8 %copy-start.10 = (f32[6912]{0:T(1024)S(1)}, f32[6912]{0:T(1024)}, u32[]{:S(2)}) copy-start(f32[6912]{0:T(1024)} %param.30) | copy-start | bytes 82948
  22.8 8.4 %copy-start.16 = (f32[72]{0:T(128)S(1)}, f32[72]{0:T(128)}, u32[]{:S(2)}) copy-start(f32[72]{0:T(128)} %param.32) | copy-start | bytes 868
  22.8 8.5 %copy-start.15 = (f32[72]{0:T(128)S(1)}, f32[72]{0:T(128)}, u32[]{:S(2)}) copy-start(f32[72]{0:T(128)} %param.33) | copy-start | bytes 868
  22.8 8.6 %copy-start.18 = (f32[2]{0:T(128)S(1)}, f32[2]{0:T(128)}, u32[]{:S(2)}) copy-start(f32[2]{0:T(128)} %constant.121.clone) | copy-start | bytes 28
  210.2 205.0 %reduce-scatter.26.cloned.1.call-start = ((), (), s32[]{:S(2)}) async-start(), calls=%async_computation.12 | async-start | bytes 7520256 | tf_op jit(solution)/shard_map/reduce_scatter | solution.py:1019
  211.0 253.9 %reduce-scatter.20.cloned.1.call-start = ((), (), s32[]{:S(2)}) async-start(), calls=%async_computation.9 | async-start | bytes 7520256 | tf_op jit(solution)/shard_map/reduce_scatter | solution.py:1019
  211.7 347.2 %reduce-scatter.22.cloned.1.call-start = ((), (), s32[]{:S(2)}) async-start(), calls=%async_computation.10 | async-start | bytes 7520256 | tf_op jit(solution)/shard_map/reduce_scatter | solution.py:1019
  212.3 450.9 %reduce-scatter.34.cloned.1.call-start = ((), (), s32[]{:S(2)}) async-start(), calls=%async_computation.16 | async-start | bytes 8460288
  298.6 0.7 copy-start.20
  298.6 0.7 copy-start.22
  298.6 27.4 %copy-start.24 = (f32[8]{0:T(128)S(1)}, f32[8]{0:T(128)}, u32[]{:S(2)}) copy-start(f32[8]{0:T(128)} %param.24) | copy-start | bytes 100
  298.7 381.0 %reduce-scatter.30.cloned.1.call-start = ((), (), s32[]{:S(2)}) async-start(), calls=%async_computation.14 | async-start | bytes 442368
  322.1 5.2 copy-start.13
  326.4 0.9 copy-start.6
  326.4 0.9 copy-start.8
  334.8 77.8 %copy-start.4 = (bf16[1024,1152]{1,0:T(8,128)(2,1)S(1)}, bf16[1024,1152]{1,0:T(8,128)(2,1)}, u32[]{:S(2)}) copy-start(bf16[1024,1152]{1,0:T(8,128)(2,1)} %get-tuple-element.45) | copy-start | bytes 7077892
  412.6 282.8 %reduce-scatter.32.cloned.1.call-start = ((), (), s32[]{:S(2)}) async-start(), calls=%async_computation.15 | async-start | bytes 884736
  414.3 165.9 %collective-permute-start.3 = (bf16[512,1152]{1,0:T(8,128)(2,1)}, bf16[512,1152]{1,0:T(8,128)(2,1)S(1)}, u32[]{:S(2)}, u32[]{:S(2)}) collective-permute-start(bf16[512,1152]{1,0:T(8,128)(2,1)} %get-tuple-element.77), channel_id=1, source_target_pairs={{0,1},{1,0},{2,3},{3,2},{4,5},{5,4},{6,7},{7,6},{8,9},{9,8},{10,11... | collective-permute-start | bytes 3538952 | tf_op jit(solution)/shard_map/ppermute | solution.py:917
  417.3 299.5 %reduce-scatter.24.cloned.1.call-start = ((), (), s32[]{:S(2)}) async-start(), calls=%async_computation.11 | async-start | bytes 1327104 | tf_op jit(solution)/shard_map/reduce_scatter | solution.py:1029
  420.6 244.9 %collective-permute-start.4 = (bf16[512,1152]{1,0:T(8,128)(2,1)}, bf16[512,1152]{1,0:T(8,128)(2,1)}, u32[]{:S(2)}, u32[]{:S(2)}) collective-permute-start(bf16[512,1152]{1,0:T(8,128)(2,1)} %get-tuple-element.75), channel_id=1, source_target_pairs={{0,1},{1,0},{2,3},{3,2},{4,5},{5,4},{6,7},{7,6},{8,9},{9,8},{10,11... | collective-permute-start | bytes 3538952 | tf_op jit(solution)/shard_map/ppermute | solution.py:917
  561.0 176.7 %reduce-scatter.28.cloned.1.call-start = ((), (), s32[]{:S(2)}) async-start(), calls=%async_computation.13 | async-start | bytes 1327104
  561.0 10.3 %copy-start.7 = (bf16[32,128]{1,0:T(8,128)(2,1)S(1)}, bf16[32,128]{1,0:T(8,128)(2,1)}, u32[]{:S(2)}) copy-start(bf16[32,128]{1,0:T(8,128)(2,1)} %copy-done.6) | copy-start | bytes 24580
  561.0 10.3 %copy-start.9 = (bf16[32,128]{1,0:T(8,128)(2,1)S(1)}, bf16[32,128]{1,0:T(8,128)(2,1)}, u32[]{:S(2)}) copy-start(bf16[32,128]{1,0:T(8,128)(2,1)} %copy-done.8) | copy-start | bytes 24580
  571.3 4.4 copy-start.14
  575.8 5.4 copy-start.2
  580.2 1.0 copy-start.5
  671.1 4.2 copy-start.1
  671.1 4.2 copy-start.17
Sparse Core Ops, SparseCore 0:
  210.3 65.7 reduce-scatter.35
  280.7 90.6 reduce-scatter.25
  375.3 89.4 reduce-scatter.19
  469.2 89.5 reduce-scatter.21
  562.8 100.3 reduce-scatter.33
  665.9 11.8 reduce-scatter.29
  680.2 15.2 reduce-scatter.31
  698.3 18.4 reduce-scatter.23
  719.1 18.5 reduce-scatter.27

commit v2 on v1

--- a/solution.py
+++ b/solution.py
@@ -1,3 +1,4 @@
+import functools
 import math
 
 import jax
@@ -395,6 +396,125 @@
     return high, values - high
 
 
+MESH_ID = pl.DeviceIdType.MESH
+
+
+def pair_axes():
+    bits = lax.axis_size("img").bit_length() - 1
+    return ["y"] + [f"b{bit}" for bit in reversed(range(bits))]
+
+
+def own_places():
+    img = lax.axis_index("img")
+    places = {"y": lax.axis_index("band")}
+    for bit in range(lax.axis_size("img").bit_length() - 1):
+        places[f"b{bit}"] = lax.rem(lax.div(img, 2**bit), 2)
+    return places
+
+
+def partner_id(axis, places):
+    if axis == "y":
+        return {"band": 1 - places["y"]}
+    bit = int(axis[1:])
+    return {"img": lax.axis_index("img") + (1 - 2 * places[axis]) * 2**bit}
+
+
+def greet(places):
+    barrier = pltpu.get_barrier_semaphore()
+    for axis in places:
+        pl.semaphore_signal(
+            barrier, inc=1, device_id=partner_id(axis, places), device_id_type=MESH_ID
+        )
+    pl.semaphore_wait(barrier, len(places))
+
+
+class Halving:
+    def __init__(self, places, dims, order, held, arrived, send, receive, lead=(), tail=()):
+        self.places, self.dims, self.order = places, list(dims), list(order)
+        self.held, self.arrived, self.send, self.receive = held, arrived, send, receive
+        self.lead, self.tail = tuple(lead), tuple(tail)
+
+    def source_index(self, mine):
+        first = self.order[0]
+        place = self.places[first] if mine else 1 - self.places[first]
+        return [place if name == first else slice(None) for name in self.dims]
+
+    def held_index(self, step, mine):
+        picked = []
+        for name in self.dims:
+            place = self.order.index(name)
+            if place == 0:
+                continue
+            if place < step:
+                picked.append(self.places[name])
+            elif place == step:
+                picked.append(self.places[name] if mine else 1 - self.places[name])
+            else:
+                picked.append(slice(None))
+        return picked
+
+    def copy(self, step, source=None):
+        if step == 0:
+            block = source.at[tuple(self.source_index(False)) + self.tail]
+        else:
+            block = self.held.at[self.lead + tuple(self.held_index(step, False))]
+        arrived = self.arrived[step]
+        return pltpu.make_async_remote_copy(
+            src_ref=block,
+            dst_ref=arrived.at[self.lead] if self.lead else arrived,
+            send_sem=self.send.at[self.lead + (step,)],
+            recv_sem=self.receive.at[self.lead + (step,)],
+            device_id=partner_id(self.order[step], self.places),
+            device_id_type=MESH_ID,
+        )
+
+    def own_half(self, source, semaphore):
+        return pltpu.make_async_copy(
+            source.at[tuple(self.source_index(True)) + self.tail],
+            self.held.at[self.lead] if self.lead else self.held,
+            semaphore,
+        )
+
+    def add(self, step, source=None, put=None):
+        picked = self.held_index(step, True)
+        free = [place for place, entry in enumerate(picked) if isinstance(entry, slice)]
+        if not free:
+            total = self.held[self.lead + tuple(picked)].astype(f32)
+            put(total + self.arrived[step][self.lead + (...,)].astype(f32))
+            return
+
+        def one(number, _):
+            digits = [lax.rem(lax.div(number, 2**place), 2) for place in range(len(free))]
+            target = list(picked)
+            for place, digit in zip(free, digits):
+                target[place] = digit
+            if source is not None:
+                rest = iter(digits)
+                spot = [next(rest) if isinstance(e, slice) else e for e in self.source_index(True)]
+                old = source[tuple(spot)]
+            else:
+                old = self.held[self.lead + tuple(target)]
+            self.held[self.lead + tuple(target)] = (
+                old + self.arrived[step][self.lead + tuple(digits)]
+            )
+            return 0
+
+        lax.fori_loop(0, 2 ** len(free), one, 0)
+
+
+def halving_scratch(dims, tail, lead=()):
+    left = len(dims) - 1
+    shapes = [lead + (2,) * left + tail]
+    shapes += [lead + (2,) * (left - step) + tail for step in range(len(dims))]
+    semaphores = pltpu.SemaphoreType.DMA(lead + (len(dims),))
+    return [pltpu.VMEM(shape, bf16) for shape in shapes] + [semaphores, semaphores]
+
+
+def order_of(dims, *first):
+    rest = [name for name in reversed(dims) if name not in first]
+    return list(first) + rest
+
+
 def front_kernel(
     x_ref, scale_ref, shift_ref, w_ref, gains_ref, cos_ref, sin_ref,
     entry_ref, heads_ref, unit_ref, factor_ref,
@@ -541,16 +661,53 @@
     )(mixed, proj_weight, x, c, vectors)
 
 
+MLP_TILE = 512
+MLP_SUB = 256
+HOSTED = 4
+
+
 def mlp_kernel(
-    entry_ref, fed_grad_ref, wg_ref, wu_ref, wd_ref,
-    fed_ref, entry_grad_ref, down_ref, gate_out_ref, up_out_ref,
-    hidden_ref, gate_grad_ref, up_grad_ref,
+    dims, entry_ref, fed_grad_ref, wg_ref, wu_ref, wd_ref,
+    fed_ref, entry_grad_ref, down_ref, done_ref, left_ref,
+    hidden_ref, gate_grad_ref, up_grad_ref, source_ref, left_sem, held, *rest,
 ):
+    *arrived, send, receive = rest
     tile = pl.program_id(0)
+    places = own_places()
+    orders = [order_of(dims, "b0", "y", "b1"), order_of(dims, "b0", "b1", "y")]
+    steps = len(dims)
+
+    def streams(number):
+        slot = lax.rem(number, 2)
+        return [
+            Halving(places, dims, orders[sub], held, arrived, send, receive, (slot, sub))
+            for sub in range(2)
+        ]
+
+    def advance(number, step):
+        @pl.when((number >= 0) & (number < HOSTED))
+        def _():
+            for sub, stream in enumerate(streams(number)):
+                source = source_ref.at[sub]
+                stream.copy(step, source).wait()
+
+                def put(values):
+                    done_ref[number, sub] = values.astype(bf16)
+
+                stream.add(step, source if step == 0 else None, put)
+                if step + 1 < steps:
+                    stream.copy(step + 1).start()
+
+    @pl.when(tile == 0)
+    def _():
+        greet(places)
+
     entry = entry_ref[...]
     fed_grad = fed_grad_ref[...]
     gate = dot(entry, wg_ref[...], 1, 0)
     up = dot(entry, wu_ref[...], 1, 0)
+    advance(tile - 2, 3)
+    advance(tile - 1, 0)
     sigma = jax.nn.sigmoid(gate)
     silu = gate * sigma
     hidden_ref[...] = (silu * up).astype(bf16)
@@ -572,18 +729,58 @@
         fed_ref[...] += fed
         entry_grad_ref[...] += entry_grad
 
-    down_ref[...] = dot(hidden_ref[...], fed_grad, 0, 0).astype(bf16)
-    gate_out_ref[...] = dot(entry, gate_grad_ref[...], 0, 0).astype(bf16)
-    up_out_ref[...] = dot(entry, up_grad_ref[...], 0, 0).astype(bf16)
+    for step in range(4, steps):
+        advance(tile - 2, step)
+    advance(tile - 1, 1)
+    down = dot(hidden_ref[...], fed_grad, 0, 0)
+    column_half = down.shape[1] // 2
+    down_ref[0] = down[:, :column_half].astype(bf16)
+    down_ref[1] = down[:, column_half:].astype(bf16)
+    grads = [dot(entry, ref[...], 0, 0) for ref in (gate_grad_ref, up_grad_ref)]
+    advance(tile - 1, 2)
+
+    def leave(number):
+        return pltpu.make_async_copy(
+            source_ref, left_ref.at[jnp.maximum(number - HOSTED, 0)], left_sem
+        )
+
+    @pl.when(tile > HOSTED)
+    def _():
+        leave(tile - 1).wait()
+
+    blocks = 2 ** (steps - 1)
+    rows = grads[0].shape[0] // blocks
+    for half, grad in enumerate(grads):
+        for block in range(blocks):
+            spot = tuple(block // 2**bit % 2 for bit in reversed(range(steps - 1)))
+            part = grad[block * rows : (block + 1) * rows, :].astype(bf16)
+            for sub in range(2):
+                source_ref[(sub, half) + spot] = part[:, sub * MLP_SUB : (sub + 1) * MLP_SUB]
+
+    @pl.when(tile < HOSTED)
+    def _():
+        for sub, stream in enumerate(streams(tile)):
+            stream.copy(0, source_ref.at[sub]).start()
+
+    @pl.when(tile >= HOSTED)
+    def _():
+        leave(tile).start()
+
+    @pl.when(tile == pl.num_programs(0) - 1)
+    def _():
+        leave(tile).wait()
 
 
 def mlp(entry, fed_grad, gateup_weight, down_weight):
     patches, width = entry.shape
     inner = down_weight.shape[0]
-    tile = 512
+    tile = MLP_TILE
     tiles = inner // tile
+    dims = pair_axes()
+    rows = width // lax.axis_size("img")
+    tail = (rows, MLP_SUB)
     return pl.pallas_call(
-        mlp_kernel,
+        functools.partial(mlp_kernel, dims),
         grid=(tiles,),
         in_specs=[
             whole((patches, width)),
@@ -593,21 +790,23 @@
             pl.BlockSpec((tile, width), lambda t: (t, 0)),
         ],
         out_specs=[
-            pl.BlockSpec((patches, width), lambda t: (0, 0)),
-            pl.BlockSpec((patches, width), lambda t: (0, 0)),
-            pl.BlockSpec((tile, width), lambda t: (t, 0)),
-            pl.BlockSpec((width, tile), lambda t: (0, t)),
-            pl.BlockSpec((width, tile), lambda t: (0, t)),
+            whole((patches, width)),
+            whole((patches, width)),
+            pl.BlockSpec((2, tile, width // 2), lambda t: (0, t, 0)),
+            whole((HOSTED, 2) + tail),
+            pl.BlockSpec(memory_space=pl.ANY),
         ],
         out_shape=[
             jax.ShapeDtypeStruct((patches, width), f32),
             jax.ShapeDtypeStruct((patches, width), f32),
-            jax.ShapeDtypeStruct((inner, width), bf16),
-            jax.ShapeDtypeStruct((width, inner), bf16),
-            jax.ShapeDtypeStruct((width, inner), bf16),
-        ],
-        scratch_shapes=[pltpu.VMEM((patches, tile), bf16)] * 3,
-        compiler_params=params_of(),
+            jax.ShapeDtypeStruct((2, inner, width // 2), bf16),
+            jax.ShapeDtypeStruct((HOSTED, 2) + tail, bf16),
+            jax.ShapeDtypeStruct((tiles - HOSTED, 2) + (2,) * len(dims) + tail, bf16),
+        ],
+        scratch_shapes=[pltpu.VMEM((patches, tile), bf16)] * 3
+        + [pltpu.VMEM((2,) + (2,) * len(dims) + tail, bf16), pltpu.SemaphoreType.DMA]
+        + halving_scratch(dims, tail, (2, 2)),
+        compiler_params=params_of(collective_id=0, has_side_effects=True),
         cost_estimate=cost(18 * patches * width * inner, 56e6),
         name="mlp",
     )(entry, fed_grad, gateup_weight, gateup_weight, down_weight)
@@ -659,7 +858,9 @@
 
     @pl.when(step == pl.num_programs(0) - 1)
     def _():
-        grad_proj_ref[...] = total_ref[...].astype(bf16)
+        half = total_ref.shape[1] // 2
+        grad_proj_ref[0] = total_ref[:, :half].astype(bf16)
+        grad_proj_ref[1] = total_ref[:, half:].astype(bf16)
 
 
 def turn_step(fed, entry_grad, x, attended, c, mixed, proj_weight, vectors):
@@ -675,14 +876,14 @@
             block,
             block,
             across,
-            pl.BlockSpec((width, width), lambda t: (0, 0)),
+            pl.BlockSpec((2, width, width // 2), lambda t: (0, 0, 0)),
             pl.BlockSpec((8, width), lambda t: (0, 0)),
         ],
         out_shape=[
             jax.ShapeDtypeStruct((patches, width), bf16),
             jax.ShapeDtypeStruct((patches, width), f32),
             jax.ShapeDtypeStruct((width, patches), bf16),
-            jax.ShapeDtypeStruct((width, width), bf16),
+            jax.ShapeDtypeStruct((2, width, width // 2), bf16),
             jax.ShapeDtypeStruct((8, width), f32),
         ],
         scratch_shapes=[pltpu.VMEM((width, width), f32)],
@@ -692,11 +893,77 @@
     )(fed, entry_grad, x, attended, c, mixed, proj_weight, vectors)
 
 
+def back_plan(dims):
+    first, second = pl.ds(0, 96), pl.ds(96, 96)
+    return [
+        ("down", (0,), (first,), order_of(dims, "b0", "b1", "b2", "y"), (0, 2, 8, 11, 13, 15)),
+        ("down", (1,), (second,), order_of(dims, "b0", "b2", "b1", "y"), (0, 2, 8, 11, 13, 15)),
+        ("left", (0, 0), (), order_of(dims, "b0", "y", "b1"), (0, 3, 7, 10, 12, 14)),
+        ("left", (1, 0), (), order_of(dims, "b0", "y", "b1"), (0, 3, 7, 10, 12, 14)),
+        ("left", (0, 1), (), order_of(dims, "b0", "y", "b2"), (0, 3, 10, 12, 14, 15)),
+        ("left", (1, 1), (), order_of(dims, "b0", "y", "b2"), (0, 3, 10, 12, 14, 15)),
+        ("proj", (), (), order_of(dims, "b0", "y", "b1"), (1, 4, 12, 14, 15, 15)),
+    ]
+
+
 def attend_back_kernel(
-    q_ref, k_ref, v_ref, mg_ref, mixed_ref, unit_ref, factor_ref, gains_ref, cos_ref, sin_ref,
-    out_ref, gain_out_ref, mg_ext_ref, acc_ref,
+    dims, q_ref, k_ref, v_ref, mg_ref, mixed_ref, unit_ref, factor_ref, gains_ref, cos_ref,
+    sin_ref, down_ref, left_ref, proj_ref,
+    out_ref, gain_out_ref, down_out_ref, left_out_ref, proj_out_ref,
+    mg_ext_ref, acc_ref, own_sem, *buffers,
 ):
     head = pl.program_id(0)
+    places = own_places()
+    steps = len(dims)
+    sizes = steps + 3
+    groups = {
+        name: buffers[place * sizes : (place + 1) * sizes]
+        for place, name in enumerate(("down", "left", "proj"))
+    }
+    sources = {"down": down_ref, "left": left_ref, "proj": proj_ref}
+    outs = {"down": down_out_ref, "left": left_out_ref, "proj": proj_out_ref}
+
+    @pl.when(head == 0)
+    def _():
+        greet(places)
+
+    def streams():
+        for number, (name, lead, rows, order, heads) in enumerate(back_plan(dims)):
+            held, *arrived, send, receive = groups[name]
+            source, tail = sources[name], ()
+            if name == "down":
+                tail = rows + (slice(None),)
+            if name == "left":
+                source = source.at[lead]
+            stream = Halving(places, dims, order, held, arrived, send, receive, lead, tail)
+            yield number, name, lead, stream, source, heads
+
+    def advance(now, last=False):
+        for number, name, lead, stream, source, heads in streams():
+            for step in range(-1, steps):
+                if (heads[step + 1] == now) and (last == (step == steps - 1 and now == HEADS - 1)):
+                    due(now, number, name, lead, stream, source, step)
+
+    def due(now, number, name, lead, stream, source, step):
+        @pl.when(head == now)
+        def _():
+            if step < 0:
+                stream.copy(0, source).start()
+                stream.own_half(source, own_sem.at[number]).start()
+                return
+            stream.copy(step, source).wait()
+            if step == 0:
+                stream.own_half(source, own_sem.at[number]).wait()
+
+            def put(values):
+                outs[name][lead + (...,)] = values.astype(bf16)
+
+            stream.add(step, None, put)
+            if step + 1 < steps:
+                stream.copy(step + 1).start()
+
+    for now in range(HEADS):
+        advance(now)
     patches = q_ref.shape[-1]
     step = patches // 2
     scaling = HD ** (-0.5)
@@ -743,17 +1010,29 @@
         raw = factor_ref[member] * (inner - unit * jnp.mean(inner * unit, axis=0, keepdims=True))
         out_ref[member] = raw.astype(bf16)
     out_ref[2] = acc_ref[2, :HD, :].astype(bf16)
-
-
-def attend_back(query, heads, mixed_grad, mixed, unit, factor, gains, cosine, sine):
+    advance(HEADS - 1, True)
+
+
+def attend_back(
+    query, heads, mixed_grad, mixed, unit, factor, gains, cosine, sine, down, left, proj
+):
     patches = query.shape[-1]
+    dims = pair_axes()
+    split = (2,) * (len(dims) - 1)
+    devices = lax.axis_size("img")
+    down = down.reshape((2,) + split + (down.shape[1] // devices, down.shape[2]))
+    proj = proj.reshape((2,) + split + (proj.shape[1] // devices, proj.shape[2]))
+    down_tail = (down.shape[-2] // 2, down.shape[-1])
+    left_tail, proj_tail = left.shape[-2:], proj.shape[-2:]
+    left_lead = left.shape[:2]
+    anywhere = pl.BlockSpec(memory_space=pl.ANY)
     section = lambda member: pl.BlockSpec(
         (None, None, HDP, patches), lambda h: (member, h, 0, 0)
     )
     single = lambda rows: pl.BlockSpec((None, rows, patches), lambda h: (h, 0, 0))
     pair = lambda rows: pl.BlockSpec((2, None, rows, patches), lambda h: (0, h, 0, 0))
     return pl.pallas_call(
-        attend_back_kernel,
+        functools.partial(attend_back_kernel, dims),
         grid=(HEADS,),
         in_specs=[
             single(HDP),
@@ -766,23 +1045,38 @@
             whole((2, HD, 1)),
             whole((HD, patches)),
             whole((HD, patches)),
+            anywhere,
+            anywhere,
+            anywhere,
         ],
         out_specs=[
             pl.BlockSpec((3, None, HD, patches), lambda h: (0, h, 0, 0)),
             pl.BlockSpec((2, HD, patches), lambda h: (0, 0, 0)),
+            whole((2,) + down_tail),
+            whole(left_lead + left_tail),
+            whole(proj_tail),
         ],
         out_shape=[
             jax.ShapeDtypeStruct((3, HEADS, HD, patches), bf16),
             jax.ShapeDtypeStruct((2, HD, patches), f32),
+            jax.ShapeDtypeStruct((2,) + down_tail, bf16),
+            jax.ShapeDtypeStruct(left_lead + left_tail, bf16),
+            jax.ShapeDtypeStruct(proj_tail, bf16),
         ],
         scratch_shapes=[
             pltpu.VMEM((HDP, patches), bf16),
             pltpu.VMEM((3, HDP, patches), f32),
-        ],
-        compiler_params=params_of(),
+            pltpu.SemaphoreType.DMA((len(back_plan(dims)),)),
+        ]
+        + halving_scratch(dims, down_tail, (2,))
+        + halving_scratch(dims, left_tail, left_lead)
+        + halving_scratch(dims, proj_tail),
+        compiler_params=params_of(collective_id=1, has_side_effects=True),
         cost_estimate=cost(20 * HEADS * patches * patches * HDP, 32e6, HEADS * patches**2),
         name="attend_back",
-    )(query, heads, heads, mixed_grad, mixed, unit, factor, gains, cosine, sine)
+    )(
+        query, heads, heads, mixed_grad, mixed, unit, factor, gains, cosine, sine, down, left, proj
+    )
 
 
 def back_kernel(pg_ref, w_ref, entry_ref, grad_ref, entry_grad_ref):
@@ -963,15 +1257,15 @@
     patches = x.shape[0]
     mixed_flat = mixed.reshape(width, patches)
     attended, entry_two, fed_grad = middle_step(mixed_flat, proj_weight, x, c, vectors)
-    fed, entry_two_grad, grad_down, grad_gate, grad_up = mlp(
+    fed, entry_two_grad, grad_down, gateup_done, gateup_left = mlp(
         entry_two, fed_grad, gateup_weight, down_weight
     )
     result, middle_grad, mixed_grad, grad_proj, sums_two = turn_step(
         fed, entry_two_grad, x, attended, c, mixed_flat, proj_weight, vectors
     )
-    projected_grad, gain_terms = attend_back(
+    projected_grad, gain_terms, sum_down, gateup_rest, sum_proj = attend_back(
         query, heads, mixed_grad.reshape(HEADS, HD, patches), mixed, unit, factor, gains,
-        cosine, sine,
+        cosine, sine, grad_down, gateup_left, grad_proj,
     )
     grad_qkv, entry_one_grad = back_step(
         projected_grad.reshape(3, width, patches), qkv_weight, entry_one
@@ -1015,20 +1309,12 @@
     sum_class = jnp.dot(class_all.T, before_grad, precision=highest)
     sum_bias = jnp.sum(modulation_all.astype(f32), axis=0)
 
-    def scattered(grad, dim):
-        part = lax.psum_scatter(grad, "img", scatter_dimension=0, tiled=True)
-        return part
-
-    part_down = scattered(grad_down, 0)
-    part_gate = scattered(grad_gate, 0)
-    part_up = scattered(grad_up, 0)
-    part_gateup = jnp.concatenate([part_gate, part_up], axis=1)
-    part_proj = scattered(grad_proj, 0)
-    part_qkv = scattered(grad_qkv, 0)
-    sum_qkv, sum_proj, sum_gateup, sum_down = [
-        lax.psum_scatter(part, "band", scatter_dimension=1, tiled=True).astype(f32)
-        for part in (part_qkv, part_proj, part_gateup, part_down)
-    ]
+    sum_down = sum_down.reshape(-1, sum_down.shape[-1]).astype(f32)
+    sum_proj = sum_proj.astype(f32)
+    gateup = jnp.concatenate([gateup_done, gateup_rest], axis=0)
+    sum_gateup = jnp.transpose(gateup, (2, 0, 1, 3)).reshape(gateup.shape[2], -1).astype(f32)
+    part_qkv = lax.psum_scatter(grad_qkv, "img", scatter_dimension=0, tiled=True)
+    sum_qkv = lax.psum_scatter(part_qkv, "band", scatter_dimension=1, tiled=True).astype(f32)
     return (
         give_back(result),
         give_back(grad_latents),
@@ -1046,7 +1332,8 @@
 
 
 def per_device(latents, *others):
-    if latents.shape[0] == lax.axis_size("band"):
+    devices = lax.axis_size("img")
+    if latents.shape[0] == lax.axis_size("band") == 2 and devices >= 8 and devices & (devices - 1) == 0:
         return per_device_whole(latents, *others)
     return per_device_banded(latents, *others)
 

time: 751 us -> 556 us (0.74)
  waiting for transfers between devices: 279 us -> 7.35 us
  Pallas kernels: 255 us -> 307 us
  blocking collectives: 95.2 us -> 134 us
  other arithmetic: 31.4 us -> 23.5 us
    reduce_scatter x4 -> x0, waiting for transfers between devices: 157 us -> none  [the longest x3 137 us: scattered(): part = lax.psum_scatter(grad, 'img', scatter_dimension=0, tiled=True)]
    unnamed x14 -> x4, waiting for transfers between devices: 115 us -> 0.62 us
    pallas_call x2, Pallas kernels: 148 us -> 201 us  [the longest x1 113 us: mlp(): pl.pallas_call(functools.partial(mlp_kernel, dims), grid=(tiles,), in_spe...]
    all_gather x1, blocking collectives: 72.7 us -> 115 us  [per_device_whole(): gathered = lax.all_gather(own_grad[None], everything, axis=0, tiled=True)]
  transfers between devices with their start and end apart: 14 -> 7, of which waited for: 7 -> 2; matrix products, arithmetic and copies ran while one was open for 11% -> 13% of each run, Pallas kernels for 18% -> 9%
where the time goes in v2:
time: 556 us; the launch traced here: 551 us
  Pallas kernels  307 us (55%)
  blocking collectives  134 us (24%)
  local copies, waits for them, and re-layouts  28.7 us (5%)
  matrix products  25.4 us (5%)
  other arithmetic  23.5 us (4%)
  between operations  17.5 us (3%)
  waiting for transfers between devices  7.35 us (1%)
  starting transfers between devices  7.14 us (1%)
    all_gather x1, blocking collectives, per_device_whole(): gathered = lax.all_gather(own_grad[None], everything, axis=0, tiled=True)  115 us
    pallas_call x1, Pallas kernels, mlp(): pl.pallas_call(functools.partial(mlp_kernel, dims), grid=(tiles,), in_spe...  113 us
    pallas_call x1, Pallas kernels, attend_back(): pl.pallas_call(functools.partial(attend_back_kernel, dims), grid=(HEADS,)...  87.5 us
    pallas_call x1, Pallas kernels, back_step(): pl.pallas_call(back_kernel, grid=(3,), in_specs=[pl.BlockSpec((None, widt...  26.8 us
    pallas_call x1, Pallas kernels, front(): pl.pallas_call(front_kernel, grid=(3,), in_specs=[whole((patches, width))...  23.6 us
    pallas_call x1, Pallas kernels, attend(): pl.pallas_call(lambda q, k, v, mixed, qext: attend_kernel(q, k, v, mixed,...  20.4 us
    pallas_call x1, Pallas kernels, turn_step(): pl.pallas_call(turn_kernel, grid=(patches // rows,), in_specs=[block] * 5...  19 us
    all_gather x1, blocking collectives, per_device_whole(): lax.all_gather(jnp.stack([group_ids, labels], axis=1), 'img', axis=0, til...  18.6 us
  transfers between devices with their start and end apart: 7, of which 2 were waited for; matrix products, arithmetic and copies ran while one was open for 13% of the time, Pallas kernels for 9%

profile of v2, /device:TPU:0, one launch (start us, length us, event | category | flops | bytes accessed | tf_op | source)
XLA Modules:
  0.0 550.9 jit_solution(14606223816872734523)
XLA Ops:
  7.3 3.0 dynamic-slice_bitcast_fusion.3
  10.3 3.0 collective-permute-start
  13.4 1.2 dynamic-slice_bitcast_fusion.1
  14.6 2.0 collective-permute-start.2
  17.2 1.2 fusion.23
  19.2 0.6 dynamic_slice.35
  22.0 0.8 fusion.20
  22.8 7.7 %convolution_reduce_fusion = f32[6912]{0:T(1024)S(1)} fusion(bf16[1152,1]{0,1:T(2,128)(2,1)S(1)} %reshape.350, bf16[1152,6912]{1,0:T(8,128)(2,1)} %param.29), kind=kOutput, calls=%fused_computation.17 | convolution fusion | flops 15925248 | bytes 15955200 | tf_op jit(solution)/shard_map/dot_general | solution.py:1245
  30.6 0.6 fusion.32
  31.5 0.7 maximum_multiply_fusion.gains_ref
  32.2 0.7 copy.49.gains_ref
  33.0 0.7 concatenate.58.vectors_ref
  33.6 6.7 %collective-permute-done.1 = s32[512,2]{0,1:T(2,128)S(1)} collective-permute-done((s32[512,2]{0,1:T(2,128)S(1)}, s32[512,2]{0,1:T(2,128)S(1)}, u32[]{:S(2)}, u32[]{:S(2)}) %collective-permute-start.1) | collective-permute-done | bytes 4128 | tf_op jit(solution)/shard_map/ppermute | solution.py:1223
  40.3 0.8 multiply_sine_fusion
  41.1 0.8 pad_maximum_fusion.4.cos_ref
  41.9 0.8 pad_maximum_fusion.5.sin_ref
  42.7 2.9 pad_maximum_fusion.x_ref
  45.5 23.6 %front.1 = (bf16[1024,1152]{1,0:T(8,128)(2,1)}, bf16[3,16,80,1024]{3,2,1,0:T(8,128)(2,1)}, bf16[2,16,72,1024]{3,2,1,0:T(8,128)(2,1)}, f32[2,16,1,1024]{3,2,1,0:T(1,128)}) custom-call(bf16[1024,1152]{1,0:T(8,128)(2,1)} %pad_maximum_fusion.x_ref, f32[1,1152]{1,0:T(1,128)} %get-tuple-element.99.scale_ref, f32[1,1152]{1,0:T(1,128)} %get-tuple-element.98.shift_ref, ...), custom_call_target="tpu_custom_call" | custom-call | flops 8153726976 | bytes 24000000 | tf_op jit(solution)/shard_map/front/pallas_call | solution.py:559
  69.1 20.4 %attend.1 = (bf16[16,72,1024]{2,1,0:T(8,128)(2,1)}, bf16[16,80,1024]{2,1,0:T(8,128)(2,1)}) custom-call(bf16[3,16,80,1024]{3,2,1,0:T(8,128)(2,1)} %get-tuple-element.41.q.k.v.k_ref.v_ref, bf16[3,16,80,1024]{3,2,1,0:T(8,128)(2,1)} %get-tuple-element.41.q.k.v.k_ref.v_ref, bf16[3,16,80,1024]{3,2,1,0:T(8,128)(2,1)} %get-tuple-element.41.q.k.v.k_ref.v_ref), custom_call_target="tpu_custom_call" | custom-call | flops 10737418240 | bytes 14000000 | tf_op jit(solution)/shard_map/attend/pallas_call | solution.py:611
  89.6 2.9 pad_maximum_fusion.1.c_ref
  92.4 9.5 %middle.1 = (bf16[1024,1152]{1,0:T(8,128)(2,1)}, bf16[1024,1152]{1,0:T(8,128)(2,1)}, bf16[1024,1152]{1,0:T(8,128)(2,1)}) custom-call(bf16[1152,1024]{1,0:T(8,128)(2,1)} %bitcast.93, bf16[1152,1152]{1,0:T(8,128)(2,1)} %w_ref.6, bf16[1024,1152]{1,0:T(8,128)(2,1)} %pad_maximum_fusion.x_ref, bf16[1024,1152]{1,0:T(8,128)(2,1)} %pad_maximum_fusion.1.c_ref, ...), custom_call_target="tpu_custom_call" | custom-call | flops 2717908992 | bytes 17000000 | tf_op jit(solution)/shard_map/middle/pallas_call | solution.py:646
  101.9 113.1 %mlp.1 = (f32[1024,1152]{1,0:T(8,128)}, f32[1024,1152]{1,0:T(8,128)}, bf16[2,3072,576]{2,1,0:T(8,128)(2,1)}, bf16[4,2,72,256]{3,2,1,0:T(8,128)(2,1)}, bf16[2,2,2,2,2,2,2,72,256]{8,7,6,5,4,3,2,1,0:T(8,128)(2,1)}) custom-call(bf16[1024,1152]{1,0:T(8,128)(2,1)} %get-tuple-element.43.entry_ref, bf16[1024,1152]{1,0:T(8,128)(2,1)} %get-tuple-element.44.fed_grad_ref, ...), custom_call_target="tpu_custom_call" | custom-call | flops 65229815808 | bytes 56000000 | tf_op jit(solution)/shard_map/mlp/pallas_call | solution.py:782
  215.0 19.0 %turn.1 = (bf16[1024,1152]{1,0:T(8,128)(2,1)}, f32[1024,1152]{1,0:T(8,128)}, bf16[1152,1024]{1,0:T(8,128)(2,1)}, bf16[2,1152,576]{2,1,0:T(8,128)(2,1)}, f32[8,1152]{1,0:T(8,128)}) custom-call(f32[1024,1152]{1,0:T(8,128)} %get-tuple-element.45.fed_ref, f32[1024,1152]{1,0:T(8,128)} %get-tuple-element.46.entry_grad_ref, ...), custom_call_target="tpu_custom_call" | custom-call | flops 5435817984 | bytes 35000000 | tf_op jit(solution)/shard_map/turn/pallas_call | solution.py:871
  234.1 87.5 %attend_back.1 = (bf16[3,16,72,1024]{3,2,1,0:T(8,128)(2,1)}, f32[2,72,1024]{2,1,0:T(8,128)}, bf16[2,96,576]{2,1,0:T(8,128)(2,1)}, bf16[2,2,72,256]{3,2,1,0:T(8,128)(2,1)}, bf16[72,576]{1,0:T(8,128)(2,1)}) custom-call(bf16[16,80,1024]{2,1,0:T(8,128)(2,1)} %get-tuple-element.49.q_ref, bf16[3,16,80,1024]{3,2,1,0:T(8,128)(2,1)} %get-tuple-element.41.q.k.v.k_ref.v_ref, ...), custom_call_target="tpu_custom_call" | custom-call | flops 26843545600 | bytes 32000000 | tf_op jit(solution)/shard_map/attend_back/pallas_call | solution.py:1034
  321.5 26.8 %back.1 = (bf16[1152,3456]{1,0:T(8,128)(2,1)}, f32[1152,1024]{1,0:T(8,128)}) custom-call(bf16[3,1152,1024]{2,1,0:T(8,128)(2,1)} %bitcast.114, bf16[1152,3456]{1,0:T(8,128)(2,1)} %w_ref.7, bf16[1024,1152]{1,0:T(8,128)(2,1)} %get-tuple-element.57.entry_ref), custom_call_target="tpu_custom_call" | custom-call | flops 16307453952 | bytes 32000000 | tf_op jit(solution)/shard_map/back/pallas_call | solution.py:1098
  349.1 18.6 %all-gather = s32[16,2,2]{2,1,0:T(2,128)S(1)} all-gather(s32[1,2,2]{2,1,0:T(2,128)S(1)} %bitcast.102), channel_id=1, replica_groups=mesh['img'=16,'band'=2] {'img'}, dimensions={0}, use_global_device_ids=true | all-gather | bytes 272 | tf_op jit(solution)/shard_map/all_gather | solution.py:1288
  367.8 2.7 gather_fusion
  371.3 7.5 %last.1 = (bf16[1024,1152]{1,0:T(8,128)(2,1)}, f32[8,1152]{1,0:T(8,128)}) custom-call(f32[1152,1024]{1,0:T(8,128)} %get-tuple-element.58.entry_grad_ref, bf16[1024,1152]{1,0:T(8,128)(2,1)} %pad_maximum_fusion.x_ref, f32[1024,1152]{1,0:T(8,128)} %get-tuple-element.59.middle_grad_ref, f32[1,1152]{1,0:T(1,128)} %get-tuple-element.99.scale_ref), custom_call_target="tpu_custom_call" | custom-call | flops 23592960 | bytes 17000000 | tf_op jit(solution)/shard_map/last/pallas_call | solution.py:1149
  378.8 3.0 slice_bitcast_fusion
  381.8 1.7 collective-permute-start.4
  383.5 1.6 slice_bitcast_fusion.1
  385.8 115.3 %all-gather.1 = bf16[32,1,7056]{2,1,0:T(2,128)(2,1)S(1)} all-gather(bf16[1,1,7056]{2,1,0:T(2,128)(2,1)S(1)} %bitcast.97), channel_id=1, replica_groups=mesh['img'=16,'band'=2] {'img','band'}, dimensions={0}, use_global_device_ids=true | all-gather | bytes 465696 | tf_op jit(solution)/shard_map/all_gather | solution.py:1287
  501.3 1.3 fusion.5
  502.7 10.3 %convolution_multiply_fusion = f32[32,1152]{1,0:T(8,128)S(1)} fusion(bf16[1152,6912]{1,0:T(8,128)(2,1)} %param.29, f32[32,1152]{1,0:T(8,128)S(1)} %get-tuple-element.111, bf16[32,7056]{1,0:T(8,128)(2,1)S(1)} %bitcast.89), kind=kOutput, calls=%fused_computation.10 | convolution fusion | flops 509902848 | bytes 16662528 | tf_op jit(solution)/shard_map/dot_general | solution.py:1295
  513.1 0.9 fusion.8
  514.0 0.7 convert_reduce_fusion
  514.7 0.7 convert_element_type.73
  515.9 1.6 reshape.301
  518.1 0.8 bitcast_convert_fusion
  518.9 4.4 fusion.7
  523.4 1.5 pad_maximum_fusion.3
  524.9 2.3 copy.56
  527.2 3.3 pad_maximum_fusion.2
  530.5 2.2 gather_fusion.2
  532.7 4.1 gather_fusion.1
  536.8 4.4 broadcast_select_fusion
  541.7 1.2 copy.57
  542.9 0.8 convert_element_type.71
  (111 shorter events, 5.6 us)
Async XLA Ops:
  7.2 14.6 %copy-start = (bf16[256,1152]{1,0:T(8,128)(2,1)S(1)}, bf16[256,1152]{1,0:T(8,128)(2,1)}, u32[]{:S(2)}) copy-start(bf16[256,1152]{1,0:T(8,128)(2,1)} %param.27) | copy-start | bytes 1769476
  7.2 517.7 %reduce-scatter.9.cloned.1.call-start = ((), (), s32[]{:S(2)}) async-start(), calls=%async_computation.3 | async-start | bytes 8460288
  7.3 6.0 %copy-start.13 = (s32[512]{0:T(512)S(1)}, s32[512]{0:T(512)}, u32[]{:S(2)}) copy-start(s32[512]{0:T(512)} %param.26) | copy-start | bytes 6148
  7.3 6.0 %copy-start.14 = (s32[512]{0:T(512)S(1)}, s32[512]{0:T(512)}, u32[]{:S(2)}) copy-start(s32[512]{0:T(512)} %param.25) | copy-start | bytes 6148
  7.3 6.1 %copy-start.3 = (bf16[2,512,1152]{2,1,0:T(8,128)(2,1)S(1)}, bf16[2,512,1152]{2,1,0:T(8,128)(2,1)}, u32[]{:S(2)}) copy-start(bf16[2,512,1152]{2,1,0:T(8,128)(2,1)} %param.21) | copy-start | bytes 7077892
  10.3 32.4 %collective-permute-start = (bf16[512,1152]{1,0:T(8,128)(2,1)}, bf16[512,1152]{1,0:T(8,128)(2,1)}, u32[]{:S(2)}, u32[]{:S(2)}) collective-permute-start(bf16[512,1152]{1,0:T(8,128)(2,1)} %get-tuple-element.87), channel_id=1, source_target_pairs={{0,1},{1,0},{2,3},{3,2},{4,5},{5,4},{6,7},{7,6},{8,9},{9,8},{10,11... | collective-permute-start | bytes 3538952 | tf_op jit(solution)/shard_map/ppermute | solution.py:1203
  13.2 3.3 copy-start.18
  13.3 3.9 copy-start.22
  13.3 6.0 %copy-start.20 = (s32[2]{0:T(128)S(1)}, s32[2]{0:T(128)}, u32[]{:S(2)}) copy-start(s32[2]{0:T(128)} %param.22) | copy-start | bytes 28
  13.3 27.1 %collective-permute-start.1 = (s32[512,2]{0,1:T(2,128)S(1)}, s32[512,2]{0,1:T(2,128)S(1)}, u32[]{:S(2)}, u32[]{:S(2)}) collective-permute-start(s32[512,2]{0,1:T(2,128)S(1)} %pad_add_fusion), channel_id=1, source_target_pairs={{0,1},{1,0},{2,3},{3,2},{4,5},{5,4},{6,7},{7,6},{8,9},{9,8},{10,11... | collective-permute-start | bytes 12296 | tf_op jit(solution)/shard_map/ppermute | solution.py:1223
  14.6 75.0 %collective-permute-start.2 = (bf16[512,1152]{1,0:T(8,128)(2,1)}, bf16[512,1152]{1,0:T(8,128)(2,1)}, u32[]{:S(2)}, u32[]{:S(2)}) collective-permute-start(bf16[512,1152]{1,0:T(8,128)(2,1)} %get-tuple-element.85), channel_id=1, source_target_pairs={{0,1},{1,0},{2,3},{3,2},{4,5},{5,4},{6,7},{7,6},{8,9},{9,8},{10,11... | collective-permute-start | bytes 3538952 | tf_op jit(solution)/shard_map/ppermute | solution.py:1203
  22.8 7.8 %copy-start.12 = (f32[6912]{0:T(1024)S(1)}, f32[6912]{0:T(1024)}, u32[]{:S(2)}) copy-start(f32[6912]{0:T(1024)} %param.30) | copy-start | bytes 82948
  22.8 8.5 %copy-start.15 = (f32[72]{0:T(128)S(1)}, f32[72]{0:T(128)}, u32[]{:S(2)}) copy-start(f32[72]{0:T(128)} %param.33) | copy-start | bytes 868
  22.8 8.6 %copy-start.16 = (f32[72]{0:T(128)S(1)}, f32[72]{0:T(128)}, u32[]{:S(2)}) copy-start(f32[72]{0:T(128)} %param.32) | copy-start | bytes 868
  22.8 8.7 %copy-start.17 = (f32[2]{0:T(128)S(1)}, f32[2]{0:T(128)}, u32[]{:S(2)}) copy-start(f32[2]{0:T(128)} %constant.121.clone) | copy-start | bytes 28
  348.3 0.7 copy-start.19
  348.3 0.7 copy-start.21
  348.3 22.4 %copy-start.23 = (f32[8]{0:T(128)S(1)}, f32[8]{0:T(128)}, u32[]{:S(2)}) copy-start(f32[8]{0:T(128)} %param.24) | copy-start | bytes 100
  348.3 193.4 %reduce-scatter.7.cloned.1.call-start = ((), (), s32[]{:S(2)}) async-start(), calls=%async_computation.2 | async-start | bytes 1327104
  378.8 4.7 copy-start.4
  381.8 141.6 %collective-permute-start.4 = (bf16[512,1152]{1,0:T(8,128)(2,1)S(1)}, bf16[512,1152]{1,0:T(8,128)(2,1)}, u32[]{:S(2)}, u32[]{:S(2)}) collective-permute-start(bf16[512,1152]{1,0:T(8,128)(2,1)S(1)} %get-tuple-element.81), channel_id=1, source_target_pairs={{0,1},{1,0},{2,3},{3,2},{4,5},{5,4},{6,7},{7,6},{8,9},{9,8},{10,11... | collective-permute-start | bytes 3538952 | tf_op jit(solution)/shard_map/ppermute | solution.py:1211
  383.5 1.9 copy-start.11
  383.5 1.9 copy-start.10
  383.5 1.9 copy-start.5
  385.1 142.1 %collective-permute-start.3 = (bf16[512,1152]{1,0:T(8,128)(2,1)}, bf16[512,1152]{1,0:T(8,128)(2,1)}, u32[]{:S(2)}, u32[]{:S(2)}) collective-permute-start(bf16[512,1152]{1,0:T(8,128)(2,1)} %get-tuple-element.83), channel_id=1, source_target_pairs={{0,1},{1,0},{2,3},{3,2},{4,5},{5,4},{6,7},{7,6},{8,9},{9,8},{10,11... | collective-permute-start | bytes 3538952 | tf_op jit(solution)/shard_map/ppermute | solution.py:1211
  502.6 10.3 %copy-start.6 = (bf16[4,2,72,256]{3,2,1,0:T(8,128)(2,1)S(1)}, bf16[4,2,72,256]{3,2,1,0:T(8,128)(2,1)}, u32[]{:S(2)}) copy-start(bf16[4,2,72,256]{3,2,1,0:T(8,128)(2,1)} %get-tuple-element.66) | copy-start | bytes 884740
  502.7 10.3 %copy-start.8 = (bf16[2,2,72,256]{3,2,1,0:T(8,128)(2,1)S(1)}, bf16[2,2,72,256]{3,2,1,0:T(8,128)(2,1)}, u32[]{:S(2)}) copy-start(bf16[2,2,72,256]{3,2,1,0:T(8,128)(2,1)} %get-tuple-element.67) | copy-start | bytes 442372
  502.7 12.1 %copy-start.9 = (bf16[72,576]{1,0:T(8,128)(2,1)S(1)}, bf16[72,576]{1,0:T(8,128)(2,1)}, u32[]{:S(2)}) copy-start(bf16[72,576]{1,0:T(8,128)(2,1)} %get-tuple-element.65) | copy-start | bytes 248836
  513.1 5.0 copy-start.7
  518.9 4.4 copy-start.2
  532.7 4.1 copy-start.1
Sparse Core Ops, SparseCore 0:
  348.4 100.2 reduce-scatter.8
  527.3 14.3 reduce-scatter.6

commit v3 on v2

--- a/solution.py
+++ b/solution.py
@@ -428,6 +428,20 @@
     pl.semaphore_wait(barrier, len(places))
 
 
+def dispatch(value, cases):
+    if not cases:
+        return
+    keys = sorted(cases)
+    if len(keys) == 1:
+        pl.when(value == keys[0])(cases[keys[0]])
+        return
+    middle = keys[len(keys) // 2]
+    low = {key: cases[key] for key in keys if key < middle}
+    high = {key: cases[key] for key in keys if key >= middle}
+    pl.when(value < middle)(functools.partial(dispatch, value, low))
+    pl.when(value >= middle)(functools.partial(dispatch, value, high))
+
+
 class Halving:
     def __init__(self, places, dims, order, held, arrived, send, receive, lead=(), tail=()):
         self.places, self.dims, self.order = places, list(dims), list(order)
@@ -452,6 +466,14 @@
             else:
                 picked.append(slice(None))
         return picked
+
+    def settled(self, step):
+        picked = []
+        for name in self.dims:
+            place = self.order.index(name)
+            if place > 0:
+                picked.append(self.places[name] if place < step else slice(None))
+        return self.lead + tuple(picked)
 
     def copy(self, step, source=None):
         if step == 0:
@@ -477,29 +499,46 @@
 
     def add(self, step, source=None, put=None):
         picked = self.held_index(step, True)
-        free = [place for place, entry in enumerate(picked) if isinstance(entry, slice)]
-        if not free:
-            total = self.held[self.lead + tuple(picked)].astype(f32)
-            put(total + self.arrived[step][self.lead + (...,)].astype(f32))
-            return
-
-        def one(number, _):
-            digits = [lax.rem(lax.div(number, 2**place), 2) for place in range(len(free))]
-            target = list(picked)
-            for place, digit in zip(free, digits):
-                target[place] = digit
-            if source is not None:
-                rest = iter(digits)
-                spot = [next(rest) if isinstance(e, slice) else e for e in self.source_index(True)]
-                old = source[tuple(spot)]
-            else:
-                old = self.held[self.lead + tuple(target)]
-            self.held[self.lead + tuple(target)] = (
-                old + self.arrived[step][self.lead + tuple(digits)]
-            )
-            return 0
-
-        lax.fori_loop(0, 2 ** len(free), one, 0)
+        spot = self.lead + tuple(picked)
+        if source is None:
+            old = self.held[spot + (...,)]
+        else:
+            old = source[tuple(self.source_index(True)) + self.tail + (...,)]
+        new = self.arrived[step][self.lead + (...,)]
+        if step == len(self.order) - 1:
+            put(old.astype(f32) + new.astype(f32))
+        else:
+            self.held[spot + (...,)] = old + new
+
+
+class Doubling:
+    def __init__(self, places, dims, order, blocks, send, receive):
+        self.places, self.dims, self.order = places, list(dims), list(order)
+        self.blocks, self.send, self.receive = blocks, send, receive
+
+    def own(self):
+        return tuple(self.places[name] for name in self.dims)
+
+    def copy(self, step):
+        known = self.order[:step]
+        spot = tuple(slice(None) if n in known else self.places[n] for n in self.dims)
+        return pltpu.make_async_remote_copy(
+            src_ref=self.blocks.at[spot],
+            dst_ref=self.blocks.at[spot],
+            send_sem=self.send.at[step],
+            recv_sem=self.receive.at[step],
+            device_id=partner_id(self.order[step], self.places),
+            device_id_type=MESH_ID,
+        )
+
+
+def doubling_order(dims):
+    bits = [name for name in dims if name not in ("y", "b0", "b1")]
+    return bits + ["y", "b1", "b0"]
+
+
+def doubling_scratch(dims):
+    return [pltpu.SemaphoreType.DMA((len(dims),))] * 2
 
 
 def halving_scratch(dims, tail, lead=()):
@@ -516,17 +555,21 @@
 
 
 def front_kernel(
-    x_ref, scale_ref, shift_ref, w_ref, gains_ref, cos_ref, sin_ref,
+    own_ref, other_ref, scale_ref, shift_ref, w_ref, gains_ref, cos_ref, sin_ref,
     entry_ref, heads_ref, unit_ref, factor_ref,
 ):
     section = pl.program_id(0)
-    patches = x_ref.shape[0]
+    patches = entry_ref.shape[0]
+    half = patches // 2
 
     @pl.when(section == 0)
     def _():
-        source = x_ref[...].astype(f32)
-        normed = source * lax.rsqrt(jnp.mean(source * source, axis=1, keepdims=True) + epsilon)
-        entry_ref[...] = (normed * (1.0 + scale_ref[...]) + shift_ref[...]).astype(bf16)
+        for number, ref in enumerate((own_ref, other_ref)):
+            source = ref[...].astype(f32)
+            normed = source * lax.rsqrt(jnp.mean(source * source, axis=1, keepdims=True) + epsilon)
+            entry_ref[number * half : (number + 1) * half, :] = (
+                normed * (1.0 + scale_ref[...]) + shift_ref[...]
+            ).astype(bf16)
 
     raw = dot(w_ref[...], entry_ref[...], 0, 1)
 
@@ -553,14 +596,20 @@
             heads_ref[0, head] = jnp.concatenate([part, extra], axis=0).astype(bf16)
 
 
-def front(x, scale, shift, qkv_weight, gains, cosine, sine):
-    patches, width = x.shape
+def own_image(rows, width, block):
+    return pl.BlockSpec((None, rows, width), lambda t: (lax.axis_index("band"), block(t), 0))
+
+
+def front(images, other, scale, shift, qkv_weight, gains, cosine, sine):
+    half, width = other.shape
+    patches = 2 * half
     last = lambda s: jnp.minimum(s, 1)
     return pl.pallas_call(
         front_kernel,
         grid=(3,),
         in_specs=[
-            whole((patches, width)),
+            own_image(half, width, lambda s: 0),
+            whole((half, width)),
             whole((1, width)),
             whole((1, width)),
             pl.BlockSpec((width, width), lambda s: (0, s)),
@@ -583,7 +632,7 @@
         compiler_params=params_of(),
         cost_estimate=cost(6 * patches * width * width, 24e6),
         name="front",
-    )(x, scale, shift, qkv_weight, gains, cosine, sine)
+    )(images, other, scale, shift, qkv_weight, gains, cosine, sine)
 
 
 def attend_kernel(q_ref, k_ref, v_ref, mixed_ref, lse_ref, qext_ref):
@@ -627,30 +676,40 @@
 
 
 def middle_kernel(
-    mixed_ref, w_ref, x_ref, c_ref, vectors_ref, attended_ref, entry_ref, fed_grad_ref
+    mixed_ref, w_ref, own_x_ref, other_x_ref, own_c_ref, other_c_ref, vectors_ref,
+    attended_ref, entry_ref, fed_grad_ref,
 ):
+    in_own = pl.program_id(0) < pl.num_programs(0) // 2
+    x = jnp.where(in_own, own_x_ref[...].astype(f32), other_x_ref[...].astype(f32))
+    c = jnp.where(in_own, own_c_ref[...].astype(f32), other_c_ref[...].astype(f32))
     attended = dot(mixed_ref[...], w_ref[...], 0, 0)
     attended_bf = attended.astype(bf16)
     attended_ref[...] = attended_bf
     gate_one, scale_two, shift_two, gate_two = [vectors_ref[i : i + 1, :] for i in range(4)]
-    middle = x_ref[...].astype(f32) + gate_one * attended_bf.astype(f32)
+    middle = x + gate_one * attended_bf.astype(f32)
     normed = middle * lax.rsqrt(jnp.mean(middle * middle, axis=1, keepdims=True) + epsilon)
     entry_ref[...] = (normed * (1.0 + scale_two) + shift_two).astype(bf16)
-    fed_grad_ref[...] = (c_ref[...].astype(f32) * gate_two).astype(bf16)
-
-
-def middle_step(mixed, proj_weight, x, c, vectors):
-    patches, width = x.shape
+    fed_grad_ref[...] = (c * gate_two).astype(bf16)
+
+
+def middle_step(mixed, proj_weight, latents, other_x, cotangent, other_c, vectors):
+    half, width = other_x.shape
+    patches = 2 * half
     rows = 256
+    blocks = half // rows
     block = pl.BlockSpec((rows, width), lambda t: (t, 0))
+    own = own_image(rows, width, lambda t: jnp.minimum(t, blocks - 1))
+    other = pl.BlockSpec((rows, width), lambda t: (jnp.maximum(t - blocks, 0), 0))
     return pl.pallas_call(
         middle_kernel,
         grid=(patches // rows,),
         in_specs=[
             pl.BlockSpec((width, rows), lambda t: (0, t)),
             whole((width, width)),
-            block,
-            block,
+            own,
+            other,
+            own,
+            other,
             whole((8, width)),
         ],
         out_specs=[block] * 3,
@@ -658,23 +717,24 @@
         compiler_params=params_of(),
         cost_estimate=cost(2 * patches * width * width, 17e6),
         name="middle",
-    )(mixed, proj_weight, x, c, vectors)
+    )(mixed, proj_weight, latents, other_x, cotangent, other_c, vectors)
 
 
 MLP_TILE = 512
 MLP_SUB = 256
-HOSTED = 4
+HOSTED = 5
+CARRIED = ((3, 4), (4, 2))
 
 
 def mlp_kernel(
     dims, entry_ref, fed_grad_ref, wg_ref, wu_ref, wd_ref,
-    fed_ref, entry_grad_ref, down_ref, done_ref, left_ref,
-    hidden_ref, gate_grad_ref, up_grad_ref, source_ref, left_sem, held, *rest,
+    fed_ref, entry_grad_ref, down_ref, done_ref, left_ref, *rest,
 ):
-    *arrived, send, receive = rest
+    carry_refs, rest = rest[: 2 * len(CARRIED)], rest[2 * len(CARRIED) :]
+    hidden_ref, gate_grad_ref, up_grad_ref, source_ref, left_sem, held, *arrived, send, receive = rest
     tile = pl.program_id(0)
     places = own_places()
-    orders = [order_of(dims, "b0", "y", "b1"), order_of(dims, "b0", "b1", "y")]
+    orders = mlp_orders(dims)
     steps = len(dims)
 
     def streams(number):
@@ -695,59 +755,50 @@
                     done_ref[number, sub] = values.astype(bf16)
 
                 stream.add(step, source if step == 0 else None, put)
+                leaves = [place for place, (_, ended) in enumerate(CARRIED) if ended == step + 1]
+                for place in leaves:
+
+                    @pl.when(number == CARRIED[place][0])
+                    def _():
+                        carry_refs[2 * place + sub][...] = held[stream.settled(step + 1)]
+
                 if step + 1 < steps:
-                    stream.copy(step + 1).start()
+                    goes_on = True
+                    for place in leaves:
+                        goes_on = goes_on & (number != CARRIED[place][0])
+                    if leaves:
+                        pl.when(goes_on)(stream.copy(step + 1).start)
+                    else:
+                        stream.copy(step + 1).start()
 
     @pl.when(tile == 0)
     def _():
+        fed_ref[...] = jnp.zeros_like(fed_ref)
+        entry_grad_ref[...] = jnp.zeros_like(entry_grad_ref)
         greet(places)
 
     entry = entry_ref[...]
     fed_grad = fed_grad_ref[...]
     gate = dot(entry, wg_ref[...], 1, 0)
     up = dot(entry, wu_ref[...], 1, 0)
-    advance(tile - 2, 3)
-    advance(tile - 1, 0)
     sigma = jax.nn.sigmoid(gate)
     silu = gate * sigma
     hidden_ref[...] = (silu * up).astype(bf16)
     hidden_grad = dot(fed_grad, wd_ref[...], 1, 1)
     gate_grad_ref[...] = (hidden_grad * up * (sigma * (1.0 + gate * (1.0 - sigma)))).astype(bf16)
     up_grad_ref[...] = (hidden_grad * silu).astype(bf16)
-    fed = dot(hidden_ref[...], wd_ref[...], 1, 0)
-    entry_grad = dot(gate_grad_ref[...], wg_ref[...], 1, 1) + dot(
+    advance(tile - 3, 4)
+    advance(tile - 2, 2)
+    advance(tile - 1, 0)
+    fed_ref[...] += dot(hidden_ref[...], wd_ref[...], 1, 0)
+    entry_grad_ref[...] += dot(gate_grad_ref[...], wg_ref[...], 1, 1) + dot(
         up_grad_ref[...], wu_ref[...], 1, 1
     )
-
-    @pl.when(tile == 0)
-    def _():
-        fed_ref[...] = fed
-        entry_grad_ref[...] = entry_grad
-
-    @pl.when(tile > 0)
-    def _():
-        fed_ref[...] += fed
-        entry_grad_ref[...] += entry_grad
-
-    for step in range(4, steps):
-        advance(tile - 2, step)
-    advance(tile - 1, 1)
-    down = dot(hidden_ref[...], fed_grad, 0, 0)
+    down = dot(hidden_ref[...], fed_grad, 0, 0).astype(bf16)
     column_half = down.shape[1] // 2
-    down_ref[0] = down[:, :column_half].astype(bf16)
-    down_ref[1] = down[:, column_half:].astype(bf16)
+    down_ref[0] = down[:, :column_half]
+    down_ref[1] = down[:, column_half:]
     grads = [dot(entry, ref[...], 0, 0) for ref in (gate_grad_ref, up_grad_ref)]
-    advance(tile - 1, 2)
-
-    def leave(number):
-        return pltpu.make_async_copy(
-            source_ref, left_ref.at[jnp.maximum(number - HOSTED, 0)], left_sem
-        )
-
-    @pl.when(tile > HOSTED)
-    def _():
-        leave(tile - 1).wait()
-
     blocks = 2 ** (steps - 1)
     rows = grads[0].shape[0] // blocks
     for half, grad in enumerate(grads):
@@ -762,13 +813,28 @@
         for sub, stream in enumerate(streams(tile)):
             stream.copy(0, source_ref.at[sub]).start()
 
-    @pl.when(tile >= HOSTED)
+    @pl.when(tile == HOSTED)
     def _():
-        leave(tile).start()
-
-    @pl.when(tile == pl.num_programs(0) - 1)
+        pltpu.make_async_copy(source_ref, left_ref, left_sem).start()
+
+    advance(tile - 2, 3)
+    advance(tile - 1, 1)
+
+    @pl.when(tile == HOSTED)
     def _():
-        leave(tile).wait()
+        pltpu.make_async_copy(source_ref, left_ref, left_sem).wait()
+
+
+def mlp_orders(dims):
+    return [order_of(dims, "b0", "y", "b2", "b1"), order_of(dims, "b0", "b1", "y", "b2")]
+
+
+def carried_orders(dims):
+    return [order[ended:] for _, ended in CARRIED for order in mlp_orders(dims)]
+
+
+def carried_dims(dims):
+    return [[name for name in dims if name in order] for order in carried_orders(dims)]
 
 
 def mlp(entry, fed_grad, gateup_weight, down_weight):
@@ -779,6 +845,7 @@
     dims = pair_axes()
     rows = width // lax.axis_size("img")
     tail = (rows, MLP_SUB)
+    carried = [(2,) * len(names) + tail for names in carried_dims(dims)]
     return pl.pallas_call(
         functools.partial(mlp_kernel, dims),
         grid=(tiles,),
@@ -793,16 +860,18 @@
             whole((patches, width)),
             whole((patches, width)),
             pl.BlockSpec((2, tile, width // 2), lambda t: (0, t, 0)),
-            whole((HOSTED, 2) + tail),
+            whole((HOSTED - len(CARRIED), 2) + tail),
             pl.BlockSpec(memory_space=pl.ANY),
-        ],
+        ]
+        + [whole(shape) for shape in carried],
         out_shape=[
             jax.ShapeDtypeStruct((patches, width), f32),
             jax.ShapeDtypeStruct((patches, width), f32),
             jax.ShapeDtypeStruct((2, inner, width // 2), bf16),
-            jax.ShapeDtypeStruct((HOSTED, 2) + tail, bf16),
-            jax.ShapeDtypeStruct((tiles - HOSTED, 2) + (2,) * len(dims) + tail, bf16),
-        ],
+            jax.ShapeDtypeStruct((HOSTED - len(CARRIED), 2) + tail, bf16),
+            jax.ShapeDtypeStruct((2,) + (2,) * len(dims) + tail, bf16),
+        ]
+        + [jax.ShapeDtypeStruct(shape, bf16) for shape in carried],
         scratch_shapes=[pltpu.VMEM((patches, tile), bf16)] * 3
         + [pltpu.VMEM((2,) + (2,) * len(dims) + tail, bf16), pltpu.SemaphoreType.DMA]
         + halving_scratch(dims, tail, (2, 2)),
@@ -812,162 +881,234 @@
     )(entry, fed_grad, gateup_weight, gateup_weight, down_weight)
 
 
-def turn_kernel(
-    fed_ref, entry_grad_ref, x_ref, attended_ref, c_ref, mixed_ref, w_ref, vectors_ref,
-    result_ref, middle_grad_ref, mixed_grad_ref, grad_proj_ref, sums_ref, total_ref,
+TURN_ROWS = 128
+
+
+def core_plan(dims):
+    return [
+        ("down", 0, order_of(dims, "b0", "y", "b1", "b2", "b3"), (2, 9, 25, 31, 35, 40)),
+        ("down", 1, order_of(dims, "b0", "b2", "y", "b3", "b1"), (2, 9, 23, 27, 33, 35)),
+        ("down", 2, order_of(dims, "b0", "b2", "b3", "b1", "y"), (0, 6, 21, 31, 35, 37)),
+        ("down", 3, order_of(dims, "b0", "b1", "b2", "y", "b3"), (2, 9, 23, 31, 35, 40)),
+        ("left", 0, order_of(dims, "b0", "b1", "y", "b2", "b3"), (1, 6, 11, 21, 25, 29)),
+        ("left", 1, order_of(dims, "b0", "b2", "b1", "b3", "y"), (0, 3, 9, 15, 19, 21)),
+        ("proj", 0, order_of(dims, "b0", "b1", "y", "b2", "b3"), (7, 11, 27, 33, 37, 44)),
+        ("carry", 0, ["b3"], (0, 3)),
+        ("carry", 1, ["b3"], (0, 3)),
+        ("carry", 2, ["b2", "b1", "b3"], (0, 4, 6, 9)),
+        ("carry", 3, ["y", "b2", "b3"], (0, 7, 11, 15)),
+    ]
+
+
+def core_kernel(
+    dims, fed_ref, entry_grad_ref, own_x_ref, other_x_ref, own_c_ref, other_c_ref, attended_ref,
+    all_mixed_ref, w_ref, vectors_ref, codes_ref,
+    q_ref, k_ref, v_ref, mixed_ref, unit_ref, factor_ref, gains_ref, cos_ref, sin_ref,
+    down_ref, left_ref, *rest,
 ):
+    carry_refs, rest = rest[: 2 * len(CARRIED)], rest[2 * len(CARRIED) :]
+    (
+        result_ref, middle_grad_ref, out_ref, gain_out_ref,
+        down_out_ref, left_out_ref, carry_out_ref, proj_out_ref, modes_out_ref,
+        attended_grad_ref, mixed_grad_ref, proj_ref, rows_ref, row_send, row_receive,
+        mg_ext_ref, acc_ref, own_sem, modes_ref, doubling_send, doubling_receive, *buffers,
+    ) = rest
     step = pl.program_id(0)
-    gate_one, scale_two, _, gate_two = [vectors_ref[i : i + 1, :] for i in range(4)]
-    attended = attended_ref[...].astype(f32)
-    upstream = c_ref[...].astype(f32)
-    fed = fed_ref[...]
-    middle = x_ref[...].astype(f32) + gate_one * attended
-    result_ref[...] = (middle + gate_two * fed).astype(bf16)
-    factor = lax.rsqrt(jnp.mean(middle * middle, axis=1, keepdims=True) + epsilon)
-    normed = middle * factor
-    entry_grad = entry_grad_ref[...]
-    inner = entry_grad * (1.0 + scale_two)
-    middle_grad = upstream + factor * (
-        inner - normed * jnp.mean(inner * normed, axis=1, keepdims=True)
-    )
-    middle_grad_ref[...] = middle_grad
-    attended_grad = (middle_grad * gate_one).astype(bf16)
-    mixed_grad_ref[...] = dot(w_ref[...], attended_grad, 1, 1).astype(bf16)
-    grad_proj = dot(mixed_ref[...], attended_grad, 1, 0)
-    add = lambda v: jnp.sum(v, axis=0, keepdims=True)
-    sums = jnp.concatenate(
-        [
-            add(middle_grad * attended),
-            add(entry_grad),
-            add(entry_grad * normed),
-            add(upstream * fed),
-            jnp.zeros((4, fed.shape[1]), f32),
-        ],
-        axis=0,
-    )
+    places = own_places()
+    patches = q_ref.shape[-1]
+    turns = patches // TURN_ROWS
+    axes = len(dims)
+    carries = carried_dims(dims)
+    groups, used = {}, 0
+    kinds = [("down", axes), ("left", axes), ("proj", axes)]
+    kinds += [(f"carry{part}", len(names)) for part, names in enumerate(carries)]
+    for name, count in kinds:
+        groups[name] = buffers[used : used + count + 3]
+        used += count + 3
+
+    def streams():
+        for number, (name, part, order, points) in enumerate(core_plan(dims)):
+            names, lead, tail = dims, (), ()
+            if name == "down":
+                lead = (part,)
+                source = down_ref
+                rows = source.shape[-2] // 4
+                tail = (pl.ds(part * rows, rows), slice(None))
+                out, spot = down_out_ref, (part,)
+            elif name == "left":
+                lead = (part,)
+                source = left_ref.at[part]
+                out, spot = left_out_ref, (part,)
+            elif name == "proj":
+                source, out, spot = proj_ref, proj_out_ref, ()
+            else:
+                names = carries[part]
+                source = carry_refs[part]
+                out, spot = carry_out_ref, (part,)
+            held, *arrived, send, receive = groups[name if name in groups else f"{name}{part}"]
+            stream = Halving(places, names, order, held, arrived, send, receive, lead, tail)
+            yield number, name, stream, source, points, out, spot
+
+    def events(point):
+        for number, name, stream, source, points, out, spot in streams():
+            local = name in ("proj", "carry")
+            steps = len(points) - 1
+            for phase in range(-1, steps):
+                if points[phase + 1] != point:
+                    continue
+                if phase >= 0:
+                    stream.copy(phase, source).wait()
+                    if phase == 0 and not local:
+                        stream.own_half(source, own_sem.at[number]).wait()
+
+                    def put(values):
+                        out[spot + (...,)] = values.astype(bf16)
+
+                    stream.add(phase, source if local and phase == 0 else None, put)
+                if phase + 1 < steps:
+                    stream.copy(phase + 1, source).start()
+                    if phase < 0 and not local:
+                        stream.own_half(source, own_sem.at[number]).start()
+
+    band = places["y"]
+
+    def away(number):
+        return pltpu.make_async_remote_copy(
+            src_ref=rows_ref.at[number],
+            dst_ref=result_ref.at[band, pl.ds(number * TURN_ROWS, TURN_ROWS)],
+            send_sem=row_send.at[number],
+            recv_sem=row_receive.at[number],
+            device_id=partner_id("y", places),
+            device_id_type=MESH_ID,
+        )
+
+    def stay(number):
+        return pltpu.make_async_copy(
+            rows_ref.at[number + turns // 2],
+            result_ref.at[band, pl.ds(number * TURN_ROWS, TURN_ROWS)],
+            row_send.at[number + turns // 2],
+        )
 
     @pl.when(step == 0)
     def _():
-        total_ref[...] = grad_proj
-        sums_ref[...] = sums
-
-    @pl.when(step > 0)
+        greet(places)
+
+    doubling = Doubling(places, dims, doubling_order(dims), modes_ref, doubling_send, doubling_receive)
+    width = w_ref.shape[0]
+    half = width // 2
+    pair = 2 * TURN_ROWS
+
+    def turn(number):
+        x_ref, c_ref = (own_x_ref, own_c_ref) if number >= turns // 2 else (other_x_ref, other_c_ref)
+        gate_one, scale_two, _, gate_two = [vectors_ref[i : i + 1, :] for i in range(4)]
+        attended = attended_ref[...].astype(f32)
+        upstream = c_ref[...].astype(f32)
+        fed = fed_ref[...]
+        middle = x_ref[...].astype(f32) + gate_one * attended
+        rows_ref[number] = (middle + gate_two * fed).astype(bf16)
+        factor = lax.rsqrt(jnp.mean(middle * middle, axis=1, keepdims=True) + epsilon)
+        normed = middle * factor
+        entry_grad = entry_grad_ref[...]
+        inner = entry_grad * (1.0 + scale_two)
+        middle_grad = upstream + factor * (
+            inner - normed * jnp.mean(inner * normed, axis=1, keepdims=True)
+        )
+        middle_grad_ref[...] = middle_grad
+        start = (number + turns // 2) % turns * TURN_ROWS
+        attended_grad_ref[start : start + TURN_ROWS, :] = (middle_grad * gate_one).astype(bf16)
+        add = lambda v: jnp.sum(v, axis=0, keepdims=True)
+        sums = jnp.concatenate(
+            [
+                add(middle_grad * attended),
+                add(entry_grad),
+                add(entry_grad * normed),
+                add(upstream * fed),
+            ],
+            axis=0,
+        )
+        if number == 0:
+            modes_ref[doubling.own() + (slice(None), slice(0, width))] = sums
+            modes_ref[doubling.own() + (slice(None), slice(width, None))] = codes_ref[...]
+        else:
+            modes_ref[doubling.own() + (slice(None), slice(0, width))] += sums
+        if number < turns // 2:
+            away(number).start()
+        else:
+            stay(number - turns // 2).start()
+        if number % 2 == 1:
+            first = start - TURN_ROWS
+            grads = dot(w_ref[...], attended_grad_ref[first : first + pair, :], 1, 1)
+            for head in range(HEADS):
+                mixed_grad_ref[head, :, first : first + pair] = grads[
+                    head * HD : (head + 1) * HD, :
+                ].astype(bf16)
+        if number == turns - 1:
+            blocks = 2 ** (axes - 1)
+            rows = width // blocks
+            grads = dot(all_mixed_ref[...], attended_grad_ref[...], 1, 0)
+            for block in range(blocks):
+                spot = tuple(block // 2**bit % 2 for bit in reversed(range(axes - 1)))
+                part = grads[block * rows : (block + 1) * rows, :]
+                proj_ref[(0,) + spot] = part[:, :half].astype(bf16)
+                proj_ref[(1,) + spot] = part[:, half:].astype(bf16)
+            doubling.copy(0).start()
+        events(number)
+
+    for number in range(turns):
+
+        @pl.when(step == number)
+        def _():
+            turn(number)
+
+    points = {point for plan in core_plan(dims) for point in plan[3]}
+
+    class Events:
+        @staticmethod
+        def at_head(head, end):
+            def run(now):
+                if turns + 2 * now + end in points:
+                    events(turns + 2 * now + end)
+                turn, odd = divmod(now - 2, 2)
+                if end and odd == 0 and 0 <= turn < axes:
+                    doubling.copy(turn).wait()
+                    if turn + 1 < axes:
+                        doubling.copy(turn + 1).start()
+
+            wanted = [
+                now
+                for now in range(HEADS)
+                if turns + 2 * now + end in points or (end and now in range(2, 2 + 2 * axes, 2))
+            ]
+            dispatch(head, {now: functools.partial(run, now) for now in wanted})
+
+    @pl.when(step >= turns)
     def _():
-        total_ref[...] += grad_proj
-        sums_ref[...] += sums
+        attend_back(
+            step - turns, Events(), mixed_grad_ref,
+            q_ref, k_ref, v_ref, mixed_ref, unit_ref, factor_ref, gains_ref, cos_ref, sin_ref,
+            out_ref, gain_out_ref, mg_ext_ref, acc_ref,
+        )
 
     @pl.when(step == pl.num_programs(0) - 1)
     def _():
-        half = total_ref.shape[1] // 2
-        grad_proj_ref[0] = total_ref[:, :half].astype(bf16)
-        grad_proj_ref[1] = total_ref[:, half:].astype(bf16)
-
-
-def turn_step(fed, entry_grad, x, attended, c, mixed, proj_weight, vectors):
-    patches, width = x.shape
-    rows = 256
-    block = pl.BlockSpec((rows, width), lambda t: (t, 0))
-    across = pl.BlockSpec((width, rows), lambda t: (0, t))
-    return pl.pallas_call(
-        turn_kernel,
-        grid=(patches // rows,),
-        in_specs=[block] * 5 + [across, whole((width, width)), whole((8, width))],
-        out_specs=[
-            block,
-            block,
-            across,
-            pl.BlockSpec((2, width, width // 2), lambda t: (0, 0, 0)),
-            pl.BlockSpec((8, width), lambda t: (0, 0)),
-        ],
-        out_shape=[
-            jax.ShapeDtypeStruct((patches, width), bf16),
-            jax.ShapeDtypeStruct((patches, width), f32),
-            jax.ShapeDtypeStruct((width, patches), bf16),
-            jax.ShapeDtypeStruct((2, width, width // 2), bf16),
-            jax.ShapeDtypeStruct((8, width), f32),
-        ],
-        scratch_shapes=[pltpu.VMEM((width, width), f32)],
-        compiler_params=params_of(),
-        cost_estimate=cost(4 * patches * width * width, 35e6),
-        name="turn",
-    )(fed, entry_grad, x, attended, c, mixed, proj_weight, vectors)
-
-
-def back_plan(dims):
-    first, second = pl.ds(0, 96), pl.ds(96, 96)
-    return [
-        ("down", (0,), (first,), order_of(dims, "b0", "b1", "b2", "y"), (0, 2, 8, 11, 13, 15)),
-        ("down", (1,), (second,), order_of(dims, "b0", "b2", "b1", "y"), (0, 2, 8, 11, 13, 15)),
-        ("left", (0, 0), (), order_of(dims, "b0", "y", "b1"), (0, 3, 7, 10, 12, 14)),
-        ("left", (1, 0), (), order_of(dims, "b0", "y", "b1"), (0, 3, 7, 10, 12, 14)),
-        ("left", (0, 1), (), order_of(dims, "b0", "y", "b2"), (0, 3, 10, 12, 14, 15)),
-        ("left", (1, 1), (), order_of(dims, "b0", "y", "b2"), (0, 3, 10, 12, 14, 15)),
-        ("proj", (), (), order_of(dims, "b0", "y", "b1"), (1, 4, 12, 14, 15, 15)),
-    ]
-
-
-def attend_back_kernel(
-    dims, q_ref, k_ref, v_ref, mg_ref, mixed_ref, unit_ref, factor_ref, gains_ref, cos_ref,
-    sin_ref, down_ref, left_ref, proj_ref,
-    out_ref, gain_out_ref, down_out_ref, left_out_ref, proj_out_ref,
-    mg_ext_ref, acc_ref, own_sem, *buffers,
+        last = max(point for stream in core_plan(dims) for point in stream[3])
+        for point in range(turns + 2 * HEADS, last + 1):
+            events(point)
+        modes_out_ref[...] = modes_ref[...]
+        for number in range(turns // 2):
+            away(number).wait()
+            stay(number).wait()
+
+
+def attend_back(
+    head, events, mixed_grad_ref,
+    q_ref, k_ref, v_ref, mixed_ref, unit_ref, factor_ref, gains_ref, cos_ref, sin_ref,
+    out_ref, gain_out_ref, mg_ext_ref, acc_ref,
 ):
-    head = pl.program_id(0)
-    places = own_places()
-    steps = len(dims)
-    sizes = steps + 3
-    groups = {
-        name: buffers[place * sizes : (place + 1) * sizes]
-        for place, name in enumerate(("down", "left", "proj"))
-    }
-    sources = {"down": down_ref, "left": left_ref, "proj": proj_ref}
-    outs = {"down": down_out_ref, "left": left_out_ref, "proj": proj_out_ref}
-
-    @pl.when(head == 0)
-    def _():
-        greet(places)
-
-    def streams():
-        for number, (name, lead, rows, order, heads) in enumerate(back_plan(dims)):
-            held, *arrived, send, receive = groups[name]
-            source, tail = sources[name], ()
-            if name == "down":
-                tail = rows + (slice(None),)
-            if name == "left":
-                source = source.at[lead]
-            stream = Halving(places, dims, order, held, arrived, send, receive, lead, tail)
-            yield number, name, lead, stream, source, heads
-
-    def advance(now, last=False):
-        for number, name, lead, stream, source, heads in streams():
-            for step in range(-1, steps):
-                if (heads[step + 1] == now) and (last == (step == steps - 1 and now == HEADS - 1)):
-                    due(now, number, name, lead, stream, source, step)
-
-    def due(now, number, name, lead, stream, source, step):
-        @pl.when(head == now)
-        def _():
-            if step < 0:
-                stream.copy(0, source).start()
-                stream.own_half(source, own_sem.at[number]).start()
-                return
-            stream.copy(step, source).wait()
-            if step == 0:
-                stream.own_half(source, own_sem.at[number]).wait()
-
-            def put(values):
-                outs[name][lead + (...,)] = values.astype(bf16)
-
-            stream.add(step, None, put)
-            if step + 1 < steps:
-                stream.copy(step + 1).start()
-
-    for now in range(HEADS):
-        advance(now)
     patches = q_ref.shape[-1]
     step = patches // 2
     scaling = HD ** (-0.5)
-    mixed_grad = mg_ref[...].astype(f32)
+    mixed_grad = mixed_grad_ref[head].astype(f32)
     offsets = jnp.sum(mixed_grad * mixed_ref[...].astype(f32), axis=0, keepdims=True)
     high, low = split_two(-offsets)
     mg_ext_ref[...] = jnp.concatenate(
@@ -988,6 +1129,7 @@
         if start == 0:
             acc_ref[1] = key_term
             acc_ref[2] = value_term
+            events.at_head(head, 0)
         else:
             acc_ref[1] += key_term
             acc_ref[2] += value_term
@@ -1010,160 +1152,316 @@
         raw = factor_ref[member] * (inner - unit * jnp.mean(inner * unit, axis=0, keepdims=True))
         out_ref[member] = raw.astype(bf16)
     out_ref[2] = acc_ref[2, :HD, :].astype(bf16)
-    advance(HEADS - 1, True)
-
-
-def attend_back(
-    query, heads, mixed_grad, mixed, unit, factor, gains, cosine, sine, down, left, proj
+    events.at_head(head, 1)
+
+
+def core_step(
+    fed, entry_grad, latents, other_x, cotangent, other_c, attended, mixed, proj_weight, vectors,
+    codes, query, heads, unit, factor, gains, cosine, sine, down, left, carries,
 ):
-    patches = query.shape[-1]
+    half, width = other_x.shape
+    patches = 2 * half
     dims = pair_axes()
-    split = (2,) * (len(dims) - 1)
+    turns = patches // TURN_ROWS
     devices = lax.axis_size("img")
-    down = down.reshape((2,) + split + (down.shape[1] // devices, down.shape[2]))
-    proj = proj.reshape((2,) + split + (proj.shape[1] // devices, proj.shape[2]))
-    down_tail = (down.shape[-2] // 2, down.shape[-1])
-    left_tail, proj_tail = left.shape[-2:], proj.shape[-2:]
-    left_lead = left.shape[:2]
+    split = (2,) * len(dims)
+    down = down.reshape(split + (down.shape[1] // devices, down.shape[2]))
+    down_tail = (down.shape[-2] // 4, down.shape[-1])
+    left_tail = left.shape[-2:]
+    proj_tail = (width // devices, width // 2)
+    row_block = lambda t: lax.rem(jnp.minimum(t, turns - 1) + turns // 2, turns)
+    block = pl.BlockSpec((TURN_ROWS, width), lambda t: (row_block(t), 0))
+    own = own_image(TURN_ROWS, width, lambda t: jnp.clip(t - turns // 2, 0, turns // 2 - 1))
+    other = pl.BlockSpec((TURN_ROWS, width), lambda t: (jnp.minimum(t, turns // 2 - 1), 0))
+    head_of = lambda t: jnp.maximum(t - turns, 0)
+    section = lambda member: pl.BlockSpec(
+        (None, None, HDP, patches), lambda t: (member, head_of(t), 0, 0)
+    )
+    single = lambda rows: pl.BlockSpec((None, rows, patches), lambda t: (head_of(t), 0, 0))
+    couple = lambda rows: pl.BlockSpec((2, None, rows, patches), lambda t: (0, head_of(t), 0, 0))
     anywhere = pl.BlockSpec(memory_space=pl.ANY)
-    section = lambda member: pl.BlockSpec(
-        (None, None, HDP, patches), lambda h: (member, h, 0, 0)
-    )
-    single = lambda rows: pl.BlockSpec((None, rows, patches), lambda h: (h, 0, 0))
-    pair = lambda rows: pl.BlockSpec((2, None, rows, patches), lambda h: (0, h, 0, 0))
+    sums = [(4,) + down_tail, (2,) + left_tail, (len(carries),) + left_tail, proj_tail, ()]
+    sums[-1] = split + (codes.shape[0], width + codes.shape[1])
     return pl.pallas_call(
-        functools.partial(attend_back_kernel, dims),
-        grid=(HEADS,),
+        functools.partial(core_kernel, dims),
+        grid=(turns + HEADS,),
         in_specs=[
+            block,
+            block,
+            own,
+            other,
+            own,
+            other,
+            block,
+            whole((width, patches)),
+            whole((width, width)),
+            whole((8, width)),
+            whole(codes.shape),
             single(HDP),
             section(1),
             section(2),
             single(HD),
-            single(HD),
-            pair(HD),
-            pair(1),
+            couple(HD),
+            couple(1),
             whole((2, HD, 1)),
             whole((HD, patches)),
             whole((HD, patches)),
             anywhere,
             anywhere,
+        ]
+        + [whole(carry.shape) for carry in carries],
+        out_specs=[
             anywhere,
+            block,
+            pl.BlockSpec((3, None, HD, patches), lambda t: (0, head_of(t), 0, 0)),
+            whole((2, HD, patches)),
+        ]
+        + [whole(shape) for shape in sums],
+        out_shape=[
+            jax.ShapeDtypeStruct((2, half, width), bf16),
+            jax.ShapeDtypeStruct((patches, width), f32),
+            jax.ShapeDtypeStruct((3, HEADS, HD, patches), bf16),
+            jax.ShapeDtypeStruct((2, HD, patches), f32),
+        ]
+        + [jax.ShapeDtypeStruct(shape, bf16) for shape in sums[:-1]]
+        + [jax.ShapeDtypeStruct(sums[-1], f32)],
+        scratch_shapes=[
+            pltpu.VMEM((patches, width), bf16),
+            pltpu.VMEM((HEADS, HD, patches), bf16),
+            pltpu.VMEM(split + proj_tail, bf16),
+            pltpu.VMEM((turns, TURN_ROWS, width), bf16),
+            pltpu.SemaphoreType.DMA((turns,)),
+            pltpu.SemaphoreType.DMA((turns // 2,)),
+            pltpu.VMEM((HDP, patches), bf16),
+            pltpu.VMEM((3, HDP, patches), f32),
+            pltpu.SemaphoreType.DMA((len(core_plan(dims)),)),
+            pltpu.VMEM(sums[-1], f32),
+        ]
+        + doubling_scratch(dims)
+        + halving_scratch(dims, down_tail, (4,))
+        + halving_scratch(dims, left_tail, (2,))
+        + halving_scratch(dims, proj_tail)
+        + [ref for names in carried_dims(dims) for ref in halving_scratch(names, left_tail)],
+        compiler_params=params_of(collective_id=1, has_side_effects=True),
+        cost_estimate=cost(24 * HEADS * patches * patches * HDP, 70e6, HEADS * patches**2),
+        name="core",
+    )(
+        fed, entry_grad, latents, other_x, cotangent, other_c, attended, mixed, proj_weight,
+        vectors, codes, query, heads, heads, mixed.reshape(HEADS, HD, patches), unit, factor,
+        gains, cosine, sine, down, left, *carries,
+    )
+
+
+BACK_ROWS = 256
+
+
+def tail_plan(dims):
+    return [
+        ("pair", pl.ds(0, 384), order_of(dims, "b0", "b1", "y", "b3", "b2"), (1, 4, 9, 27, 36, 40)),
+        ("pair", pl.ds(384, 384), order_of(dims, "b0", "y", "b1", "b2", "b3"), (1, 4, 18, 27, 35, 40)),
+        ("pair", pl.ds(768, 384), order_of(dims, "b0", "b2", "b1", "b3", "y"), (1, 4, 15, 24, 33, 39)),
+        ("single", None, order_of(dims, "b0", "b2", "b1", "y", "b3"), (2, 5, 25, 35, 45, 51)),
+    ]
+
+
+def back_kernel(
+    dims, pg_ref, w_ref, entry_ref, own_x_ref, other_x_ref, middle_grad_ref, scale_ref,
+    gain_terms_ref,
+    latents_out_ref, sums_out_ref, pair_out_ref, single_out_ref,
+    entry_grad_ref, pair_ref, single_ref, rows_ref, row_send, row_receive, *buffers,
+):
+    step = pl.program_id(0)
+    places = own_places()
+    phases = len(dims)
+    size = phases + 3
+    *buffers, sums_ref, send, receive = buffers
+    streams = []
+    for place, (name, columns, order, when) in enumerate(tail_plan(dims)):
+        held, *arrived, s, r = buffers[place * size : (place + 1) * size]
+        tail = () if columns is None else (slice(None), columns)
+        stream = Halving(places, dims, order, held, arrived, s, r, (), tail)
+        if name == "pair":
+            streams.append((stream, pair_ref, when, pair_out_ref.at[:, columns]))
+        else:
+            streams.append((stream, single_ref, when, single_out_ref))
+    doubling = Doubling(places, dims, doubling_order(dims), sums_ref, send, receive)
+    width = entry_grad_ref.shape[0]
+    half = width // 2
+    blocks = 2 ** (phases - 1)
+    rows = width // blocks
+
+    @pl.when(step == 0)
+    def _():
+        entry_grad_ref[...] = jnp.zeros_like(entry_grad_ref)
+        greet(places)
+
+    @pl.when(step < 3)
+    def _():
+        grad = dot(entry_ref[...], pg_ref[...], 0, 1)
+
+        def spot(block):
+            return tuple(block // 2**bit % 2 for bit in reversed(range(phases - 1)))
+
+        def part(block):
+            return grad[block * rows : (block + 1) * rows, :]
+
+        @pl.when(step < 2)
+        def _():
+            for block in range(blocks):
+                pair_ref[(step,) + spot(block)] = part(block).astype(bf16)
+
+        @pl.when(step == 2)
+        def _():
+            for block in range(blocks):
+                single_ref[(0,) + spot(block)] = part(block)[:, :half].astype(bf16)
+                single_ref[(1,) + spot(block)] = part(block)[:, half:].astype(bf16)
+
+    @pl.when((step >= 3) & (step < 6))
+    def _():
+        entry_grad_ref[...] += dot(w_ref[...], pg_ref[...], 1, 0)
+
+    band = places["y"]
+
+    def away(number):
+        return pltpu.make_async_remote_copy(
+            src_ref=rows_ref.at[number],
+            dst_ref=latents_out_ref.at[band, pl.ds(number * BACK_ROWS, BACK_ROWS)],
+            send_sem=row_send.at[number],
+            recv_sem=row_receive.at[number],
+            device_id=partner_id("y", places),
+            device_id_type=MESH_ID,
+        )
+
+    def stay(number):
+        return pltpu.make_async_copy(
+            rows_ref.at[number + 2],
+            latents_out_ref.at[band, pl.ds(number * BACK_ROWS, BACK_ROWS)],
+            row_send.at[number + 2],
+        )
+
+    for number in range(4):
+        block = (number + 2) % 4
+
+        @pl.when(step == 6 + number)
+        def _():
+            entry_grad = entry_grad_ref[:, block * BACK_ROWS : (block + 1) * BACK_ROWS].T
+            source = (other_x_ref if number < 2 else own_x_ref)[...].astype(f32)
+            factor = lax.rsqrt(jnp.mean(source * source, axis=1, keepdims=True) + epsilon)
+            normed = source * factor
+            inner = entry_grad * (1.0 + scale_ref[...])
+            grads = middle_grad_ref[...] + factor * (
+                inner - normed * jnp.mean(inner * normed, axis=1, keepdims=True)
+            )
+            rows_ref[number] = grads.astype(bf16)
+            add = lambda v: jnp.sum(v, axis=0, keepdims=True)
+            sums = jnp.concatenate([add(entry_grad), add(entry_grad * normed)], axis=0)
+            if number == 0:
+                sums_ref[doubling.own() + (slice(0, 2),)] = sums
+                sums_ref[doubling.own() + (slice(2, 4),)] = gain_terms_ref[...]
+            else:
+                sums_ref[doubling.own() + (slice(0, 2),)] += sums
+            if number < 2:
+                away(number).start()
+            else:
+                stay(number - 2).start()
+
+    def due(now):
+        for stream, source, when, out in streams:
+            for phase in range(-1, phases):
+                if when[phase + 1] != now:
+                    continue
+                if phase >= 0:
+                    stream.copy(phase, source).wait()
+
+                    def put(values):
+                        out[...] = values.astype(bf16)
+
+                    stream.add(phase, source if phase == 0 else None, put)
+                if phase + 1 < phases:
+                    stream.copy(phase + 1, source).start()
+
+    for now in range(1, 10):
+
+        @pl.when(step == now)
+        def _():
+            if now == 9:
+                doubling.copy(0).start()
+            due(now)
+            if now == 9:
+                last = max(point for plan in tail_plan(dims) for point in plan[3])
+                for later in range(10, last + 1):
+                    due(later)
+                    turn, odd = divmod(later - 12, 3)
+                    if odd == 0 and 0 <= turn < phases:
+                        doubling.copy(turn).wait()
+                        if turn + 1 < phases:
+                            doubling.copy(turn + 1).start()
+                sums_out_ref[...] = sums_ref[...]
+                for number in range(2):
+                    away(number).wait()
+                    stay(number).wait()
+
+
+def back_step(
+    projected_grad, qkv_weight, entry, latents, other_x, middle_grad, scale, gain_rows
+):
+    patches, width = entry.shape
+    dims = pair_axes()
+    rows = width // lax.axis_size("img")
+    sections = (0, 2, 1, 0, 1, 2)
+
+    def section_of(step):
+        place = jnp.int32(sections[-1])
+        for number, section in enumerate(sections[:-1]):
+            place = jnp.where(step == number, section, place)
+        return place
+
+    weight_section = lambda t: jnp.where(t < 4, 0, jnp.minimum(t - 3, 2))
+    row_block = lambda t: lax.rem(jnp.clip(t - 6, 0, 3) + 2, 4)
+    block = pl.BlockSpec((BACK_ROWS, width), lambda t: (row_block(t), 0))
+    own = own_image(BACK_ROWS, width, lambda t: jnp.clip(t - 8, 0, 1))
+    other = pl.BlockSpec((BACK_ROWS, width), lambda t: (jnp.clip(t - 6, 0, 1), 0))
+    tails = [(rows, 384)] * 3 + [(rows, width // 2)]
+    sums = [(rows, width), (rows, width // 2)]
+    wide = (2,) * len(dims)
+    scratch = [
+        pltpu.VMEM((width, patches), f32),
+        pltpu.VMEM(wide + (rows, width), bf16),
+        pltpu.VMEM(wide + (rows, width // 2), bf16),
+        pltpu.VMEM((4, BACK_ROWS, width), bf16),
+        pltpu.SemaphoreType.DMA((4,)),
+        pltpu.SemaphoreType.DMA((2,)),
+    ]
+    for tail in tails:
+        scratch += halving_scratch(dims, tail)
+    return pl.pallas_call(
+        functools.partial(back_kernel, dims),
+        grid=(10,),
+        in_specs=[
+            pl.BlockSpec((None, width, patches), lambda t: (section_of(t), 0, 0)),
+            pl.BlockSpec((width, width), lambda t: (0, weight_section(t))),
+            whole((patches, width)),
+            own,
+            other,
+            block,
+            whole((1, width)),
+            whole((2, width)),
         ],
         out_specs=[
-            pl.BlockSpec((3, None, HD, patches), lambda h: (0, h, 0, 0)),
-            pl.BlockSpec((2, HD, patches), lambda h: (0, 0, 0)),
-            whole((2,) + down_tail),
-            whole(left_lead + left_tail),
-            whole(proj_tail),
-        ],
+            pl.BlockSpec(memory_space=pl.ANY),
+            whole(wide + (4, width)),
+        ]
+        + [whole(shape) for shape in sums],
         out_shape=[
-            jax.ShapeDtypeStruct((3, HEADS, HD, patches), bf16),
-            jax.ShapeDtypeStruct((2, HD, patches), f32),
-            jax.ShapeDtypeStruct((2,) + down_tail, bf16),
-            jax.ShapeDtypeStruct(left_lead + left_tail, bf16),
-            jax.ShapeDtypeStruct(proj_tail, bf16),
-        ],
-        scratch_shapes=[
-            pltpu.VMEM((HDP, patches), bf16),
-            pltpu.VMEM((3, HDP, patches), f32),
-            pltpu.SemaphoreType.DMA((len(back_plan(dims)),)),
+            jax.ShapeDtypeStruct((2, patches // 2, width), bf16),
+            jax.ShapeDtypeStruct(wide + (4, width), f32),
         ]
-        + halving_scratch(dims, down_tail, (2,))
-        + halving_scratch(dims, left_tail, left_lead)
-        + halving_scratch(dims, proj_tail),
-        compiler_params=params_of(collective_id=1, has_side_effects=True),
-        cost_estimate=cost(20 * HEADS * patches * patches * HDP, 32e6, HEADS * patches**2),
-        name="attend_back",
-    )(
-        query, heads, heads, mixed_grad, mixed, unit, factor, gains, cosine, sine, down, left, proj
-    )
-
-
-def back_kernel(pg_ref, w_ref, entry_ref, grad_ref, entry_grad_ref):
-    section = pl.program_id(0)
-    grad_ref[...] = dot(entry_ref[...], pg_ref[...], 0, 1).astype(bf16)
-    term = dot(w_ref[...], pg_ref[...], 1, 0)
-
-    @pl.when(section == 0)
-    def _():
-        entry_grad_ref[...] = term
-
-    @pl.when(section > 0)
-    def _():
-        entry_grad_ref[...] += term
-
-
-def back_step(projected_grad, qkv_weight, entry):
-    patches, width = entry.shape
-    return pl.pallas_call(
-        back_kernel,
-        grid=(3,),
-        in_specs=[
-            pl.BlockSpec((None, width, patches), lambda s: (s, 0, 0)),
-            pl.BlockSpec((width, width), lambda s: (0, s)),
-            whole((patches, width)),
-        ],
-        out_specs=[
-            pl.BlockSpec((width, width), lambda s: (0, s)),
-            pl.BlockSpec((width, patches), lambda s: (0, 0)),
-        ],
-        out_shape=[
-            jax.ShapeDtypeStruct((width, 3 * width), bf16),
-            jax.ShapeDtypeStruct((width, patches), f32),
-        ],
-        compiler_params=params_of(),
-        cost_estimate=cost(12 * patches * width * width, 32e6),
+        + [jax.ShapeDtypeStruct(shape, bf16) for shape in sums],
+        scratch_shapes=scratch + [pltpu.VMEM(wide + (4, width), f32)] + doubling_scratch(dims),
+        compiler_params=params_of(collective_id=2, has_side_effects=True),
+        cost_estimate=cost(12 * patches * width * width, 40e6),
         name="back",
-    )(projected_grad, qkv_weight, entry)
-
-
-def last_kernel(entry_grad_ref, x_ref, middle_grad_ref, scale_ref, out_ref, sums_ref):
-    step = pl.program_id(0)
-    entry_grad = entry_grad_ref[...].T
-    source = x_ref[...].astype(f32)
-    factor = lax.rsqrt(jnp.mean(source * source, axis=1, keepdims=True) + epsilon)
-    normed = source * factor
-    inner = entry_grad * (1.0 + scale_ref[...])
-    grads = middle_grad_ref[...] + factor * (
-        inner - normed * jnp.mean(inner * normed, axis=1, keepdims=True)
-    )
-    out_ref[...] = grads.astype(bf16)
-    add = lambda v: jnp.sum(v, axis=0, keepdims=True)
-    sums = jnp.concatenate(
-        [add(entry_grad), add(entry_grad * normed), jnp.zeros((6, source.shape[1]), f32)], axis=0
-    )
-
-    @pl.when(step == 0)
-    def _():
-        sums_ref[...] = sums
-
-    @pl.when(step > 0)
-    def _():
-        sums_ref[...] += sums
-
-
-def last_step(entry_grad, x, middle_grad, scale):
-    patches, width = x.shape
-    rows = 256
-    block = pl.BlockSpec((rows, width), lambda t: (t, 0))
-    return pl.pallas_call(
-        last_kernel,
-        grid=(patches // rows,),
-        in_specs=[
-            pl.BlockSpec((width, rows), lambda t: (0, t)),
-            block,
-            block,
-            whole((1, width)),
-        ],
-        out_specs=[block, pl.BlockSpec((8, width), lambda t: (0, 0))],
-        out_shape=[
-            jax.ShapeDtypeStruct((patches, width), bf16),
-            jax.ShapeDtypeStruct((8, width), f32),
-        ],
-        compiler_params=params_of(),
-        cost_estimate=cost(20 * patches * width, 17e6),
-        name="last",
-    )(entry_grad, x, middle_grad, scale)
+    )(projected_grad, qkv_weight, entry, latents, other_x, middle_grad, scale, gain_rows)
 
 
 def pick(values, index):
@@ -1193,35 +1491,14 @@
     bands = lax.axis_size("band")
     img_index = lax.axis_index("img")
     band_index = lax.axis_index("band")
-    half = latents.shape[1]
-
-    def exchange(own):
-        parts = [pick(own, band_index)]
-        for shift in range(1, bands):
-            pairs = [(i, (i + shift) % bands) for i in range(bands)]
-            away = pick(own, lax.rem(band_index + shift, bands))
-            parts.append(lax.ppermute(away, "band", pairs))
-        return jnp.concatenate(parts, axis=0)
-
-    def give_back(values):
-        back = [values[:half]]
-        for shift in range(1, bands):
-            pairs = [(i, (i - shift) % bands) for i in range(bands)]
-            back.append(
-                lax.ppermute(values[shift * half : (shift + 1) * half], "band", pairs)
-            )
-        stacked = jnp.stack(back)
-        order = lax.rem(jnp.arange(bands) - band_index + bands, bands)
-        return jnp.take(stacked, order, axis=0)
-
-    x = exchange(latents)
-    c = exchange(cotangent)
+
+    def from_other(values):
+        return lax.ppermute(values, "band", [(0, 1), (1, 0)])
+
+    other_x = from_other(pick(latents, 1 - band_index))
+    other_c = from_other(pick(cotangent, 1 - band_index))
     places = jnp.stack([row_pos, col_pos], axis=1)
-    place_parts = [places]
-    for shift in range(1, bands):
-        pairs = [(i, (i + shift) % bands) for i in range(bands)]
-        place_parts.append(lax.ppermute(places, "band", pairs))
-    places = jnp.concatenate(place_parts, axis=0)
+    places = jnp.concatenate([places, from_other(places)], axis=0)
 
     quarter = HD // 4
     frequency = jnp.exp(-math.log(10000.0) * jnp.arange(quarter, dtype=f32) / quarter)
@@ -1251,47 +1528,41 @@
     gains = jnp.stack([query_gain, key_gain])[:, :, None]
     scaled_gains = gains * jnp.array([scaling * LOG2E, 1.0], f32)[:, None, None]
     entry_one, heads, unit, factor = front(
-        x, scale_one, shift_one, qkv_weight, scaled_gains, cosine, sine
+        latents, other_x, scale_one, shift_one, qkv_weight, scaled_gains, cosine, sine
     )
     mixed, query = attend(heads)
-    patches = x.shape[0]
-    mixed_flat = mixed.reshape(width, patches)
-    attended, entry_two, fed_grad = middle_step(mixed_flat, proj_weight, x, c, vectors)
-    fed, entry_two_grad, grad_down, gateup_done, gateup_left = mlp(
+    mixed = mixed.reshape(width, -1)
+    attended, entry_two, fed_grad = middle_step(
+        mixed, proj_weight, latents, other_x, cotangent, other_c, vectors
+    )
+    fed, entry_two_grad, grad_down, gateup_done, gateup_left, *carries = mlp(
         entry_two, fed_grad, gateup_weight, down_weight
     )
-    result, middle_grad, mixed_grad, grad_proj, sums_two = turn_step(
-        fed, entry_two_grad, x, attended, c, mixed_flat, proj_weight, vectors
-    )
-    projected_grad, gain_terms, sum_down, gateup_rest, sum_proj = attend_back(
-        query, heads, mixed_grad.reshape(HEADS, HD, patches), mixed, unit, factor, gains,
-        cosine, sine, grad_down, gateup_left, grad_proj,
-    )
-    grad_qkv, entry_one_grad = back_step(
-        projected_grad.reshape(3, width, patches), qkv_weight, entry_one
-    )
-    grad_latents, sums_one = last_step(entry_one_grad, x, middle_grad, scale_one)
-
-    everything = ("img", "band")
-    own_grad = jnp.concatenate(
-        [
-            sums_one[0],
-            sums_one[1],
-            sums_two[0],
-            sums_two[1],
-            sums_two[2],
-            sums_two[3],
-            jnp.sum(gain_terms, axis=2).reshape(-1),
-        ]
+    codes = jnp.stack([own_label, own_group], axis=0).astype(f32)
+    codes = jnp.pad(codes, ((0, 2), (0, 127)))
+    (
+        result, middle_grad, projected_grad, gain_terms,
+        sum_down, gateup_last, gateup_carried, sum_proj, modes_early,
+    ) = core_step(
+        fed, entry_two_grad, latents, other_x, cotangent, other_c, attended, mixed, proj_weight,
+        vectors, codes, query, heads, unit, factor, gains, cosine, sine, grad_down, gateup_left,
+        carries,
+    )
+    gain_rows = jnp.pad(jnp.sum(gain_terms, axis=2), ((0, 0), (0, width - HD)))
+    grad_latents, modes_late, qkv_pair, qkv_single = back_step(
+        projected_grad.reshape(3, width, -1), qkv_weight, entry_one, latents, other_x, middle_grad,
+        scale_one, gain_rows,
+    )
+    modes_early = modes_early.reshape(-1, 4, modes_early.shape[-1])
+    modes_late = modes_late.reshape(-1, 4, width)
+    modulation_all = jnp.concatenate(
+        [modes_late[:, 0], modes_late[:, 1]] + [modes_early[:, place, :width] for place in range(4)],
+        axis=1,
     ).astype(bf16)
-    gathered = lax.all_gather(own_grad[None], everything, axis=0, tiled=True)
-    codes = lax.all_gather(
-        jnp.stack([group_ids, labels], axis=1), "img", axis=0, tiled=True
-    )
-    modulation_all = gathered[:, : 6 * width]
-    gain_sums = jnp.sum(gathered[:, 6 * width :].astype(f32), axis=0)
-    sum_query_gain, sum_key_gain = gain_sums[:HD], gain_sums[HD:]
-    features_all, before_all, condition_all = condition_of(codes[:, 0], codes[:, 1])
+    gain_sums = jnp.sum(modes_late[:, 2:, :HD], axis=0)
+    sum_query_gain, sum_key_gain = gain_sums[0], gain_sums[1]
+    codes = modes_early[:, :2, width].astype(jnp.int32).T
+    features_all, before_all, condition_all = condition_of(codes[1], codes[0])
     before_grad = lax.dot_general(
         modulation_all, ada_weight, (((1,), (1,)), ((), ())), preferred_element_type=f32
     ) * silu_slope(before_all)
@@ -1305,19 +1576,23 @@
     features_part = lax.dynamic_slice_in_dim(features_all, img_index * time_rows, time_rows, 1)
     before_part = lax.dynamic_slice_in_dim(before_grad, band_index * time_cols, time_cols, 1)
     sum_time = jnp.dot(features_part.astype(f32).T, before_part, precision=highest)
-    class_all = (codes[:, 1][:, None] == jnp.arange(NCLASS, dtype=jnp.int32)[None, :]).astype(f32)
+    class_all = (codes[0][:, None] == jnp.arange(NCLASS, dtype=jnp.int32)[None, :]).astype(f32)
     sum_class = jnp.dot(class_all.T, before_grad, precision=highest)
     sum_bias = jnp.sum(modulation_all.astype(f32), axis=0)
 
     sum_down = sum_down.reshape(-1, sum_down.shape[-1]).astype(f32)
     sum_proj = sum_proj.astype(f32)
-    gateup = jnp.concatenate([gateup_done, gateup_rest], axis=0)
+    gateup_carried = gateup_carried.reshape((len(CARRIED), 2) + gateup_carried.shape[1:])
+    gateup = jnp.concatenate([gateup_done, gateup_carried, gateup_last[None]], axis=0)
     sum_gateup = jnp.transpose(gateup, (2, 0, 1, 3)).reshape(gateup.shape[2], -1).astype(f32)
-    part_qkv = lax.psum_scatter(grad_qkv, "img", scatter_dimension=0, tiled=True)
-    sum_qkv = lax.psum_scatter(part_qkv, "band", scatter_dimension=1, tiled=True).astype(f32)
+    sum_qkv = jnp.where(
+        band_index == 0,
+        jnp.concatenate([qkv_pair, qkv_single], axis=1),
+        jnp.concatenate([qkv_single, qkv_pair], axis=1),
+    ).astype(f32)
     return (
-        give_back(result),
-        give_back(grad_latents),
+        result,
+        grad_latents,
         sum_time,
         sum_class,
         sum_ada,
@@ -1332,8 +1607,7 @@
 
 
 def per_device(latents, *others):
-    devices = lax.axis_size("img")
-    if latents.shape[0] == lax.axis_size("band") == 2 and devices >= 8 and devices & (devices - 1) == 0:
+    if latents.shape[0] == lax.axis_size("band") == 2 and lax.axis_size("img") == 16:
         return per_device_whole(latents, *others)
     return per_device_banded(latents, *others)
 

time: 556 us -> 419 us (0.75)
  blocking collectives: 134 us -> 0 us
  Pallas kernels: 307 us -> 340 us
  between operations: 17.5 us -> 4.16 us
  other arithmetic: 23.5 us -> 12.7 us
  local copies, waits for them, and re-layouts: 28.7 us -> 21.9 us
    all_gather x2 -> x0, blocking collectives: 134 us -> none  [the longest x1 115 us: per_device_whole(): gathered = lax.all_gather(own_grad[None], everything, axis=0, tiled=True)]
    pallas_call x5 -> x3, Pallas kernels: 164 us -> 214 us  [the longest x1 95.9 us: core_step(): pl.pallas_call(functools.partial(core_kernel, dims), grid=(turns + HEADS,...]
    pallas_call x1, Pallas kernels: 113 us -> 95.7 us  [mlp(): pl.pallas_call(functools.partial(mlp_kernel, dims), grid=(tiles,), in_spe...]
    gather x2 -> x0, local copies, waits for them, and re-layouts: 6.27 us -> none  [give_back(): return jnp.take(stacked, order, axis=0)]
    concatenate x2 -> x0, other arithmetic: 5.71 us -> none  [exchange(): return jnp.concatenate(parts, axis=0)]
  transfers between devices with their start and end apart: 7 -> 3, of which waited for: 2 -> 1; matrix products, arithmetic and copies ran while one was open for 13% -> 5% of each run, Pallas kernels for 9% -> 11%
where the time goes in v3:
time: 419 us; the launch traced here: 414 us
  Pallas kernels  340 us (81%)
  matrix products  25.4 us (6%)
  local copies, waits for them, and re-layouts  21.9 us (5%)
  other arithmetic  12.7 us (3%)
  starting transfers between devices  4.99 us (1%)
  waiting for transfers between devices  4.65 us (1%)
    pallas_call x1, Pallas kernels, core_step(): pl.pallas_call(functools.partial(core_kernel, dims), grid=(turns + HEADS,...  95.9 us
    pallas_call x1, Pallas kernels, mlp(): pl.pallas_call(functools.partial(mlp_kernel, dims), grid=(tiles,), in_spe...  95.7 us
    pallas_call x1, Pallas kernels, back_step(): pl.pallas_call(functools.partial(back_kernel, dims), grid=(10,), in_specs...  94.6 us
    pallas_call x1, Pallas kernels, front(): pl.pallas_call(front_kernel, grid=(3,), in_specs=[own_image(half, width,...  23.6 us
    pallas_call x1, Pallas kernels, attend(): pl.pallas_call(lambda q, k, v, mixed, qext: attend_kernel(q, k, v, mixed,...  20.4 us
    dot_general x1, matrix products, per_device_whole(): lax.dot_general(modulation_all, ada_weight, (((1,), (1,)), ((), ())), pre...  10.3 us
    pallas_call x1, Pallas kernels, middle_step(): pl.pallas_call(middle_kernel, grid=(patches // rows,), in_specs=[pl.Block...  10.3 us
  transfers between devices with their start and end apart: 3, of which 1 were waited for; matrix products, arithmetic and copies ran while one was open for 5% of the time, Pallas kernels for 11%

profile of v3, /device:TPU:0, one launch (start us, length us, event | category | flops | bytes accessed | tf_op | source)
XLA Modules:
  0.0 414.2 jit_solution(17387875880716558177)
XLA Ops:
  0.7 0.9 pad_add_fusion
  1.5 3.0 collective-permute-start.1
  4.5 2.4 dynamic-slice_bitcast_fusion.1
  7.0 1.2 dynamic-slice_bitcast_fusion
  8.2 2.0 collective-permute-start.2
  10.1 0.6 dynamic_slice.28
  12.7 0.6 dynamic_slice.27
  13.3 1.2 fusion.30
  15.5 0.8 fusion.27
  16.4 7.7 %convolution_reduce_fusion = f32[6912]{0:T(1024)S(1)} fusion(bf16[1152,1]{0,1:T(2,128)(2,1)S(1)} %reshape.308, bf16[1152,6912]{1,0:T(8,128)(2,1)} %param.27), kind=kOutput, calls=%fused_computation.5 | convolution fusion | flops 15925248 | bytes 15955200 | tf_op jit(solution)/shard_map/dot_general | solution.py:1522
  24.2 0.6 fusion.37
  25.1 1.3 add_convert_fusion.1
  26.4 0.7 maximum_multiply_fusion.gains_ref
  27.1 0.7 copy.52.gains_ref
  27.9 0.6 pad.8.codes_ref
  28.5 0.7 concatenate.55.vectors_ref
  29.2 0.8 multiply_sine_fusion
  30.0 0.8 pad_maximum_fusion.cos_ref
  30.7 0.8 pad_maximum_fusion.1.sin_ref
  31.5 4.6 %collective-permute-done.other_ref.other_x_ref = bf16[512,1152]{1,0:T(8,128)(2,1)} collective-permute-done((bf16[512,1152]{1,0:T(8,128)(2,1)}, bf16[512,1152]{1,0:T(8,128)(2,1)}, u32[]{:S(2)}, u32[]{:S(2)}) %collective-permute-start) | collective-permute-done | bytes 1179680 | tf_op jit(solution)/shard_map/ppermute | solution.py:1496
  36.1 23.6 %front.1 = (bf16[1024,1152]{1,0:T(8,128)(2,1)}, bf16[3,16,80,1024]{3,2,1,0:T(8,128)(2,1)}, bf16[2,16,72,1024]{3,2,1,0:T(8,128)(2,1)}, f32[2,16,1,1024]{3,2,1,0:T(1,128)}) custom-call(bf16[2,512,1152]{2,1,0:T(8,128)(2,1)} %own_x_ref.5, bf16[512,1152]{1,0:T(8,128)(2,1)} %collective-permute-done.other_ref.other_x_ref, f32[1,1152]{1,0:T(1,128)} %get-tuple-element.96.scale_ref, ...), custom_call_target="tpu_custom_call" | custom-call | flops 8153726976 | bytes 24000000 | tf_op jit(solution)/shard_map/front/pallas_call | solution.py:607
  59.7 20.4 %attend.1 = (bf16[16,72,1024]{2,1,0:T(8,128)(2,1)}, bf16[16,80,1024]{2,1,0:T(8,128)(2,1)}) custom-call(bf16[3,16,80,1024]{3,2,1,0:T(8,128)(2,1)} %get-tuple-element.43.q.k.v.k_ref.v_ref, bf16[3,16,80,1024]{3,2,1,0:T(8,128)(2,1)} %get-tuple-element.43.q.k.v.k_ref.v_ref, bf16[3,16,80,1024]{3,2,1,0:T(8,128)(2,1)} %get-tuple-element.43.q.k.v.k_ref.v_ref), custom_call_target="tpu_custom_call" | custom-call | flops 10737418240 | bytes 14000000 | tf_op jit(solution)/shard_map/attend/pallas_call | solution.py:660
  80.1 1.0 copy-done.4
  81.2 10.3 %middle.1 = (bf16[1024,1152]{1,0:T(8,128)(2,1)}, bf16[1024,1152]{1,0:T(8,128)(2,1)}, bf16[1024,1152]{1,0:T(8,128)(2,1)}) custom-call(bf16[1152,1024]{1,0:T(8,128)(2,1)} %bitcast.108, bf16[1152,1152]{1,0:T(8,128)(2,1)} %w_ref.6, bf16[2,512,1152]{2,1,0:T(8,128)(2,1)} %own_x_ref.5, bf16[512,1152]{1,0:T(8,128)(2,1)} %collective-permute-done.other_ref.other_x_ref, ...), custom_call_target="tpu_custom_call" | custom-call | flops 2717908992 | bytes 17000000 | tf_op jit(solution)/shard_map/middle/pallas_call | solution.py:703
  91.4 95.7 %mlp.1 = (f32[1024,1152]{1,0:T(8,128)}, f32[1024,1152]{1,0:T(8,128)}, bf16[2,3072,576]{2,1,0:T(8,128)(2,1)}, bf16[3,2,72,256]{3,2,1,0:T(8,128)(2,1)}, bf16[2,2,2...) custom-call(bf16[1024,1152]{1,0:T(8,128)(2,1)} %get-tuple-element.45, ...), custom_call_target="tpu_custom_call" | custom-call | flops 65229815808 | bytes 56000000 | tf_op jit(solution)/shard_map/mlp/pallas_call | solution.py:849
  187.1 95.9 %core.1 = (bf16[2,512,1152]{2,1,0:T(8,128)(2,1)}, f32[1024,1152]{1,0:T(8,128)}, bf16[3,16,72,1024]{3,2,1,0:T(8,128)(2,1)}, f32[2,72,1024]{2,1,0:T(8,128)}, bf16[...) custom-call(f32[1024,1152]{1,0:T(8,128)} %get-tuple-element.47.fed_r, ...), custom_call_target="tpu_custom_call" | custom-call | flops 32212254720 | bytes 70000000 | tf_op jit(solution)/shard_map/core/pallas_call | solution.py:1185
  283.1 0.9 slice.133
  284.0 1.2 copy.62
  285.2 1.2 reduce_sum.27
  286.4 0.6 pad.9.gain_terms_ref
  287.0 94.6 %back.1 = (bf16[2,512,1152]{2,1,0:T(8,128)(2,1)}, f32[2,2,2,2,2,4,1152]{6,5,4,3,2,1,0:T(4,128)}, bf16[72,1152]{1,0:T(8,128)(2,1)}, bf16[72,576]{1,0:T(8,128)(2,1)}) custom-call(bf16[3,1152,1024]{2,1,0:T(8,128)(2,1)} %bitcast.125, bf16[1152,3456]{1,0:T(8,128)(2,1)} %w_ref.7, bf16[1024,1152]{1,0:T(8,128)(2,1)} %get-tuple-element.61.entry_ref, ...), custom_call_target="tpu_custom_call" | custom-call | flops 16307453952 | bytes 40000000 | tf_op jit(solution)/shard_map/back/pallas_call | solution.py:1437
  381.6 1.1 copy.63
  382.7 0.9 slice_reduce_fusion
  383.7 0.5 copy.56
  384.2 1.6 reshape.285
  385.8 2.6 gather_fusion
  388.8 0.7 convert_reduce_fusion
  389.9 10.3 %convolution_multiply_fusion = f32[32,1152]{1,0:T(8,128)S(1)} fusion(bf16[32,6912]{1,0:T(8,128)(2,1)S(1)} %fusion.11, bf16[1152,6912]{1,0:T(8,128)(2,1)} %param.27, f32[32,1152]{1,0:T(8,128)S(1)} %get-tuple-element.106), kind=kOutput, calls=%fused_computation.2 | convolution fusion | flops 509902848 | bytes 16662528 | tf_op jit(solution)/shard_map/dot_general | solution.py:1566
  400.2 0.5 slice_bitcast_fusion.10
  400.7 0.8 bitcast_convert_fusion
  401.6 0.7 convert_element_type.86
  402.3 4.4 %fusion.8 = f32[1000,1152]{1,0:T(8,128)} fusion(f32[32,1152]{1,0:T(8,128)S(1)} %convolution_multiply_fusion, s32[32]{0:T(128)S(1)} %get-tuple-element.101), kind=kOutput, calls=%fused_computation.28 | convolution fusion | flops 442400000 | bytes 4755584 | tf_op jit(solution)/shard_map/dot_general | solution.py:1580
  406.7 0.9 fusion.9
  407.6 0.9 fusion.5
  408.5 1.3 fusion.6
  409.9 1.4 copy.71
  411.3 1.1 copy-done.3
  412.4 1.4 copy.72
  (79 shorter events, 1.7 us)
Async XLA Ops:
  0.6 14.7 %copy-start = (bf16[256,1152]{1,0:T(8,128)(2,1)S(1)}, bf16[256,1152]{1,0:T(8,128)(2,1)}, u32[]{:S(2)}) copy-start(bf16[256,1152]{1,0:T(8,128)(2,1)} %param.25) | copy-start | bytes 1769476
  0.7 6.3 %copy-start.1 = (bf16[2,512,1152]{2,1,0:T(8,128)(2,1)S(1)}, bf16[2,512,1152]{2,1,0:T(8,128)(2,1)}, u32[]{:S(2)}) copy-start(bf16[2,512,1152]{2,1,0:T(8,128)(2,1)} %own_c_ref.3) | copy-start | bytes 7077892
  1.5 27.6 %collective-permute-start.1 = (s32[512,2]{0,1:T(2,128)S(1)}, s32[512,2]{0,1:T(2,128)S(1)}, u32[]{:S(2)}, u32[]{:S(2)}) collective-permute-start(s32[512,2]{0,1:T(2,128)S(1)} %pad_add_fusion), channel_id=1, source_target_pairs={{0,1},{1,0},{2,3},{3,2},{4,5},{5,4},{6,7},{7,6},{8,9},{9,8},{10,11... | collective-permute-start | bytes 12296 | tf_op jit(solution)/shard_map/ppermute | solution.py:1496
  4.5 5.6 %copy-start.18 = (s32[2]{0:T(128)S(1)}, s32[2]{0:T(128)}, u32[]{:S(2)}) copy-start(s32[2]{0:T(128)} %param.20) | copy-start | bytes 28
  4.5 8.2 %copy-start.19 = (s32[2]{0:T(128)S(1)}, s32[2]{0:T(128)}, u32[]{:S(2)}) copy-start(s32[2]{0:T(128)} %param.21) | copy-start | bytes 28
  4.5 8.8 %copy-start.20 = (f32[8]{0:T(128)S(1)}, f32[8]{0:T(128)}, u32[]{:S(2)}) copy-start(f32[8]{0:T(128)} %param.22) | copy-start | bytes 100
  6.9 29.2 %collective-permute-start = (bf16[512,1152]{1,0:T(8,128)(2,1)}, bf16[512,1152]{1,0:T(8,128)(2,1)}, u32[]{:S(2)}, u32[]{:S(2)}) collective-permute-start(bf16[512,1152]{1,0:T(8,128)(2,1)} %dynamic-slice_bitcast_fusion.1), channel_id=1, source_target_pairs={{0,1},{1,0},{2,3},{3,2},{4,5},{5,4},{6,7},{7,6},{8,9},{9,8},{10,11... | collective-permute-start | bytes 3538952 | tf_op jit(solution)/shard_map/ppermute | solution.py:1496
  8.2 72.0 %collective-permute-start.2 = (bf16[512,1152]{1,0:T(8,128)(2,1)}, bf16[512,1152]{1,0:T(8,128)(2,1)S(1)}, u32[]{:S(2)}, u32[]{:S(2)}) collective-permute-start(bf16[512,1152]{1,0:T(8,128)(2,1)} %dynamic-slice_bitcast_fusion), channel_id=1, source_target_pairs={{0,1},{1,0},{2,3},{3,2},{4,5},{5,4},{6,7},{7,6},{8,9},{9,8},{10,11... | collective-permute-start | bytes 3538952 | tf_op jit(solution)/shard_map/ppermute | solution.py:1496
  16.3 7.8 %copy-start.12 = (f32[6912]{0:T(1024)S(1)}, f32[6912]{0:T(1024)}, u32[]{:S(2)}) copy-start(f32[6912]{0:T(1024)} %param.28) | copy-start | bytes 82948
  16.3 8.5 %copy-start.16 = (f32[72]{0:T(128)S(1)}, f32[72]{0:T(128)}, u32[]{:S(2)}) copy-start(f32[72]{0:T(128)} %param.30) | copy-start | bytes 868
  16.4 8.6 %copy-start.15 = (f32[72]{0:T(128)S(1)}, f32[72]{0:T(128)}, u32[]{:S(2)}) copy-start(f32[72]{0:T(128)} %param.31) | copy-start | bytes 868
  16.4 10.0 %copy-start.17 = (f32[2]{0:T(128)S(1)}, f32[2]{0:T(128)}, u32[]{:S(2)}) copy-start(f32[2]{0:T(128)} %constant.104.clone) | copy-start | bytes 28
  16.4 12.8 %copy-start.13 = (s32[512]{0:T(512)S(1)}, s32[512]{0:T(512)}, u32[]{:S(2)}) copy-start(s32[512]{0:T(512)} %param.24) | copy-start | bytes 6148
  16.4 12.8 %copy-start.14 = (s32[512]{0:T(512)S(1)}, s32[512]{0:T(512)}, u32[]{:S(2)}) copy-start(s32[512]{0:T(512)} %param.23) | copy-start | bytes 6148
  80.1 1.0 copy-start.4
  287.0 96.6 %copy-start.6 = (bf16[3,2,72,256]{3,2,1,0:T(8,128)(2,1)S(1)}, bf16[3,2,72,256]{3,2,1,0:T(8,128)(2,1)}, u32[]{:S(2)}) copy-start(bf16[3,2,72,256]{3,2,1,0:T(8,128)(2,1)} %get-tuple-element.70) | copy-start | bytes 663556
  287.0 96.6 %copy-start.8 = (bf16[4,72,256]{2,1,0:T(8,128)(2,1)S(1)}, bf16[4,72,256]{2,1,0:T(8,128)(2,1)}, u32[]{:S(2)}) copy-start(bf16[4,72,256]{2,1,0:T(8,128)(2,1)} %get-tuple-element.71) | copy-start | bytes 442372
  287.0 96.6 %copy-start.11 = (bf16[2,72,256]{2,1,0:T(8,128)(2,1)S(1)}, bf16[2,72,256]{2,1,0:T(8,128)(2,1)}, u32[]{:S(2)}) copy-start(bf16[2,72,256]{2,1,0:T(8,128)(2,1)} %get-tuple-element.72) | copy-start | bytes 221188
  383.7 4.7 %copy-start.21 = (f32[8]{0:T(128)S(1)}, f32[8]{0:T(128)}, u32[]{:S(2)}) copy-start(f32[8]{0:T(128)} %param.22) | copy-start | bytes 100
  389.9 10.9 %copy-start.5 = (bf16[4,48,576]{2,1,0:T(8,128)(2,1)S(1)}, bf16[4,48,576]{2,1,0:T(8,128)(2,1)}, u32[]{:S(2)}) copy-start(bf16[4,48,576]{2,1,0:T(8,128)(2,1)} %get-tuple-element.73) | copy-start | bytes 663556
  389.9 11.7 %copy-start.9 = (bf16[72,576]{1,0:T(8,128)(2,1)S(1)}, bf16[72,576]{1,0:T(8,128)(2,1)}, u32[]{:S(2)}) copy-start(bf16[72,576]{1,0:T(8,128)(2,1)} %get-tuple-element.69) | copy-start | bytes 248836
  402.3 5.3 %copy-start.7 = (bf16[72,1152]{1,0:T(8,128)(2,1)S(1)}, bf16[72,1152]{1,0:T(8,128)(2,1)}, u32[]{:S(2)}) copy-start(bf16[72,1152]{1,0:T(8,128)(2,1)} %get-tuple-element.67) | copy-start | bytes 497668
  402.3 5.3 %copy-start.10 = (bf16[72,576]{1,0:T(8,128)(2,1)S(1)}, bf16[72,576]{1,0:T(8,128)(2,1)}, u32[]{:S(2)}) copy-start(bf16[72,576]{1,0:T(8,128)(2,1)} %get-tuple-element.68) | copy-start | bytes 248836
  402.3 7.6 %copy-start.2 = (bf16[2,512,1152]{2,1,0:T(8,128)(2,1)S(1)}, bf16[2,512,1152]{2,1,0:T(8,128)(2,1)}, u32[]{:S(2)}) copy-start(bf16[2,512,1152]{2,1,0:T(8,128)(2,1)} %get-tuple-element.123) | copy-start | bytes 7077892
  409.9 2.5 copy-start.3

commit v4 on v3

--- a/solution.py
+++ b/solution.py
@@ -519,6 +519,14 @@
     def own(self):
         return tuple(self.places[name] for name in self.dims)
 
+    def events(self, point, points):
+        for step in range(-1, len(self.order)):
+            if points[step + 1] == point:
+                if step >= 0:
+                    self.copy(step).wait()
+                if step + 1 < len(self.order):
+                    self.copy(step + 1).start()
+
     def copy(self, step):
         known = self.order[:step]
         spot = tuple(slice(None) if n in known else self.places[n] for n in self.dims)
@@ -532,11 +540,6 @@
         )
 
 
-def doubling_order(dims):
-    bits = [name for name in dims if name not in ("y", "b0", "b1")]
-    return bits + ["y", "b1", "b0"]
-
-
 def doubling_scratch(dims):
     return [pltpu.SemaphoreType.DMA((len(dims),))] * 2
 
@@ -554,8 +557,15 @@
     return list(first) + rest
 
 
+def modes_of(modulation_ref, *members):
+    width = modulation_ref.shape[1] // 6
+    names = ("shift_one", "scale_one", "gate_one", "shift_two", "scale_two", "gate_two")
+    places = [names.index(member) * width for member in members]
+    return [modulation_ref[:, place : place + width] for place in places]
+
+
 def front_kernel(
-    own_ref, other_ref, scale_ref, shift_ref, w_ref, gains_ref, cos_ref, sin_ref,
+    own_ref, other_ref, modulation_ref, w_ref, gains_ref, cos_ref, sin_ref,
     entry_ref, heads_ref, unit_ref, factor_ref,
 ):
     section = pl.program_id(0)
@@ -564,11 +574,12 @@
 
     @pl.when(section == 0)
     def _():
+        shift, scale = modes_of(modulation_ref, "shift_one", "scale_one")
         for number, ref in enumerate((own_ref, other_ref)):
             source = ref[...].astype(f32)
             normed = source * lax.rsqrt(jnp.mean(source * source, axis=1, keepdims=True) + epsilon)
             entry_ref[number * half : (number + 1) * half, :] = (
-                normed * (1.0 + scale_ref[...]) + shift_ref[...]
+                normed * (1.0 + scale) + shift
             ).astype(bf16)
 
     raw = dot(w_ref[...], entry_ref[...], 0, 1)
@@ -600,7 +611,7 @@
     return pl.BlockSpec((None, rows, width), lambda t: (lax.axis_index("band"), block(t), 0))
 
 
-def front(images, other, scale, shift, qkv_weight, gains, cosine, sine):
+def front(images, other, modulation, qkv_weight, gains, cosine, sine):
     half, width = other.shape
     patches = 2 * half
     last = lambda s: jnp.minimum(s, 1)
@@ -610,8 +621,7 @@
         in_specs=[
             own_image(half, width, lambda s: 0),
             whole((half, width)),
-            whole((1, width)),
-            whole((1, width)),
+            whole(modulation.shape),
             pl.BlockSpec((width, width), lambda s: (0, s)),
             pl.BlockSpec((1, HD, 1), lambda s: (last(s), 0, 0)),
             whole((HD, patches)),
@@ -632,7 +642,7 @@
         compiler_params=params_of(),
         cost_estimate=cost(6 * patches * width * width, 24e6),
         name="front",
-    )(images, other, scale, shift, qkv_weight, gains, cosine, sine)
+    )(images, other, modulation, qkv_weight, gains, cosine, sine)
 
 
 def attend_kernel(q_ref, k_ref, v_ref, mixed_ref, lse_ref, qext_ref):
@@ -676,7 +686,7 @@
 
 
 def middle_kernel(
-    mixed_ref, w_ref, own_x_ref, other_x_ref, own_c_ref, other_c_ref, vectors_ref,
+    mixed_ref, w_ref, own_x_ref, other_x_ref, own_c_ref, other_c_ref, modulation_ref,
     attended_ref, entry_ref, fed_grad_ref,
 ):
     in_own = pl.program_id(0) < pl.num_programs(0) // 2
@@ -685,14 +695,16 @@
     attended = dot(mixed_ref[...], w_ref[...], 0, 0)
     attended_bf = attended.astype(bf16)
     attended_ref[...] = attended_bf
-    gate_one, scale_two, shift_two, gate_two = [vectors_ref[i : i + 1, :] for i in range(4)]
+    gate_one, scale_two, shift_two, gate_two = modes_of(
+        modulation_ref, "gate_one", "scale_two", "shift_two", "gate_two"
+    )
     middle = x + gate_one * attended_bf.astype(f32)
     normed = middle * lax.rsqrt(jnp.mean(middle * middle, axis=1, keepdims=True) + epsilon)
     entry_ref[...] = (normed * (1.0 + scale_two) + shift_two).astype(bf16)
     fed_grad_ref[...] = (c * gate_two).astype(bf16)
 
 
-def middle_step(mixed, proj_weight, latents, other_x, cotangent, other_c, vectors):
+def middle_step(mixed, proj_weight, latents, other_x, cotangent, other_c, modulation):
     half, width = other_x.shape
     patches = 2 * half
     rows = 256
@@ -710,14 +722,14 @@
             other,
             own,
             other,
-            whole((8, width)),
+            whole((1, 6 * width)),
         ],
         out_specs=[block] * 3,
         out_shape=[jax.ShapeDtypeStruct((patches, width), bf16)] * 3,
         compiler_params=params_of(),
         cost_estimate=cost(2 * patches * width * width, 17e6),
         name="middle",
-    )(mixed, proj_weight, latents, other_x, cotangent, other_c, vectors)
+    )(mixed, proj_weight, latents, other_x, cotangent, other_c, modulation)
 
 
 MLP_TILE = 512
@@ -881,6 +893,22 @@
     )(entry, fed_grad, gateup_weight, gateup_weight, down_weight)
 
 
+ADA_COLUMNS = 384
+ADA_PIECES = 3
+ADA_EARLY = 4 * ADA_PIECES
+
+
+def in_blocks(rows):
+    return jnp.concatenate(
+        [
+            row[:, block * ADA_COLUMNS : (block + 1) * ADA_COLUMNS]
+            for row in rows
+            for block in range(ADA_PIECES)
+        ],
+        axis=0,
+    )
+
+
 TURN_ROWS = 128
 
 
@@ -900,9 +928,13 @@
     ]
 
 
+def core_gather():
+    return ["b3", "b2", "y", "b1", "b0"], (7, 17, 23, 29, 35, 39)
+
+
 def core_kernel(
     dims, fed_ref, entry_grad_ref, own_x_ref, other_x_ref, own_c_ref, other_c_ref, attended_ref,
-    all_mixed_ref, w_ref, vectors_ref, codes_ref,
+    all_mixed_ref, w_ref, modulation_ref, codes_ref,
     q_ref, k_ref, v_ref, mixed_ref, unit_ref, factor_ref, gains_ref, cos_ref, sin_ref,
     down_ref, left_ref, *rest,
 ):
@@ -950,6 +982,7 @@
             yield number, name, stream, source, points, out, spot
 
     def events(point):
+        doubling.events(point, gather_points)
         for number, name, stream, source, points, out, spot in streams():
             local = name in ("proj", "carry")
             steps = len(points) - 1
@@ -993,14 +1026,15 @@
     def _():
         greet(places)
 
-    doubling = Doubling(places, dims, doubling_order(dims), modes_ref, doubling_send, doubling_receive)
+    gather_order, gather_points = core_gather()
+    doubling = Doubling(places, dims, gather_order, modes_ref, doubling_send, doubling_receive)
     width = w_ref.shape[0]
     half = width // 2
     pair = 2 * TURN_ROWS
 
     def turn(number):
         x_ref, c_ref = (own_x_ref, own_c_ref) if number >= turns // 2 else (other_x_ref, other_c_ref)
-        gate_one, scale_two, _, gate_two = [vectors_ref[i : i + 1, :] for i in range(4)]
+        gate_one, scale_two, gate_two = modes_of(modulation_ref, "gate_one", "scale_two", "gate_two")
         attended = attended_ref[...].astype(f32)
         upstream = c_ref[...].astype(f32)
         fed = fed_ref[...]
@@ -1017,20 +1051,19 @@
         start = (number + turns // 2) % turns * TURN_ROWS
         attended_grad_ref[start : start + TURN_ROWS, :] = (middle_grad * gate_one).astype(bf16)
         add = lambda v: jnp.sum(v, axis=0, keepdims=True)
-        sums = jnp.concatenate(
+        sums = in_blocks(
             [
                 add(middle_grad * attended),
                 add(entry_grad),
                 add(entry_grad * normed),
                 add(upstream * fed),
-            ],
-            axis=0,
+            ]
         )
         if number == 0:
-            modes_ref[doubling.own() + (slice(None), slice(0, width))] = sums
-            modes_ref[doubling.own() + (slice(None), slice(width, None))] = codes_ref[...]
+            modes_ref[doubling.own() + (slice(0, ADA_EARLY),)] = sums
+            modes_ref[doubling.own() + (slice(ADA_EARLY, None),)] = codes_ref[...]
         else:
-            modes_ref[doubling.own() + (slice(None), slice(0, width))] += sums
+            modes_ref[doubling.own() + (slice(0, ADA_EARLY),)] += sums
         if number < turns // 2:
             away(number).start()
         else:
@@ -1048,10 +1081,9 @@
             grads = dot(all_mixed_ref[...], attended_grad_ref[...], 1, 0)
             for block in range(blocks):
                 spot = tuple(block // 2**bit % 2 for bit in reversed(range(axes - 1)))
-                part = grads[block * rows : (block + 1) * rows, :]
-                proj_ref[(0,) + spot] = part[:, :half].astype(bf16)
-                proj_ref[(1,) + spot] = part[:, half:].astype(bf16)
-            doubling.copy(0).start()
+                part = grads[block * rows : (block + 1) * rows, :].astype(bf16)
+                proj_ref[(0,) + spot] = part[:, :half]
+                proj_ref[(1,) + spot] = part[:, half:]
         events(number)
 
     for number in range(turns):
@@ -1060,26 +1092,16 @@
         def _():
             turn(number)
 
-    points = {point for plan in core_plan(dims) for point in plan[3]}
+    points = {point for plan in core_plan(dims) for point in plan[3]} | set(gather_points)
 
     class Events:
         @staticmethod
         def at_head(head, end):
-            def run(now):
-                if turns + 2 * now + end in points:
-                    events(turns + 2 * now + end)
-                turn, odd = divmod(now - 2, 2)
-                if end and odd == 0 and 0 <= turn < axes:
-                    doubling.copy(turn).wait()
-                    if turn + 1 < axes:
-                        doubling.copy(turn + 1).start()
-
-            wanted = [
-                now
-                for now in range(HEADS)
-                if turns + 2 * now + end in points or (end and now in range(2, 2 + 2 * axes, 2))
-            ]
-            dispatch(head, {now: functools.partial(run, now) for now in wanted})
+            wanted = [now for now in range(HEADS) if turns + 2 * now + end in points]
+            dispatch(
+                head,
+                {now: functools.partial(events, turns + 2 * now + end) for now in wanted},
+            )
 
     @pl.when(step >= turns)
     def _():
@@ -1091,9 +1113,9 @@
 
     @pl.when(step == pl.num_programs(0) - 1)
     def _():
-        last = max(point for stream in core_plan(dims) for point in stream[3])
-        for point in range(turns + 2 * HEADS, last + 1):
-            events(point)
+        for point in sorted(points):
+            if point >= turns + 2 * HEADS:
+                events(point)
         modes_out_ref[...] = modes_ref[...]
         for number in range(turns // 2):
             away(number).wait()
@@ -1156,7 +1178,7 @@
 
 
 def core_step(
-    fed, entry_grad, latents, other_x, cotangent, other_c, attended, mixed, proj_weight, vectors,
+    fed, entry_grad, latents, other_x, cotangent, other_c, attended, mixed, proj_weight, modulation,
     codes, query, heads, unit, factor, gains, cosine, sine, down, left, carries,
 ):
     half, width = other_x.shape
@@ -1181,7 +1203,7 @@
     couple = lambda rows: pl.BlockSpec((2, None, rows, patches), lambda t: (0, head_of(t), 0, 0))
     anywhere = pl.BlockSpec(memory_space=pl.ANY)
     sums = [(4,) + down_tail, (2,) + left_tail, (len(carries),) + left_tail, proj_tail, ()]
-    sums[-1] = split + (codes.shape[0], width + codes.shape[1])
+    sums[-1] = split + (ADA_EARLY + codes.shape[0], ADA_COLUMNS)
     return pl.pallas_call(
         functools.partial(core_kernel, dims),
         grid=(turns + HEADS,),
@@ -1195,7 +1217,7 @@
             block,
             whole((width, patches)),
             whole((width, width)),
-            whole((8, width)),
+            whole((1, 6 * width)),
             whole(codes.shape),
             single(HDP),
             section(1),
@@ -1247,7 +1269,7 @@
         name="core",
     )(
         fed, entry_grad, latents, other_x, cotangent, other_c, attended, mixed, proj_weight,
-        vectors, codes, query, heads, heads, mixed.reshape(HEADS, HD, patches), unit, factor,
+        modulation, codes, query, heads, heads, mixed.reshape(HEADS, HD, patches), unit, factor,
         gains, cosine, sine, down, left, *carries,
     )
 
@@ -1257,18 +1279,118 @@
 
 def tail_plan(dims):
     return [
-        ("pair", pl.ds(0, 384), order_of(dims, "b0", "b1", "y", "b3", "b2"), (1, 4, 9, 27, 36, 40)),
-        ("pair", pl.ds(384, 384), order_of(dims, "b0", "y", "b1", "b2", "b3"), (1, 4, 18, 27, 35, 40)),
-        ("pair", pl.ds(768, 384), order_of(dims, "b0", "b2", "b1", "b3", "y"), (1, 4, 15, 24, 33, 39)),
-        ("single", None, order_of(dims, "b0", "b2", "b1", "y", "b3"), (2, 5, 25, 35, 45, 51)),
+        ("pair", pl.ds(0, 384), order_of(dims, "b0", "b2", "b3", "b1", "y"), (1, 2, 5, 13, 25, 46)),
+        ("pair", pl.ds(384, 384), order_of(dims, "b0", "y", "b2", "b1", "b3"), (1, 3, 7, 21, 40, 54)),
+        ("pair", pl.ds(768, 384), order_of(dims, "b0", "b2", "b1", "b3", "y"), (1, 4, 15, 35, 49, 61)),
+        ("single", None, order_of(dims, "b0", "b1", "b2", "y", "b3"), (2, 5, 20, 40, 54, 66)),
     ]
 
 
+def tail_gather():
+    return ["b3", "b2", "b1", "y", "b0"], (9, 14, 22, 42, 59, 64)
+
+
+class Ada:
+    def __init__(self, places, refs):
+        (
+            self.weight, self.early, self.table, self.time, self.classes_hbm,
+            self.ada_out, self.bias_out, self.time_out, self.class_out, self.gain_out,
+            self.classes, self.modes, self.codes, self.total, self.before, self.condition,
+            self.features, self.parts, self.sem,
+        ) = refs
+        self.band = places["y"]
+
+    def fetch(self):
+        return pltpu.make_async_copy(self.classes_hbm, self.classes, self.sem.at[0])
+
+    def prepare(self):
+        images = self.early.shape[0]
+
+        def one(image, _):
+            row = pl.ds(image, 1)
+            for block in range(ADA_EARLY):
+                self.modes[2 * ADA_PIECES + block, row, :] = self.early[image, block : block + 1, :]
+            for part in range(2):
+                spot = ADA_EARLY + part
+                self.codes[part, row, :] = self.early[image, spot : spot + 1, :128]
+            return 0
+
+        lax.fori_loop(0, images, one, 0)
+        self.fetch().wait()
+        label, group = self.codes[0][:, :1], self.codes[1][:, :1]
+        place = lambda shape, axis: lax.broadcasted_iota(jnp.int32, shape, axis)
+        group_hot = (group == place((images, GROUPS), 1).astype(f32)).astype(bf16)
+        features = dot(group_hot, self.table[...], 1, 0).astype(bf16)
+        before = dot(features, self.time[...], 1, 0) + dot(self.class_hot(label), self.classes[...], 1, 0)
+        self.before[...] = before
+        condition = (before * jax.nn.sigmoid(before)).astype(bf16)
+        img = lax.axis_index("img")
+
+        def own_rows(values, rows):
+            shape = (rows, values.shape[1])
+            picker = (place(shape, 1) == place(shape, 0) + img * rows).astype(bf16)
+            return dot(picker, values, 1, 1).astype(bf16)
+
+        self.condition[...] = own_rows(condition, self.condition.shape[0])
+        self.features[...] = own_rows(features, self.features.shape[0])
+        self.total[...] = jnp.zeros_like(self.total)
+
+    def class_hot(self, label):
+        shape = (label.shape[0], self.classes.shape[0])
+        return (label == lax.broadcasted_iota(jnp.int32, shape, 1).astype(f32)).astype(bf16)
+
+    def late(self, sums_ref, axes):
+        late = 2 * ADA_PIECES
+
+        def one(image, _):
+            row = pl.ds(image, 1)
+            spot = tuple(lax.rem(lax.div(image, 2**bit), 2) for bit in reversed(range(axes)))
+            for block in range(late):
+                self.modes[block, row, :] = sums_ref[spot + (slice(block, block + 1),)]
+            self.gain_out[...] += sums_ref[spot + (slice(late, late + 1),)]
+            return 0
+
+        self.gain_out[...] = jnp.zeros_like(self.gain_out)
+        lax.fori_loop(0, self.early.shape[0], one, 0)
+
+    def block(self, number):
+        modes = self.modes[number]
+        self.bias_out[...] = jnp.sum(modes, axis=0, keepdims=True)
+        modes_bf = modes.astype(bf16)
+        self.total[...] += dot(modes_bf, self.weight[...], 1, 1)
+        blocks = self.parts.shape[0]
+        here = number - blocks * self.band
+
+        @pl.when((here >= 0) & (here < blocks))
+        def _():
+            self.parts[here] = dot(self.condition[...], modes_bf, 1, 0)
+
+    def finish(self, class_ref):
+        before = self.before[...]
+        sigma = jax.nn.sigmoid(before)
+        before_grad = self.total[...] * (sigma * (1.0 + before * (1.0 - sigma)))
+        pieces, left = [], before_grad
+        for _ in range(3):
+            pieces.append(left.astype(bf16))
+            left = left - pieces[-1].astype(f32)
+        half = before.shape[1] // 2
+        times = sum(dot(self.features[...], piece, 1, 0) for piece in pieces)
+        self.time_out[...] = jnp.where(self.band == 0, times[:, :half], times[:, half:])
+        class_hot = self.class_hot(self.codes[0][:, :1])
+        class_ref[...] = sum(dot(class_hot, piece, 0, 0) for piece in pieces)
+        for block in range(self.parts.shape[0]):
+            columns = slice(block * ADA_COLUMNS, (block + 1) * ADA_COLUMNS)
+            self.ada_out[:, columns] = self.parts[block]
+
+
 def back_kernel(
-    dims, pg_ref, w_ref, entry_ref, own_x_ref, other_x_ref, middle_grad_ref, scale_ref,
-    gain_terms_ref,
-    latents_out_ref, sums_out_ref, pair_out_ref, single_out_ref,
-    entry_grad_ref, pair_ref, single_ref, rows_ref, row_send, row_receive, *buffers,
+    dims, pg_ref, w_ref, entry_ref, own_x_ref, other_x_ref, middle_grad_ref, modulation_ref,
+    gain_terms_ref, ada_ref, early_ref, table_ref, time_ref, classes_ref,
+    latents_out_ref, pair_out_ref, single_out_ref, ada_out_ref, bias_out_ref, time_out_ref,
+    class_out_ref, gain_out_ref,
+    entry_grad_ref, pair_ref, single_ref, rows_ref, row_send, row_receive,
+    classes_copy_ref, modes_ref, codes_ref, total_ref, before_ref, condition_ref, features_ref,
+    parts_ref, ada_sem, *buffers,
 ):
     step = pl.program_id(0)
     places = own_places()
@@ -1284,8 +1406,19 @@
             streams.append((stream, pair_ref, when, pair_out_ref.at[:, columns]))
         else:
             streams.append((stream, single_ref, when, single_out_ref))
-    doubling = Doubling(places, dims, doubling_order(dims), sums_ref, send, receive)
+    gather_order, gather_points = tail_gather()
+    doubling = Doubling(places, dims, gather_order, sums_ref, send, receive)
+    ada = Ada(
+        places,
+        (
+            ada_ref, early_ref, table_ref, time_ref, classes_ref,
+            ada_out_ref, bias_out_ref, time_out_ref, class_out_ref, gain_out_ref,
+            classes_copy_ref, modes_ref, codes_ref, total_ref, before_ref, condition_ref,
+            features_ref, parts_ref, ada_sem,
+        ),
+    )
     width = entry_grad_ref.shape[0]
+    patches = entry_ref.shape[0]
     half = width // 2
     blocks = 2 ** (phases - 1)
     rows = width // blocks
@@ -1293,32 +1426,32 @@
     @pl.when(step == 0)
     def _():
         entry_grad_ref[...] = jnp.zeros_like(entry_grad_ref)
+        ada.fetch().start()
         greet(places)
 
     @pl.when(step < 3)
     def _():
-        grad = dot(entry_ref[...], pg_ref[...], 0, 1)
-
         def spot(block):
             return tuple(block // 2**bit % 2 for bit in reversed(range(phases - 1)))
 
-        def part(block):
-            return grad[block * rows : (block + 1) * rows, :]
-
         @pl.when(step < 2)
         def _():
+            grad = dot(entry_ref[...], pg_ref[...], 0, 1)
             for block in range(blocks):
-                pair_ref[(step,) + spot(block)] = part(block).astype(bf16)
+                part = grad[block * rows : (block + 1) * rows, :]
+                pair_ref[(step,) + spot(block)] = part.astype(bf16)
 
         @pl.when(step == 2)
         def _():
+            grad = dot(entry_ref[...], pg_ref[...], 0, 1)
             for block in range(blocks):
-                single_ref[(0,) + spot(block)] = part(block)[:, :half].astype(bf16)
-                single_ref[(1,) + spot(block)] = part(block)[:, half:].astype(bf16)
+                part = grad[block * rows : (block + 1) * rows, :].astype(bf16)
+                single_ref[(0,) + spot(block)] = part[:, :half]
+                single_ref[(1,) + spot(block)] = part[:, half:]
 
     @pl.when((step >= 3) & (step < 6))
     def _():
-        entry_grad_ref[...] += dot(w_ref[...], pg_ref[...], 1, 0)
+        entry_grad_ref[:, :patches] += dot(w_ref[...], pg_ref[...], 1, 0)
 
     band = places["y"]
 
@@ -1348,18 +1481,20 @@
             source = (other_x_ref if number < 2 else own_x_ref)[...].astype(f32)
             factor = lax.rsqrt(jnp.mean(source * source, axis=1, keepdims=True) + epsilon)
             normed = source * factor
-            inner = entry_grad * (1.0 + scale_ref[...])
+            (scale,) = modes_of(modulation_ref, "scale_one")
+            inner = entry_grad * (1.0 + scale)
             grads = middle_grad_ref[...] + factor * (
                 inner - normed * jnp.mean(inner * normed, axis=1, keepdims=True)
             )
             rows_ref[number] = grads.astype(bf16)
             add = lambda v: jnp.sum(v, axis=0, keepdims=True)
-            sums = jnp.concatenate([add(entry_grad), add(entry_grad * normed)], axis=0)
+            sums = in_blocks([add(entry_grad), add(entry_grad * normed)])
+            late = 2 * ADA_PIECES
             if number == 0:
-                sums_ref[doubling.own() + (slice(0, 2),)] = sums
-                sums_ref[doubling.own() + (slice(2, 4),)] = gain_terms_ref[...]
+                sums_ref[doubling.own() + (slice(0, late),)] = sums
+                sums_ref[doubling.own() + (slice(late, None),)] = gain_terms_ref[...]
             else:
-                sums_ref[doubling.own() + (slice(0, 2),)] += sums
+                sums_ref[doubling.own() + (slice(0, late),)] += sums
             if number < 2:
                 away(number).start()
             else:
@@ -1380,30 +1515,57 @@
                 if phase + 1 < phases:
                     stream.copy(phase + 1, source).start()
 
-    for now in range(1, 10):
-
-        @pl.when(step == now)
-        def _():
-            if now == 9:
-                doubling.copy(0).start()
-            due(now)
-            if now == 9:
-                last = max(point for plan in tail_plan(dims) for point in plan[3])
-                for later in range(10, last + 1):
-                    due(later)
-                    turn, odd = divmod(later - 12, 3)
-                    if odd == 0 and 0 <= turn < phases:
-                        doubling.copy(turn).wait()
-                        if turn + 1 < phases:
-                            doubling.copy(turn + 1).start()
-                sums_out_ref[...] = sums_ref[...]
-                for number in range(2):
-                    away(number).wait()
-                    stay(number).wait()
+    first_ada = 10
+    ada_steps = 6 * ADA_PIECES
+
+    @pl.when(step == first_ada)
+    def _():
+        ada.prepare()
+
+    points = {when for plan in tail_plan(dims) for when in plan[3]} | set(gather_points)
+    hub = first_ada + ADA_EARLY
+
+    def point(now):
+        doubling.events(now, gather_points)
+        due(now)
+
+    dispatch(step, {now: functools.partial(point, now) for now in points if now < hub})
+
+    @pl.when(step == hub)
+    def _():
+        for later in sorted(points):
+            if hub <= later <= gather_points[-1]:
+                point(later)
+        ada.late(sums_ref, phases)
+
+    @pl.when(step >= first_ada)
+    def _():
+        number = step - first_ada
+        ada.block(jnp.where(number < ADA_EARLY, number + ada_steps - ADA_EARLY, number - ADA_EARLY))
+
+    class_ref = entry_grad_ref.at[pl.ds(0, class_out_ref.shape[0])]
+    class_copy = pltpu.make_async_copy(class_ref, class_out_ref, ada_sem.at[1])
+    final = first_ada + ada_steps - 1
+
+    @pl.when(step == final)
+    def _():
+        ada.finish(class_ref)
+        class_copy.start()
+
+    @pl.when(step == final)
+    def _():
+        for later in sorted(points):
+            if later > gather_points[-1]:
+                point(later)
+        for number in range(2):
+            away(number).wait()
+            stay(number).wait()
+        class_copy.wait()
 
 
 def back_step(
-    projected_grad, qkv_weight, entry, latents, other_x, middle_grad, scale, gain_rows
+    projected_grad, qkv_weight, entry, latents, other_x, middle_grad, modulation, gain_rows,
+    ada_weight, early, table, time_weight, class_table,
 ):
     patches, width = entry.shape
     dims = pair_axes()
@@ -1416,27 +1578,45 @@
             place = jnp.where(step == number, section, place)
         return place
 
-    weight_section = lambda t: jnp.where(t < 4, 0, jnp.minimum(t - 3, 2))
+    weight_section = lambda t: jnp.clip(t - 3, 0, 2)
     row_block = lambda t: lax.rem(jnp.clip(t - 6, 0, 3) + 2, 4)
     block = pl.BlockSpec((BACK_ROWS, width), lambda t: (row_block(t), 0))
     own = own_image(BACK_ROWS, width, lambda t: jnp.clip(t - 8, 0, 1))
     other = pl.BlockSpec((BACK_ROWS, width), lambda t: (jnp.clip(t - 6, 0, 1), 0))
     tails = [(rows, 384)] * 3 + [(rows, width // 2)]
-    sums = [(rows, width), (rows, width // 2)]
+    classes = class_table.shape[0]
+    images = early.shape[0]
+    time_rows = time_weight.shape[0] // lax.axis_size("img")
+    ada_steps = 6 * ADA_PIECES
+    half_steps = ada_steps // 2
+
+    def ada_block(t):
+        number = jnp.maximum(t - 10, 0)
+        return jnp.where(number < ADA_EARLY, number + ada_steps - ADA_EARLY, number - ADA_EARLY)
+
     wide = (2,) * len(dims)
     scratch = [
-        pltpu.VMEM((width, patches), f32),
+        pltpu.VMEM((width, width), f32),
         pltpu.VMEM(wide + (rows, width), bf16),
         pltpu.VMEM(wide + (rows, width // 2), bf16),
         pltpu.VMEM((4, BACK_ROWS, width), bf16),
         pltpu.SemaphoreType.DMA((4,)),
+        pltpu.SemaphoreType.DMA((2,)),
+        pltpu.VMEM((classes, width), bf16),
+        pltpu.VMEM((ada_steps, images, ADA_COLUMNS), f32),
+        pltpu.VMEM((2, images, 128), f32),
+        pltpu.VMEM((images, width), f32),
+        pltpu.VMEM((images, width), f32),
+        pltpu.VMEM((rows, images), bf16),
+        pltpu.VMEM((time_rows, images), bf16),
+        pltpu.VMEM((half_steps, rows, ADA_COLUMNS), f32),
         pltpu.SemaphoreType.DMA((2,)),
     ]
     for tail in tails:
         scratch += halving_scratch(dims, tail)
     return pl.pallas_call(
         functools.partial(back_kernel, dims),
-        grid=(10,),
+        grid=(10 + ada_steps,),
         in_specs=[
             pl.BlockSpec((None, width, patches), lambda t: (section_of(t), 0, 0)),
             pl.BlockSpec((width, width), lambda t: (0, weight_section(t))),
@@ -1444,24 +1624,44 @@
             own,
             other,
             block,
-            whole((1, width)),
-            whole((2, width)),
+            whole((1, 6 * width)),
+            whole((2, ADA_COLUMNS)),
+            pl.BlockSpec((width, ADA_COLUMNS), lambda t: (0, ada_block(t))),
+            whole(early.shape),
+            whole(table.shape),
+            whole(time_weight.shape),
+            pl.BlockSpec(memory_space=pl.ANY),
         ],
         out_specs=[
             pl.BlockSpec(memory_space=pl.ANY),
-            whole(wide + (4, width)),
-        ]
-        + [whole(shape) for shape in sums],
+            whole((rows, width)),
+            whole((rows, width // 2)),
+            whole((rows, 3 * width)),
+            pl.BlockSpec((1, ADA_COLUMNS), lambda t: (0, ada_block(t))),
+            whole((time_rows, width // 2)),
+            pl.BlockSpec(memory_space=pl.ANY),
+            whole((1, ADA_COLUMNS)),
+        ],
         out_shape=[
             jax.ShapeDtypeStruct((2, patches // 2, width), bf16),
-            jax.ShapeDtypeStruct(wide + (4, width), f32),
-        ]
-        + [jax.ShapeDtypeStruct(shape, bf16) for shape in sums],
-        scratch_shapes=scratch + [pltpu.VMEM(wide + (4, width), f32)] + doubling_scratch(dims),
+            jax.ShapeDtypeStruct((rows, width), bf16),
+            jax.ShapeDtypeStruct((rows, width // 2), bf16),
+            jax.ShapeDtypeStruct((rows, 3 * width), f32),
+            jax.ShapeDtypeStruct((1, 6 * width), f32),
+            jax.ShapeDtypeStruct((time_rows, width // 2), f32),
+            jax.ShapeDtypeStruct((classes, width), f32),
+            jax.ShapeDtypeStruct((1, ADA_COLUMNS), f32),
+        ],
+        scratch_shapes=scratch
+        + [pltpu.VMEM(wide + (2 * ADA_PIECES + 2, ADA_COLUMNS), f32)]
+        + doubling_scratch(dims),
         compiler_params=params_of(collective_id=2, has_side_effects=True),
         cost_estimate=cost(12 * patches * width * width, 40e6),
         name="back",
-    )(projected_grad, qkv_weight, entry, latents, other_x, middle_grad, scale, gain_rows)
+    )(
+        projected_grad, qkv_weight, entry, latents, other_x, middle_grad, modulation, gain_rows,
+        ada_weight, early, table, time_weight, class_table,
+    )
 
 
 def pick(values, index):
@@ -1489,14 +1689,14 @@
 ):
     width = latents.shape[-1]
     bands = lax.axis_size("band")
-    img_index = lax.axis_index("img")
     band_index = lax.axis_index("band")
 
     def from_other(values):
         return lax.ppermute(values, "band", [(0, 1), (1, 0)])
 
     other_x = from_other(pick(latents, 1 - band_index))
-    other_c = from_other(pick(cotangent, 1 - band_index))
+    away_c, _ = lax.optimization_barrier((pick(cotangent, 1 - band_index), other_x))
+    other_c = from_other(away_c)
     places = jnp.stack([row_pos, col_pos], axis=1)
     places = jnp.concatenate([places, from_other(places)], axis=0)
 
@@ -1507,79 +1707,49 @@
     cosine = jnp.concatenate([cosine[0], cosine[0], cosine[1], cosine[1]], axis=0)
     sine = jnp.concatenate([-sine[0], sine[0], -sine[1], sine[1]], axis=0)
 
-    def condition_of(group_ids, labels):
-        group_hot = (group_ids[:, None] == jnp.arange(GROUPS, dtype=jnp.int32)[None, :]).astype(f32)
-        times = jax.nn.sigmoid(jnp.dot(group_hot, group_logits, precision=highest))
-        features = time_features(times, FREQ // 2).astype(bf16)
-        before = jnp.dot(features, time_weight, preferred_element_type=f32) + jnp.take(
-            class_table, labels, axis=0
-        ).astype(f32)
-        return features, before, jax.nn.silu(before).astype(bf16)
-
-    own_group = pick(group_ids, band_index)[None]
-    own_label = pick(labels, band_index)[None]
-    _, _, condition = condition_of(own_group, own_label)
+    table = time_features(jax.nn.sigmoid(group_logits), FREQ // 2).astype(bf16)
+    own_group = pick(group_ids, band_index)
+    own_label = pick(labels, band_index)
+    before = jnp.dot(
+        pick(table, own_group)[None], time_weight, preferred_element_type=f32
+    ) + pick(class_table, own_label)[None].astype(f32)
+    condition = jax.nn.silu(before).astype(bf16)
     modulation = jnp.dot(condition, ada_weight, preferred_element_type=f32) + ada_bias
-    modes = modulation.reshape(6, width)
-    shift_one, scale_one = modes[0:1], modes[1:2]
-    vectors = jnp.concatenate([modes[2:3], modes[4:5], modes[3:4], modes[5:6], modes[2:6]], axis=0)
-
     scaling = HD ** (-0.5)
     gains = jnp.stack([query_gain, key_gain])[:, :, None]
     scaled_gains = gains * jnp.array([scaling * LOG2E, 1.0], f32)[:, None, None]
     entry_one, heads, unit, factor = front(
-        latents, other_x, scale_one, shift_one, qkv_weight, scaled_gains, cosine, sine
+        latents, other_x, modulation, qkv_weight, scaled_gains, cosine, sine
     )
     mixed, query = attend(heads)
     mixed = mixed.reshape(width, -1)
     attended, entry_two, fed_grad = middle_step(
-        mixed, proj_weight, latents, other_x, cotangent, other_c, vectors
+        mixed, proj_weight, latents, other_x, cotangent, other_c, modulation
     )
     fed, entry_two_grad, grad_down, gateup_done, gateup_left, *carries = mlp(
         entry_two, fed_grad, gateup_weight, down_weight
     )
-    codes = jnp.stack([own_label, own_group], axis=0).astype(f32)
-    codes = jnp.pad(codes, ((0, 2), (0, 127)))
+    codes = jnp.stack([own_label, own_group])[:, None].astype(f32)
+    codes = jnp.pad(codes, ((0, 2), (0, ADA_COLUMNS - 1)))
     (
         result, middle_grad, projected_grad, gain_terms,
         sum_down, gateup_last, gateup_carried, sum_proj, modes_early,
     ) = core_step(
         fed, entry_two_grad, latents, other_x, cotangent, other_c, attended, mixed, proj_weight,
-        vectors, codes, query, heads, unit, factor, gains, cosine, sine, grad_down, gateup_left,
+        modulation, codes, query, heads, unit, factor, gains, cosine, sine, grad_down, gateup_left,
         carries,
     )
-    gain_rows = jnp.pad(jnp.sum(gain_terms, axis=2), ((0, 0), (0, width - HD)))
-    grad_latents, modes_late, qkv_pair, qkv_single = back_step(
+    gain_rows = jnp.pad(jnp.sum(gain_terms, axis=2), ((0, 0), (0, 128 - HD))).reshape(1, -1)
+    gain_rows = jnp.pad(gain_rows, ((0, 1), (0, ADA_COLUMNS - gain_rows.shape[1])))
+    (
+        grad_latents, qkv_pair, qkv_single, sum_ada, sum_bias, sum_time, sum_class, gain_sums,
+    ) = back_step(
         projected_grad.reshape(3, width, -1), qkv_weight, entry_one, latents, other_x, middle_grad,
-        scale_one, gain_rows,
-    )
-    modes_early = modes_early.reshape(-1, 4, modes_early.shape[-1])
-    modes_late = modes_late.reshape(-1, 4, width)
-    modulation_all = jnp.concatenate(
-        [modes_late[:, 0], modes_late[:, 1]] + [modes_early[:, place, :width] for place in range(4)],
-        axis=1,
-    ).astype(bf16)
-    gain_sums = jnp.sum(modes_late[:, 2:, :HD], axis=0)
-    sum_query_gain, sum_key_gain = gain_sums[0], gain_sums[1]
-    codes = modes_early[:, :2, width].astype(jnp.int32).T
-    features_all, before_all, condition_all = condition_of(codes[1], codes[0])
-    before_grad = lax.dot_general(
-        modulation_all, ada_weight, (((1,), (1,)), ((), ())), preferred_element_type=f32
-    ) * silu_slope(before_all)
-    ada_rows = width // lax.axis_size("img")
-    ada_cols = 6 * width // bands
-    time_rows = FREQ // lax.axis_size("img")
-    time_cols = width // bands
-    condition_part = lax.dynamic_slice_in_dim(condition_all, img_index * ada_rows, ada_rows, 1)
-    modulation_part = lax.dynamic_slice_in_dim(modulation_all, band_index * ada_cols, ada_cols, 1)
-    sum_ada = jnp.dot(condition_part.T, modulation_part, preferred_element_type=f32)
-    features_part = lax.dynamic_slice_in_dim(features_all, img_index * time_rows, time_rows, 1)
-    before_part = lax.dynamic_slice_in_dim(before_grad, band_index * time_cols, time_cols, 1)
-    sum_time = jnp.dot(features_part.astype(f32).T, before_part, precision=highest)
-    class_all = (codes[0][:, None] == jnp.arange(NCLASS, dtype=jnp.int32)[None, :]).astype(f32)
-    sum_class = jnp.dot(class_all.T, before_grad, precision=highest)
-    sum_bias = jnp.sum(modulation_all.astype(f32), axis=0)
-
+        modulation, gain_rows, ada_weight, modes_early.reshape((-1,) + modes_early.shape[-2:]), table,
+        time_weight, class_table,
+    )
+    sum_bias = sum_bias.reshape(-1)
+    sum_query_gain, sum_key_gain = gain_sums[0, :HD], gain_sums[0, 128 : 128 + HD]
     sum_down = sum_down.reshape(-1, sum_down.shape[-1]).astype(f32)
     sum_proj = sum_proj.astype(f32)
     gateup_carried = gateup_carried.reshape((len(CARRIED), 2) + gateup_carried.shape[1:])

time: 419 us -> 386 us (0.921)
  matrix products: 25.4 us -> 8.15 us
  Pallas kernels: 340 us -> 328 us
  waiting for transfers between devices: 4.65 us -> 0.24 us
    dot_general x7 -> x0, matrix products: 17.6 us -> none  [the longest x1 10.3 us: per_device_whole(): lax.dot_general(modulation_all, ada_weight, (((1,), (1,)), ((), ())), pre...]
    pallas_call x1, Pallas kernels: 94.6 us -> 82.5 us  [back_step(): pl.pallas_call(functools.partial(back_kernel, dims), grid=(10 + ada_steps...]
    ppermute x3, waiting for transfers between devices: 4.65 us -> 0.24 us  [from_other(): return lax.ppermute(values, 'band', [(0, 1), (1, 0)])]
    unnamed x52 -> x45, local copies, waits for them, and re-layouts: 5.22 us -> 8.56 us
  transfers between devices with their start and end apart: 3 -> 3, of which waited for: 1 -> 1; matrix products, arithmetic and copies ran while one was open for 5% -> 7% of each run, Pallas kernels for 11% -> 12%
where the time goes in v4:
time: 386 us; the launch traced here: 381 us
  Pallas kernels  328 us (85%)
  local copies, waits for them, and re-layouts  21.8 us (6%)
  other arithmetic  13.4 us (3%)
  matrix products  8.15 us (2%)
  between operations  5.13 us (1%)
  starting transfers between devices  4.76 us (1%)
    pallas_call x1, Pallas kernels, core_step(): pl.pallas_call(functools.partial(core_kernel, dims), grid=(turns + HEADS,...  96.2 us
    pallas_call x1, Pallas kernels, mlp(): pl.pallas_call(functools.partial(mlp_kernel, dims), grid=(tiles,), in_spe...  94.8 us
    pallas_call x1, Pallas kernels, back_step(): pl.pallas_call(functools.partial(back_kernel, dims), grid=(10 + ada_steps...  82.5 us
    pallas_call x1, Pallas kernels, front(): pl.pallas_call(front_kernel, grid=(3,), in_specs=[own_image(half, width,...  23.6 us
    pallas_call x1, Pallas kernels, attend(): pl.pallas_call(lambda q, k, v, mixed, qext: attend_kernel(q, k, v, mixed,...  20.4 us
    pallas_call x1, Pallas kernels, middle_step(): pl.pallas_call(middle_kernel, grid=(patches // rows,), in_specs=[pl.Block...  10.3 us
    unnamed x45, local copies, waits for them, and re-layouts  8.56 us
    dot_general x1, matrix products, per_device_whole(): jnp.dot(condition, ada_weight, preferred_element_type=f32) + ada_bias  8.15 us
  transfers between devices with their start and end apart: 3, of which 1 were waited for; matrix products, arithmetic and copies ran while one was open for 7% of the time, Pallas kernels for 12%

profile of v4, /device:TPU:0, one launch (start us, length us, event | category | flops | bytes accessed | tf_op | source)
XLA Modules:
  0.0 381.3 jit_solution(14984096688582566377)
XLA Ops:
  0.7 0.0 copy-start
  0.7 0.9 pad_add_fusion
  1.5 3.0 collective-permute-start.1
  4.5 2.4 dynamic-slice_bitcast_fusion.1
  6.9 0.0 collective-permute-start
  6.9 0.5 multiply_exponential_fusion.1
  7.4 1.2 dynamic_slice.23
  10.0 1.2 dynamic_slice.25
  12.5 1.2 divide_multiply_fusion.2
  13.7 0.7 copy.42
  14.4 0.7 copy.41
  15.1 1.1 dynamic-slice_bitcast_fusion
  17.5 1.3 add_convert_fusion.1
  18.8 0.8 fusion.9
  19.6 0.6 pad_maximum_fusion.2.table_ref
  20.2 1.5 maximum_multiply_fusion.gains_ref
  21.7 8.2 %convolution_reduce_fusion = f32[6912]{0:T(1024)S(1)} fusion(bf16[1152,6912]{1,0:T(8,128)(2,1)} %ada_ref.1, bf16[256,1152]{1,0:T(8,128)(2,1)} %time_ref.1, bf16[1000,1152]{1,0:T(8,128)(2,1)} %classes_ref.1, s32[]{:T(128)S(6)} %select_n.29, s32[]{:T(128)S(6)} %select_n.28, bf16[8,128]{1,0:T(8,128)(2,1)S(1)} %get-tuple-element.95, ...), kind=kOutput, calls=%fused_computation.3 | convolution fusion | flops 16524160 | bytes 16551432 | tf_op jit(solution)/shard_map/dot_general | solution.py:1717
  30.0 0.6 add.48.modulation_ref
  30.6 0.7 copy.43.gains_ref
  31.3 0.6 pad.12.codes_ref
  31.9 0.0 collective-permute-done.1
  32.0 0.8 multiply_sine_fusion
  32.8 0.8 pad_maximum_fusion.cos_ref
  33.5 0.8 pad_maximum_fusion.1.sin_ref
  34.3 0.2 collective-permute-done.other_ref.other_x_ref
  34.5 1.8 collective-permute-start.2
  36.3 23.6 %front.1 = (bf16[1024,1152]{1,0:T(8,128)(2,1)}, bf16[3,16,80,1024]{3,2,1,0:T(8,128)(2,1)}, bf16[2,16,72,1024]{3,2,1,0:T(8,128)(2,1)}, f32[2,16,1,1024]{3,2,1,0:T(1,128)}) custom-call(bf16[2,512,1152]{2,1,0:T(8,128)(2,1)} %own_x_ref.5, bf16[512,1152]{1,0:T(8,128)(2,1)} %copy-done.2, f32[1,6912]{1,0:T(1,128)} %add.48.modulation_ref, bf16[1152,3456]{1,0:T(8,128)(2,1)} %w_ref.7, ...), custom_call_target="tpu_custom_call" | custom-call | flops 8153726976 | bytes 24000000 | tf_op jit(solution)/shard_map/front/pallas_call | solution.py:618
  59.9 20.4 %attend.1 = (bf16[16,72,1024]{2,1,0:T(8,128)(2,1)}, bf16[16,80,1024]{2,1,0:T(8,128)(2,1)}) custom-call(bf16[3,16,80,1024]{3,2,1,0:T(8,128)(2,1)} %get-tuple-element.48.q.k.v.k_ref.v_ref, bf16[3,16,80,1024]{3,2,1,0:T(8,128)(2,1)} %get-tuple-element.48.q.k.v.k_ref.v_ref, bf16[3,16,80,1024]{3,2,1,0:T(8,128)(2,1)} %get-tuple-element.48.q.k.v.k_ref.v_ref), custom_call_target="tpu_custom_call" | custom-call | flops 10737418240 | bytes 14000000 | tf_op jit(solution)/shard_map/attend/pallas_call | solution.py:670
  80.3 0.0 collective-permute-done.2.other_c_ref
  80.3 10.3 %middle.1 = (bf16[1024,1152]{1,0:T(8,128)(2,1)}, bf16[1024,1152]{1,0:T(8,128)(2,1)}, bf16[1024,1152]{1,0:T(8,128)(2,1)}) custom-call(bf16[1152,1024]{1,0:T(8,128)(2,1)} %bitcast.57, bf16[1152,1152]{1,0:T(8,128)(2,1)} %w_ref.6, bf16[2,512,1152]{2,1,0:T(8,128)(2,1)} %own_x_ref.5, bf16[512,1152]{1,0:T(8,128)(2,1)} %copy-done.2, ...), custom_call_target="tpu_custom_call" | custom-call | flops 2717908992 | bytes 17000000 | tf_op jit(solution)/shard_map/middle/pallas_call | solution.py:715
  90.6 94.8 %mlp.1 = (f32[1024,1152]{1,0:T(8,128)}, f32[1024,1152]{1,0:T(8,128)}, bf16[2,3072,576]{2,1,0:T(8,128)(2,1)}, bf16[3,2,72,256]{3,2,1,0:T(8,128)(2,1)}, bf16[2,2,2...) custom-call(bf16[1024,1152]{1,0:T(8,128)(2,1)} %get-tuple-element.51, ...), custom_call_target="tpu_custom_call" | custom-call | flops 65229815808 | bytes 56000000 | tf_op jit(solution)/shard_map/mlp/pallas_call | solution.py:861
  185.4 96.2 %core.1 = (bf16[2,512,1152]{2,1,0:T(8,128)(2,1)}, f32[1024,1152]{1,0:T(8,128)}, bf16[3,16,72,1024]{3,2,1,0:T(8,128)(2,1)}, f32[2,72,1024]{2,1,0:T(8,128)}, bf16[...) custom-call(f32[1024,1152]{1,0:T(8,128)} %get-tuple-element.53.fed_r, ...), custom_call_target="tpu_custom_call" | custom-call | flops 32212254720 | bytes 70000000 | tf_op jit(solution)/shard_map/core/pallas_call | solution.py:1207
  281.6 1.2 reduce_sum.9
  282.8 0.6 pad.14.gain_terms_ref
  283.4 82.5 %back.1 = (bf16[2,512,1152]{2,1,0:T(8,128)(2,1)}, bf16[72,1152]{1,0:T(8,128)(2,1)}, bf16[72,576]{1,0:T(8,128)(2,1)}, f32[72,3456]{1,0:T(8,128)}, f32[1,6912]{1,0...) custom-call(bf16[3,1152,1024]{2,1,0:T(8,128)(2,1)} %bitcast.71, bf16[1152,3456]{1,0:T(8,128)(2,1)} %w_ref.7, ...), custom_call_target="tpu_custom_call" | custom-call | flops 16307453952 | bytes 40000000 | tf_op jit(solution)/shard_map/back/pallas_call | solution.py:1617
  365.9 1.2 slice_bitcast_fusion.4
  367.1 0.7 convert_element_type.53
  367.8 0.8 bitcast_convert_fusion
  368.6 0.1 convert_bitcast_fusion
  368.7 0.5 copy.44
  369.2 1.6 reshape.168
  370.8 0.7 reduce.1
  371.5 0.9 fusion
  372.4 1.4 copy.50
  373.8 3.4 copy.51
  377.2 0.6 copy.52
  377.8 2.2 copy.53
  379.9 0.9 copy.54
  (47 shorter events, 0.2 us)
Async XLA Ops:
  0.6 13.0 %copy-start.16 = (f32[72]{0:T(128)S(1)}, f32[72]{0:T(128)}, u32[]{:S(2)}) copy-start(f32[72]{0:T(128)} %param.31) | copy-start | bytes 868
  0.7 13.7 %copy-start.17 = (f32[72]{0:T(128)S(1)}, f32[72]{0:T(128)}, u32[]{:S(2)}) copy-start(f32[72]{0:T(128)} %param.30) | copy-start | bytes 868
  0.7 14.4 %copy-start = (bf16[2,512,1152]{2,1,0:T(8,128)(2,1)S(1)}, bf16[2,512,1152]{2,1,0:T(8,128)(2,1)}, u32[]{:S(2)}) copy-start(bf16[2,512,1152]{2,1,0:T(8,128)(2,1)} %own_c_ref.3) | copy-start | bytes 7077892
  1.5 30.4 %collective-permute-start.1 = (s32[512,2]{0,1:T(2,128)S(1)}, s32[512,2]{0,1:T(2,128)S(1)}, u32[]{:S(2)}, u32[]{:S(2)}) collective-permute-start(s32[512,2]{0,1:T(2,128)S(1)} %pad_add_fusion), channel_id=1, source_target_pairs={{0,1},{1,0},{2,3},{3,2},{4,5},{5,4},{6,7},{7,6},{8,9},{9,8},{10,11... | collective-permute-start | bytes 12296 | tf_op jit(solution)/shard_map/ppermute | solution.py:1695
  6.9 27.6 %collective-permute-start = (bf16[512,1152]{1,0:T(8,128)(2,1)}, bf16[512,1152]{1,0:T(8,128)(2,1)S(1)}, u32[]{:S(2)}, u32[]{:S(2)}) collective-permute-start(bf16[512,1152]{1,0:T(8,128)(2,1)} %dynamic-slice_bitcast_fusion.1), channel_id=1, source_target_pairs={{0,1},{1,0},{2,3},{3,2},{4,5},{5,4},{6,7},{7,6},{8,9},{9,8},{10,11... | collective-permute-start | bytes 3538952 | tf_op jit(solution)/shard_map/ppermute | solution.py:1695
  21.7 8.2 %copy-start.12 = (f32[6912]{0:T(1024)S(1)}, f32[6912]{0:T(1024)}, u32[]{:S(2)}) copy-start(f32[6912]{0:T(1024)} %param.28) | copy-start | bytes 82948
  21.7 10.2 %copy-start.14 = (s32[512]{0:T(512)S(1)}, s32[512]{0:T(512)}, u32[]{:S(2)}) copy-start(s32[512]{0:T(512)} %param.24) | copy-start | bytes 6148
  21.7 10.2 %copy-start.15 = (s32[512]{0:T(512)S(1)}, s32[512]{0:T(512)}, u32[]{:S(2)}) copy-start(s32[512]{0:T(512)} %param.23) | copy-start | bytes 6148
  34.5 1.8 copy-start.2
  34.5 45.8 %collective-permute-start.2 = (bf16[512,1152]{1,0:T(8,128)(2,1)}, bf16[512,1152]{1,0:T(8,128)(2,1)}, u32[]{:S(2)}, u32[]{:S(2)}) collective-permute-start(bf16[512,1152]{1,0:T(8,128)(2,1)} %dynamic-slice_bitcast_fusion), channel_id=1, source_target_pairs={{0,1},{1,0},{2,3},{3,2},{4,5},{5,4},{6,7},{7,6},{8,9},{9,8},{10,11... | collective-permute-start | bytes 3538952 | tf_op jit(solution)/shard_map/ppermute | solution.py:1695
  283.4 83.7 %copy-start.8 = (bf16[72,576]{1,0:T(8,128)(2,1)S(1)}, bf16[72,576]{1,0:T(8,128)(2,1)}, u32[]{:S(2)}) copy-start(bf16[72,576]{1,0:T(8,128)(2,1)} %get-tuple-element.79) | copy-start | bytes 248836
  283.4 84.4 %copy-start.4 = (bf16[4,48,576]{2,1,0:T(8,128)(2,1)S(1)}, bf16[4,48,576]{2,1,0:T(8,128)(2,1)}, u32[]{:S(2)}) copy-start(bf16[4,48,576]{2,1,0:T(8,128)(2,1)} %get-tuple-element.83) | copy-start | bytes 663556
  283.4 85.2 %copy-start.5 = (bf16[3,2,72,256]{3,2,1,0:T(8,128)(2,1)S(1)}, bf16[3,2,72,256]{3,2,1,0:T(8,128)(2,1)}, u32[]{:S(2)}) copy-start(bf16[3,2,72,256]{3,2,1,0:T(8,128)(2,1)} %get-tuple-element.80) | copy-start | bytes 663556
  283.4 85.2 %copy-start.7 = (bf16[4,72,256]{2,1,0:T(8,128)(2,1)S(1)}, bf16[4,72,256]{2,1,0:T(8,128)(2,1)}, u32[]{:S(2)}) copy-start(bf16[4,72,256]{2,1,0:T(8,128)(2,1)} %get-tuple-element.81) | copy-start | bytes 442372
  283.4 85.2 %copy-start.10 = (bf16[2,72,256]{2,1,0:T(8,128)(2,1)S(1)}, bf16[2,72,256]{2,1,0:T(8,128)(2,1)}, u32[]{:S(2)}) copy-start(bf16[2,72,256]{2,1,0:T(8,128)(2,1)} %get-tuple-element.82) | copy-start | bytes 221188
  368.6 2.2 copy-start.13
  368.6 2.9 copy-start.6
  368.6 2.9 copy-start.9
  368.7 3.7 copy-start.1
  371.5 6.3 %slice-start = ((s8[4608000]{0:T(1024)(128)(4,1)}), s8[4194304]{0:T(1024)(128)(4,1)S(1)}, s32[]{:S(2)}) async-start(s8[4608000]{0:T(1024)(128)(4,1)} %bitcast.55), calls=%async_computation | async-start | bytes 8388608
  372.4 5.4 %slice-start.1 = ((s8[4608000]{0:T(1024)(128)(4,1)}), s8[413696]{0:T(1024)(128)(4,1)S(1)}, s32[]{:S(2)}) async-start(s8[4608000]{0:T(1024)(128)(4,1)} %bitcast.55), calls=%async_computation.1 | async-start | bytes 827392
  373.8 3.4 copy-start.11
  377.8 2.2 copy-start.3

commit v5 on v4

--- a/solution.py
+++ b/solution.py
@@ -588,7 +588,7 @@
     def _():
         mask = low_half_mask(patches)
         extra = tail_rows(*[jnp.where(section == 1, 1.0, 0.0)] * 2, patches)
-        gain = gains_ref[0]
+        gain = gains_ref[0] * jnp.where(section == 0, HD ** (-0.5) * LOG2E, 1.0)
         for head in range(HEADS):
             part = raw[head * HD : (head + 1) * HD, :]
             factor = lax.rsqrt(jnp.mean(part * part, axis=0, keepdims=True) + epsilon)
@@ -1279,15 +1279,15 @@
 
 def tail_plan(dims):
     return [
-        ("pair", pl.ds(0, 384), order_of(dims, "b0", "b2", "b3", "b1", "y"), (1, 2, 5, 13, 25, 46)),
-        ("pair", pl.ds(384, 384), order_of(dims, "b0", "y", "b2", "b1", "b3"), (1, 3, 7, 21, 40, 54)),
-        ("pair", pl.ds(768, 384), order_of(dims, "b0", "b2", "b1", "b3", "y"), (1, 4, 15, 35, 49, 61)),
-        ("single", None, order_of(dims, "b0", "b1", "b2", "y", "b3"), (2, 5, 20, 40, 54, 66)),
+        ("pair", pl.ds(0, 384), order_of(dims, "b0", "b1", "b3", "b2", "y"), (1, 2, 5, 13, 19, 46)),
+        ("pair", pl.ds(384, 384), order_of(dims, "b0", "y", "b1", "b2", "b3"), (1, 3, 7, 30, 46, 59)),
+        ("pair", pl.ds(768, 384), order_of(dims, "b0", "b2", "b1", "b3", "y"), (1, 4, 14, 40, 54, 61)),
+        ("single", None, order_of(dims, "b0", "b1", "b2", "y", "b3"), (2, 5, 20, 40, 54, 67)),
     ]
 
 
 def tail_gather():
-    return ["b3", "b2", "b1", "y", "b0"], (9, 14, 22, 42, 59, 64)
+    return ["b2", "b3", "b1", "y", "b0"], (9, 14, 18, 42, 59, 64)
 
 
 class Ada:
@@ -1365,7 +1365,7 @@
         def _():
             self.parts[here] = dot(self.condition[...], modes_bf, 1, 0)
 
-    def finish(self, class_ref):
+    def finish(self):
         before = self.before[...]
         sigma = jax.nn.sigmoid(before)
         before_grad = self.total[...] * (sigma * (1.0 + before * (1.0 - sigma)))
@@ -1376,8 +1376,8 @@
         half = before.shape[1] // 2
         times = sum(dot(self.features[...], piece, 1, 0) for piece in pieces)
         self.time_out[...] = jnp.where(self.band == 0, times[:, :half], times[:, half:])
-        class_hot = self.class_hot(self.codes[0][:, :1])
-        class_ref[...] = sum(dot(class_hot, piece, 0, 0) for piece in pieces)
+        self.class_out[0] = before_grad
+        self.class_out[1, :, :128] = self.codes[0]
         for block in range(self.parts.shape[0]):
             columns = slice(block * ADA_COLUMNS, (block + 1) * ADA_COLUMNS)
             self.ada_out[:, columns] = self.parts[block]
@@ -1543,14 +1543,11 @@
         number = step - first_ada
         ada.block(jnp.where(number < ADA_EARLY, number + ada_steps - ADA_EARLY, number - ADA_EARLY))
 
-    class_ref = entry_grad_ref.at[pl.ds(0, class_out_ref.shape[0])]
-    class_copy = pltpu.make_async_copy(class_ref, class_out_ref, ada_sem.at[1])
     final = first_ada + ada_steps - 1
 
     @pl.when(step == final)
     def _():
-        ada.finish(class_ref)
-        class_copy.start()
+        ada.finish()
 
     @pl.when(step == final)
     def _():
@@ -1560,7 +1557,6 @@
         for number in range(2):
             away(number).wait()
             stay(number).wait()
-        class_copy.wait()
 
 
 def back_step(
@@ -1639,7 +1635,7 @@
             whole((rows, 3 * width)),
             pl.BlockSpec((1, ADA_COLUMNS), lambda t: (0, ada_block(t))),
             whole((time_rows, width // 2)),
-            pl.BlockSpec(memory_space=pl.ANY),
+            whole((2, images, width)),
             whole((1, ADA_COLUMNS)),
         ],
         out_shape=[
@@ -1649,7 +1645,7 @@
             jax.ShapeDtypeStruct((rows, 3 * width), f32),
             jax.ShapeDtypeStruct((1, 6 * width), f32),
             jax.ShapeDtypeStruct((time_rows, width // 2), f32),
-            jax.ShapeDtypeStruct((classes, width), f32),
+            jax.ShapeDtypeStruct((2, images, width), f32),
             jax.ShapeDtypeStruct((1, ADA_COLUMNS), f32),
         ],
         scratch_shapes=scratch
@@ -1662,6 +1658,44 @@
         projected_grad, qkv_weight, entry, latents, other_x, middle_grad, modulation, gain_rows,
         ada_weight, early, table, time_weight, class_table,
     )
+
+
+def last_kernel(rows_ref, result_ref, latents_ref, class_ref, result_out, latents_out):
+    label = rows_ref[1, :, :1]
+    first = pl.program_id(0) * class_ref.shape[0]
+    place = lax.broadcasted_iota(jnp.int32, (label.shape[0], class_ref.shape[0]), 1) + first
+    class_hot = (label == place.astype(f32)).astype(bf16)
+    parts, left = [], rows_ref[0]
+    for _ in range(3):
+        parts.append(left.astype(bf16))
+        left = left - parts[-1].astype(f32)
+    class_ref[...] = dot(
+        jnp.concatenate([class_hot] * 3, axis=0), jnp.concatenate(parts, axis=0), 0, 0
+    )
+    result_out[...] = result_ref[...]
+    latents_out[...] = latents_ref[...]
+
+
+def last_step(rows, classes, result, latents):
+    width = rows.shape[2]
+    block = 256
+    steps = pl.cdiv(classes, block)
+    images, half, _ = result.shape
+    part = pl.BlockSpec((images, half // steps, width), lambda t: (0, t, 0))
+    return pl.pallas_call(
+        last_kernel,
+        grid=(steps,),
+        in_specs=[whole(rows.shape), part, part],
+        out_specs=[pl.BlockSpec((block, width), lambda t: (t, 0)), part, part],
+        out_shape=[
+            jax.ShapeDtypeStruct((classes, width), f32),
+            jax.ShapeDtypeStruct(result.shape, result.dtype),
+            jax.ShapeDtypeStruct(latents.shape, latents.dtype),
+        ],
+        compiler_params=params_of(),
+        cost_estimate=cost(6 * rows.shape[1] * classes * width, 14e6),
+        name="last",
+    )(rows, result, latents)
 
 
 def pick(values, index):
@@ -1715,11 +1749,9 @@
     ) + pick(class_table, own_label)[None].astype(f32)
     condition = jax.nn.silu(before).astype(bf16)
     modulation = jnp.dot(condition, ada_weight, preferred_element_type=f32) + ada_bias
-    scaling = HD ** (-0.5)
     gains = jnp.stack([query_gain, key_gain])[:, :, None]
-    scaled_gains = gains * jnp.array([scaling * LOG2E, 1.0], f32)[:, None, None]
     entry_one, heads, unit, factor = front(
-        latents, other_x, modulation, qkv_weight, scaled_gains, cosine, sine
+        latents, other_x, modulation, qkv_weight, gains, cosine, sine
     )
     mixed, query = attend(heads)
     mixed = mixed.reshape(width, -1)
@@ -1742,13 +1774,16 @@
     gain_rows = jnp.pad(jnp.sum(gain_terms, axis=2), ((0, 0), (0, 128 - HD))).reshape(1, -1)
     gain_rows = jnp.pad(gain_rows, ((0, 1), (0, ADA_COLUMNS - gain_rows.shape[1])))
     (
-        grad_latents, qkv_pair, qkv_single, sum_ada, sum_bias, sum_time, sum_class, gain_sums,
+        grad_latents, qkv_pair, qkv_single, sum_ada, sum_bias, sum_time, before_rows, gain_sums,
     ) = back_step(
         projected_grad.reshape(3, width, -1), qkv_weight, entry_one, latents, other_x, middle_grad,
         modulation, gain_rows, ada_weight, modes_early.reshape((-1,) + modes_early.shape[-2:]), table,
         time_weight, class_table,
     )
     sum_bias = sum_bias.reshape(-1)
+    sum_class, result, grad_latents = last_step(
+        before_rows, class_table.shape[0], result, grad_latents
+    )
     sum_query_gain, sum_key_gain = gain_sums[0, :HD], gain_sums[0, 128 : 128 + HD]
     sum_down = sum_down.reshape(-1, sum_down.shape[-1]).astype(f32)
     sum_proj = sum_proj.astype(f32)

time: 386 us -> 376 us (0.974)
  local copies, waits for them, and re-layouts: 21.8 us -> 13.5 us
  waiting for transfers between devices: 0.24 us -> 5.48 us
    pallas_call x1, Pallas kernels: 82.5 us -> 72.8 us  [back_step(): pl.pallas_call(functools.partial(back_kernel, dims), grid=(10 + ada_steps...]
    pallas_call x0 -> x1, Pallas kernels: none -> 7.18 us  [last_step(): pl.pallas_call(last_kernel, grid=(steps,), in_specs=[whole(rows.shape), p...]
    unnamed x45 -> x38, local copies, waits for them, and re-layouts: 8.56 us -> 2.37 us
    ppermute x3, waiting for transfers between devices: 0.24 us -> 5.48 us  [from_other(): return lax.ppermute(values, 'band', [(0, 1), (1, 0)])]
  transfers between devices with their start and end apart: 3 -> 3, of which waited for: 1 -> 1; matrix products, arithmetic and copies ran while one was open for 7% -> 6% of each run, Pallas kernels for 12% -> 12%
where the time goes in v5:
time: 376 us; the launch traced here: 371 us
  Pallas kernels  326 us (87%)
  local copies, waits for them, and re-layouts  13.5 us (4%)
  other arithmetic  10.2 us (3%)
  matrix products  8.16 us (2%)
  waiting for transfers between devices  5.48 us (1%)
  between operations  4.98 us (1%)
    pallas_call x1, Pallas kernels, core_step(): pl.pallas_call(functools.partial(core_kernel, dims), grid=(turns + HEADS,...  96.7 us
    pallas_call x1, Pallas kernels, mlp(): pl.pallas_call(functools.partial(mlp_kernel, dims), grid=(tiles,), in_spe...  94.7 us
    pallas_call x1, Pallas kernels, back_step(): pl.pallas_call(functools.partial(back_kernel, dims), grid=(10 + ada_steps...  72.8 us
    pallas_call x1, Pallas kernels, front(): pl.pallas_call(front_kernel, grid=(3,), in_specs=[own_image(half, width,...  23.5 us
    pallas_call x1, Pallas kernels, attend(): pl.pallas_call(lambda q, k, v, mixed, qext: attend_kernel(q, k, v, mixed,...  20.4 us
    pallas_call x1, Pallas kernels, middle_step(): pl.pallas_call(middle_kernel, grid=(patches // rows,), in_specs=[pl.Block...  10.3 us
    dot_general x1, matrix products, per_device_whole(): jnp.dot(condition, ada_weight, preferred_element_type=f32) + ada_bias  8.16 us
  transfers between devices with their start and end apart: 3, of which 1 were waited for; matrix products, arithmetic and copies ran while one was open for 6% of the time, Pallas kernels for 12%

profile of v5, /device:TPU:0, one launch (start us, length us, event | category | flops | bytes accessed | tf_op | source)
XLA Modules:
  0.0 371.2 jit_solution(4243492023094712610)
XLA Ops:
  0.6 0.0 copy-start.17
  0.7 0.0 copy-start
  0.7 0.9 pad_add_fusion
  1.5 3.0 collective-permute-start.1
  4.5 2.4 dynamic-slice_bitcast_fusion.1
  6.9 0.0 collective-permute-start
  6.9 0.6 dynamic_slice.23
  8.8 1.2 dynamic_slice.25
  11.3 0.7 divide_multiply_fusion.2
  12.0 1.1 dynamic-slice_bitcast_fusion
  14.4 1.3 add_convert_fusion.1
  15.7 0.1 fusion.9
  15.8 0.6 pad_maximum_fusion.2.table_ref
  16.4 0.0 copy-start.14
  16.5 8.2 %convolution_reduce_fusion = f32[6912]{0:T(1024)S(1)} fusion(bf16[1152,6912]{1,0:T(8,128)(2,1)} %ada_ref.1, bf16[256,1152]{1,0:T(8,128)(2,1)} %time_ref.1, bf16[1000,1152]{1,0:T(8,128)(2,1)} %classes_ref.1, s32[]{:T(128)S(6)} %select_n.29, s32[]{:T(128)S(6)} %select_n.28, bf16[8,128]{1,0:T(8,128)(2,1)S(1)} %get-tuple-element.101, ...), kind=kOutput, calls=%fused_computation.3 | convolution fusion | flops 16524160 | bytes 16551432 | tf_op jit(solution)/shard_map/dot_general | solution.py:1751
  24.7 0.6 add.48.modulation_ref
  25.3 0.7 copy.29.gains_ref
  26.1 0.6 pad.12.codes_ref
  26.7 0.0 collective-permute-done.1
  26.7 0.0 copy-done.13
  26.7 0.8 multiply_sine_fusion
  27.5 0.8 pad_maximum_fusion.cos_ref
  28.3 0.8 pad_maximum_fusion.1.sin_ref
  29.0 5.5 %collective-permute-done.other_ref.other_x_ref = bf16[512,1152]{1,0:T(8,128)(2,1)S(1)} collective-permute-done((bf16[512,1152]{1,0:T(8,128)(2,1)}, bf16[512,1152]{1,0:T(8,128)(2,1)S(1)}, u32[]{:S(2)}, u32[]{:S(2)}) %collective-permute-start) | collective-permute-done | bytes 1179680 | tf_op jit(solution)/shard_map/ppermute | solution.py:1729
  34.5 0.3 collective-permute-start.2
  34.8 0.7 copy-done.1
  35.5 23.5 %front.1 = (bf16[1024,1152]{1,0:T(8,128)(2,1)}, bf16[3,16,80,1024]{3,2,1,0:T(8,128)(2,1)}, bf16[2,16,72,1024]{3,2,1,0:T(8,128)(2,1)}, f32[2,16,1,1024]{3,2,1,0:T(1,128)}) custom-call(bf16[2,512,1152]{2,1,0:T(8,128)(2,1)} %own_x_ref.5, bf16[512,1152]{1,0:T(8,128)(2,1)} %copy-done.1, f32[1,6912]{1,0:T(1,128)} %add.48.modulation_ref, bf16[1152,3456]{1,0:T(8,128)(2,1)} %w_ref.7, ...), custom_call_target="tpu_custom_call" | custom-call | flops 8153726976 | bytes 24000000 | tf_op jit(solution)/shard_map/front/pallas_call | solution.py:618
  59.1 20.4 %attend.1 = (bf16[16,72,1024]{2,1,0:T(8,128)(2,1)}, bf16[16,80,1024]{2,1,0:T(8,128)(2,1)}) custom-call(bf16[3,16,80,1024]{3,2,1,0:T(8,128)(2,1)} %get-tuple-element.51.q.k.v.k_ref.v_ref, bf16[3,16,80,1024]{3,2,1,0:T(8,128)(2,1)} %get-tuple-element.51.q.k.v.k_ref.v_ref, bf16[3,16,80,1024]{3,2,1,0:T(8,128)(2,1)} %get-tuple-element.51.q.k.v.k_ref.v_ref), custom_call_target="tpu_custom_call" | custom-call | flops 10737418240 | bytes 14000000 | tf_op jit(solution)/shard_map/attend/pallas_call | solution.py:670
  79.5 0.0 collective-permute-done.2.other_c_ref
  79.5 10.3 %middle.1 = (bf16[1024,1152]{1,0:T(8,128)(2,1)}, bf16[1024,1152]{1,0:T(8,128)(2,1)}, bf16[1024,1152]{1,0:T(8,128)(2,1)}) custom-call(bf16[1152,1024]{1,0:T(8,128)(2,1)} %bitcast.53, bf16[1152,1152]{1,0:T(8,128)(2,1)} %w_ref.6, bf16[2,512,1152]{2,1,0:T(8,128)(2,1)} %own_x_ref.5, bf16[512,1152]{1,0:T(8,128)(2,1)} %copy-done.1, ...), custom_call_target="tpu_custom_call" | custom-call | flops 2717908992 | bytes 17000000 | tf_op jit(solution)/shard_map/middle/pallas_call | solution.py:715
  89.7 94.7 %mlp.1 = (f32[1024,1152]{1,0:T(8,128)}, f32[1024,1152]{1,0:T(8,128)}, bf16[2,3072,576]{2,1,0:T(8,128)(2,1)}, bf16[3,2,72,256]{3,2,1,0:T(8,128)(2,1)}, bf16[2,2,2...) custom-call(bf16[1024,1152]{1,0:T(8,128)(2,1)} %get-tuple-element.54, ...), custom_call_target="tpu_custom_call" | custom-call | flops 65229815808 | bytes 56000000 | tf_op jit(solution)/shard_map/mlp/pallas_call | solution.py:861
  184.5 96.7 %core.1 = (bf16[2,512,1152]{2,1,0:T(8,128)(2,1)}, f32[1024,1152]{1,0:T(8,128)}, bf16[3,16,72,1024]{3,2,1,0:T(8,128)(2,1)}, f32[2,72,1024]{2,1,0:T(8,128)}, bf16[...) custom-call(f32[1024,1152]{1,0:T(8,128)} %get-tuple-element.56.fed_r, ...), custom_call_target="tpu_custom_call" | custom-call | flops 32212254720 | bytes 70000000 | tf_op jit(solution)/shard_map/core/pallas_call | solution.py:1207
  281.2 1.2 reduce_sum.9
  282.4 0.6 pad.14.gain_terms_ref
  283.0 72.8 %back.1 = (bf16[2,512,1152]{2,1,0:T(8,128)(2,1)}, bf16[72,1152]{1,0:T(8,128)(2,1)}, bf16[72,576]{1,0:T(8,128)(2,1)}, f32[72,3456]{1,0:T(8,128)}, f32[1,6912]{1,0...) custom-call(bf16[3,1152,1024]{2,1,0:T(8,128)(2,1)} %bitcast.65, bf16[1152,3456]{1,0:T(8,128)(2,1)} %w_ref.7, ...), custom_call_target="tpu_custom_call" | custom-call | flops 16307453952 | bytes 40000000 | tf_op jit(solution)/shard_map/back/pallas_call | solution.py:1613
  355.8 1.1 slice_bitcast_fusion.4
  357.0 0.0 copy-done.7
  357.0 0.7 convert_element_type.53
  357.6 0.0 copy-done.3
  357.6 0.8 bitcast_convert_fusion
  358.5 0.1 convert_bitcast_fusion
  358.6 0.5 copy.31
  359.1 1.6 reshape.112
  360.7 0.7 reduce.1
  361.4 0.9 fusion
  362.3 7.2 %last.1 = (f32[1000,1152]{1,0:T(8,128)}, bf16[2,512,1152]{2,1,0:T(8,128)(2,1)}, bf16[2,512,1152]{2,1,0:T(8,128)(2,1)}) custom-call(f32[2,32,1152]{2,1,0:T(8,128)} %get-tuple-element.73.rows_ref, bf16[2,512,1152]{2,1,0:T(8,128)(2,1)} %get-tuple-element.74.result_ref, bf16[2,512,1152]{2,1,0:T(8,128)(2,1)} %get-tuple-element.75.latents_ref), custom_call_target="tpu_custom_call" | custom-call | flops 221184000 | bytes 14000000 | tf_op jit(solution)/shard_map/last/pallas_call | solution.py:1685
  369.5 0.6 copy.34
  370.1 0.9 copy.35
  (37 shorter events, 0.2 us)
Async XLA Ops:
  0.6 6.3 %copy-start.17 = (s32[2]{0:T(128)S(1)}, s32[2]{0:T(128)}, u32[]{:S(2)}) copy-start(s32[2]{0:T(128)} %param.20) | copy-start | bytes 28
  0.7 11.3 %copy-start = (bf16[2,512,1152]{2,1,0:T(8,128)(2,1)S(1)}, bf16[2,512,1152]{2,1,0:T(8,128)(2,1)}, u32[]{:S(2)}) copy-start(bf16[2,512,1152]{2,1,0:T(8,128)(2,1)} %own_c_ref.3) | copy-start | bytes 7077892
  1.5 25.2 %collective-permute-start.1 = (s32[512,2]{0,1:T(2,128)S(1)}, s32[512,2]{0,1:T(2,128)S(1)}, u32[]{:S(2)}, u32[]{:S(2)}) collective-permute-start(s32[512,2]{0,1:T(2,128)S(1)} %pad_add_fusion), channel_id=1, source_target_pairs={{0,1},{1,0},{2,3},{3,2},{4,5},{5,4},{6,7},{7,6},{8,9},{9,8},{10,11... | collective-permute-start | bytes 12296 | tf_op jit(solution)/shard_map/ppermute | solution.py:1729
  6.9 27.6 %collective-permute-start = (bf16[512,1152]{1,0:T(8,128)(2,1)}, bf16[512,1152]{1,0:T(8,128)(2,1)S(1)}, u32[]{:S(2)}, u32[]{:S(2)}) collective-permute-start(bf16[512,1152]{1,0:T(8,128)(2,1)} %dynamic-slice_bitcast_fusion.1), channel_id=1, source_target_pairs={{0,1},{1,0},{2,3},{3,2},{4,5},{5,4},{6,7},{7,6},{8,9},{9,8},{10,11... | collective-permute-start | bytes 3538952 | tf_op jit(solution)/shard_map/ppermute | solution.py:1729
  16.4 8.2 %copy-start.15 = (f32[72]{0:T(128)S(1)}, f32[72]{0:T(128)}, u32[]{:S(2)}) copy-start(f32[72]{0:T(128)} %param.30) | copy-start | bytes 868
  16.4 8.2 %copy-start.16 = (f32[72]{0:T(128)S(1)}, f32[72]{0:T(128)}, u32[]{:S(2)}) copy-start(f32[72]{0:T(128)} %param.29) | copy-start | bytes 868
  16.4 8.2 %copy-start.11 = (f32[6912]{0:T(1024)S(1)}, f32[6912]{0:T(1024)}, u32[]{:S(2)}) copy-start(f32[6912]{0:T(1024)} %param.27) | copy-start | bytes 82948
  16.4 10.2 %copy-start.13 = (s32[512]{0:T(512)S(1)}, s32[512]{0:T(512)}, u32[]{:S(2)}) copy-start(s32[512]{0:T(512)} %param.23) | copy-start | bytes 6148
  16.4 10.2 %copy-start.14 = (s32[512]{0:T(512)S(1)}, s32[512]{0:T(512)}, u32[]{:S(2)}) copy-start(s32[512]{0:T(512)} %param.22) | copy-start | bytes 6148
  34.5 1.0 copy-start.1
  34.5 45.0 %collective-permute-start.2 = (bf16[512,1152]{1,0:T(8,128)(2,1)}, bf16[512,1152]{1,0:T(8,128)(2,1)}, u32[]{:S(2)}, u32[]{:S(2)}) collective-permute-start(bf16[512,1152]{1,0:T(8,128)(2,1)} %dynamic-slice_bitcast_fusion), channel_id=1, source_target_pairs={{0,1},{1,0},{2,3},{3,2},{4,5},{5,4},{6,7},{7,6},{8,9},{9,8},{10,11... | collective-permute-start | bytes 3538952 | tf_op jit(solution)/shard_map/ppermute | solution.py:1729
  283.0 74.0 %copy-start.7 = (bf16[72,576]{1,0:T(8,128)(2,1)S(1)}, bf16[72,576]{1,0:T(8,128)(2,1)}, u32[]{:S(2)}) copy-start(bf16[72,576]{1,0:T(8,128)(2,1)} %get-tuple-element.85) | copy-start | bytes 248836
  283.0 74.7 %copy-start.3 = (bf16[4,48,576]{2,1,0:T(8,128)(2,1)S(1)}, bf16[4,48,576]{2,1,0:T(8,128)(2,1)}, u32[]{:S(2)}) copy-start(bf16[4,48,576]{2,1,0:T(8,128)(2,1)} %get-tuple-element.89) | copy-start | bytes 663556
  283.0 75.5 %copy-start.4 = (bf16[3,2,72,256]{3,2,1,0:T(8,128)(2,1)S(1)}, bf16[3,2,72,256]{3,2,1,0:T(8,128)(2,1)}, u32[]{:S(2)}) copy-start(bf16[3,2,72,256]{3,2,1,0:T(8,128)(2,1)} %get-tuple-element.86) | copy-start | bytes 663556
  283.0 75.5 %copy-start.6 = (bf16[4,72,256]{2,1,0:T(8,128)(2,1)S(1)}, bf16[4,72,256]{2,1,0:T(8,128)(2,1)}, u32[]{:S(2)}) copy-start(bf16[4,72,256]{2,1,0:T(8,128)(2,1)} %get-tuple-element.87) | copy-start | bytes 442372
  283.0 75.5 %copy-start.9 = (bf16[2,72,256]{2,1,0:T(8,128)(2,1)S(1)}, bf16[2,72,256]{2,1,0:T(8,128)(2,1)}, u32[]{:S(2)}) copy-start(bf16[2,72,256]{2,1,0:T(8,128)(2,1)} %get-tuple-element.88) | copy-start | bytes 221188
  358.5 2.2 copy-start.12
  358.5 2.9 copy-start.5
  358.5 2.9 copy-start.8
  362.3 7.2 %copy-start.10 = (f32[16,576]{1,0:T(8,128)S(1)}, f32[16,576]{1,0:T(8,128)}, u32[]{:S(2)}) copy-start(f32[16,576]{1,0:T(8,128)} %get-tuple-element.118) | copy-start | bytes 110596
  362.3 7.8 %copy-start.2 = (f32[72,3456]{1,0:T(8,128)S(1)}, f32[72,3456]{1,0:T(8,128)}, u32[]{:S(2)}) copy-start(f32[72,3456]{1,0:T(8,128)} %get-tuple-element.120) | copy-start | bytes 2985988
